TPU v7x, 32 devices: a whole 2x2x4 slice. The times are simulated.
32 devices in a mesh: batch: 4 (over x, core), seq: 8 (over z, y).
Axes of the slice: x: 2, y: 2, z: 4, core: 2. Of those that a mesh axis runs over, the one named last changes fastest.
Arguments:
- byte_rows: bfloat16 [8, 1536, 512], P('batch', 'seq'), may hold values from -6 to 6
- item_lengths: int32 [8], P('batch'), may hold values from 153 to 1536, as said below
- out_grad: bfloat16 [8, 1536, 512], P('batch', 'seq'), may hold values from -6 to 6
- pool_weight: bfloat16 [1536, 512], replicated, may hold values from -0.15625 to 0.15625
- norm1_gain: float32 [512], replicated, may hold values from 0.25 to 1.75
- norm1_bias: float32 [512], replicated, may hold values from -1.5 to 1.5
- query_weight: bfloat16 [512, 512], replicated, may hold values from -0.25 to 0.25
- key_weight: bfloat16 [512, 512], replicated, may hold values from -0.25 to 0.25
- value_weight: bfloat16 [512, 512], replicated, may hold values from -0.25 to 0.25
- position_weight: bfloat16 [512, 512], replicated, may hold values from -0.25 to 0.25
- content_bias: float32 [8, 64], replicated, may hold values from -2.5 to 2.5
- position_bias: float32 [8, 64], replicated, may hold values from -2.5 to 2.5
- output_weight: bfloat16 [512, 512], replicated, may hold values from -1 to 1
- norm2_gain: float32 [512], replicated, may hold values from 0.25 to 1.75
- norm2_bias: float32 [512], replicated, may hold values from -1.5 to 1.5
- inner_weight: bfloat16 [512, 2048], replicated, may hold values from -0.25 to 0.25
- outer_weight: bfloat16 [2048, 512], replicated, may hold values from -0.125 to 0.125
- upsample_weight: bfloat16 [512, 1536], replicated, may hold values from -0.25 to 0.25
Outputs:
- block_out: bfloat16 [8, 1536, 512], P('batch', 'seq')
- input_grad: float32 [8, 1536, 512], P('batch', 'seq')
- pool_weight_grad: float32 [1536, 512], replicated
- norm1_gain_grad: float32 [512], replicated
- norm1_bias_grad: float32 [512], replicated
- query_weight_grad: float32 [512, 512], replicated
- key_weight_grad: float32 [512, 512], replicated
- value_weight_grad: float32 [512, 512], replicated
- position_weight_grad: float32 [512, 512], replicated
- content_bias_grad: float32 [8, 64], replicated
- position_bias_grad: float32 [8, 64], replicated
- output_weight_grad: float32 [512, 512], replicated
- norm2_gain_grad: float32 [512], replicated
- norm2_bias_grad: float32 [512], replicated
- inner_weight_grad: float32 [512, 2048], replicated
- outer_weight_grad: float32 [2048, 512], replicated
- upsample_weight_grad: float32 [512, 1536], replicated
Inputs may be any that keep to these rules, and one draw needn't show every extreme that they name: `item_lengths`: every length is a multiple of 3. Among the 2 items 2 b to 2 b + 1 of each index b of batch, one has length 1536.
All inputs are finite; a program needn't handle non-finite values.
Results may differ from a plain program's by a relative error of at most 0.02.
Values may be sent and summed in bfloat16 or wider, within the bound.
A program may use at most 384 MiB of HBM per device.

v0:
```python
import jax
import jax.numpy as jnp
from jax import lax
from jax.sharding import PartitionSpec as P

epsilon = 1e-05
masked_value = -1e30


def shifted_2(value, axis, steps):
    count = lax.axis_size(axis)
    initial, last = (max(0, -steps), min(count, count - steps))
    return lax.ppermute(value, axis, [(source, source + steps) for source in range(initial, last)])


def relative_table(row_total, short_len, width):
    offsets = jnp.arange(row_total).astype(jnp.float32)
    distance = short_len - 1 - offsets
    steps_in = jnp.arange(0, width, 2).astype(jnp.float32)
    frequency = jnp.exp(-jnp.log(10000.0) * steps_in / width)
    angles = distance[:, None] * frequency[None, :]
    return jnp.concatenate([jnp.sin(angles), jnp.cos(angles)], axis=1)


def skew_scores(scattered_rows, block_rows, key_total):
    head_count, _, extent_length = scattered_rows.shape
    flattened = scattered_rows.reshape(head_count, block_rows * extent_length)
    flattened = lax.slice_in_dim(
        flattened, block_rows - 1, block_rows - 1 + block_rows * (extent_length - 1), axis=1
    )
    return flattened.reshape(head_count, block_rows, extent_length - 1)[:, :, :key_total]


def unskew_scores(gradient, block_rows, extent_length):
    head_count, _, key_total = gradient.shape
    widened = jnp.pad(gradient, ((0, 0), (0, 0), (0, extent_length - 1 - key_total)))
    flattened = widened.reshape(head_count, block_rows * (extent_length - 1))
    flattened = jnp.pad(flattened, ((0, 0), (block_rows - 1, 1)))
    return flattened.reshape(head_count, block_rows, extent_length)


def norm_forward(rows_in):
    row_mean = jnp.mean(rows_in, axis=-1, keepdims=True)
    centered = rows_in - row_mean
    variance = jnp.mean(centered * centered, axis=-1, keepdims=True)
    inverse = lax.rsqrt(variance + epsilon)
    return (centered * inverse, inverse)


def norm_backward(gradient, normed, inverse, gain_vec):
    scaled = gradient * gain_vec
    return inverse * (
        scaled
        - jnp.mean(scaled, axis=-1, keepdims=True)
        - normed * jnp.mean(scaled * normed, axis=-1, keepdims=True)
    )


def gelu_slope(inner):
    normal_cdf = 0.5 * (1.0 + lax.erf(inner * 0.7071067811865476))
    density = jnp.exp(-0.5 * inner * inner) * 0.3989422804014327
    return normal_cdf + inner * density


def transposed_product(left, right):
    return jnp.einsum("rk,rj->kj", left, right, preferred_element_type=jnp.float32)


def back_product(left, right):
    return jnp.einsum("rj,kj->rk", left, right, preferred_element_type=jnp.float32)


def block_logits(
    query_content, query_location, keys_in, key_count, position_heads, leading_index, block_rows
):
    head_count, short_len, head_width = query_content.shape
    key_total = leading_index + block_rows
    extent_length = key_total + block_rows - 1
    start_offset = short_len - leading_index - block_rows
    content = jnp.einsum(
        "hnd,hld->hnl",
        query_content[:, leading_index:key_total],
        keys_in[:, :key_total],
        preferred_element_type=jnp.float32,
    )
    scattered_rows = jnp.einsum(
        "hnd,hed->hne",
        query_location[:, leading_index:key_total],
        position_heads[:, start_offset : start_offset + extent_length],
        preferred_element_type=jnp.float32,
    )
    raw_scores = content + skew_scores(scattered_rows, block_rows, key_total)
    query_at = leading_index + jnp.arange(block_rows)[:, None]
    key_at = jnp.arange(key_total)[None, :]
    valid = ((key_at <= query_at) & (key_at < key_count))[None]
    logits = jnp.where(valid, raw_scores * head_width ** (-0.5), masked_value)
    return (logits, valid, start_offset, extent_length)


def attend_forward(query_content, query_location, keys_in, values_in, key_count, position_heads):
    short_len = query_content.shape[1]
    block_rows = min(512, short_len)
    outputs = []
    totals = []
    for block_index in range(short_len // block_rows):
        leading_index = block_index * block_rows
        key_total = leading_index + block_rows
        logits, valid, start_offset, extent_length = block_logits(
            query_content,
            query_location,
            keys_in,
            key_count,
            position_heads,
            leading_index,
            block_rows,
        )
        row_max = jnp.max(logits, axis=-1, keepdims=True)
        log_total = row_max + jnp.log(jnp.sum(jnp.exp(logits - row_max), axis=-1, keepdims=True))
        weights = jnp.exp(logits - log_total).astype(jnp.bfloat16)
        outputs.append(
            jnp.einsum(
                "hnl,hld->hnd",
                weights,
                values_in[:, :key_total],
                preferred_element_type=jnp.float32,
            )
        )
        totals.append(log_total[:, :, 0])
    return (jnp.concatenate(outputs, axis=1), jnp.concatenate(totals, axis=1))


def attend_backward(
    query_content,
    query_location,
    keys_in,
    values_in,
    attended_grad,
    key_count,
    log_totals,
    position_heads,
):
    head_count, short_len, head_width = query_content.shape
    block_rows = min(512, short_len)
    content_parts = []
    position_parts = []
    key_grad = jnp.zeros(query_content.shape, jnp.float32)
    value_grad = jnp.zeros(query_content.shape, jnp.float32)
    table_grad = jnp.zeros(position_heads.shape, jnp.float32)
    for block_index in range(short_len // block_rows):
        leading_index = block_index * block_rows
        key_total = leading_index + block_rows
        logits, valid, start_offset, extent_length = block_logits(
            query_content,
            query_location,
            keys_in,
            key_count,
            position_heads,
            leading_index,
            block_rows,
        )
        probs = jnp.exp(logits - log_totals[:, leading_index:key_total, None])
        weights = probs.astype(jnp.bfloat16)
        block_grad = attended_grad[:, leading_index:key_total]
        prob_grad = jnp.einsum(
            "hnd,hld->hnl", block_grad, values_in[:, :key_total], preferred_element_type=jnp.float32
        )
        delta = jnp.sum(probs * prob_grad, axis=-1, keepdims=True)
        raw_grad = (
            jnp.where(valid, probs * (prob_grad - delta), 0.0) * head_width ** (-0.5)
        ).astype(jnp.bfloat16)
        content_parts.append(
            jnp.einsum(
                "hnl,hld->hnd", raw_grad, keys_in[:, :key_total], preferred_element_type=jnp.float32
            )
        )
        key_grad = key_grad.at[:, :key_total].add(
            jnp.einsum(
                "hnl,hnd->hld",
                raw_grad,
                query_content[:, leading_index:key_total],
                preferred_element_type=jnp.float32,
            )
        )
        value_grad = value_grad.at[:, :key_total].add(
            jnp.einsum("hnl,hnd->hld", weights, block_grad, preferred_element_type=jnp.float32)
        )
        placed_grad = unskew_scores(raw_grad, block_rows, extent_length)
        position_parts.append(
            jnp.einsum(
                "hne,hed->hnd",
                placed_grad,
                position_heads[:, start_offset : start_offset + extent_length],
                preferred_element_type=jnp.float32,
            )
        )
        table_grad = table_grad.at[:, start_offset : start_offset + extent_length].add(
            jnp.einsum(
                "hne,hnd->hed",
                placed_grad,
                query_location[:, leading_index:key_total],
                preferred_element_type=jnp.float32,
            )
        )
    return (
        jnp.concatenate(content_parts, axis=1),
        jnp.concatenate(position_parts, axis=1),
        key_grad,
        value_grad,
        table_grad,
    )


def own_slice(array_in, item_count, short_len, own_short, seq_index):
    last_dim = array_in.shape[-1]
    shaped = array_in.reshape(item_count, short_len, last_dim)
    taken = lax.dynamic_slice_in_dim(shaped, seq_index * own_short, own_short, axis=1)
    return taken.reshape(item_count * own_short, last_dim)


def body(
    byte_rows,
    item_lengths,
    out_grad,
    pool_weight,
    norm1_gain,
    norm1_bias,
    query_weight,
    key_weight,
    value_weight,
    position_weight,
    content_bias,
    position_bias,
    output_weight,
    norm2_gain,
    norm2_bias,
    inner_weight,
    outer_weight,
    upsample_weight,
):
    item_count, full_rows, width = byte_rows.shape
    own_short = full_rows // 3
    seq_index = lax.axis_index("seq")
    short_len = own_short * lax.axis_size("seq")
    head_count, head_width = content_bias.shape
    block_rows = min(512, short_len)
    table_rows = short_len + block_rows - 1
    row_total = item_count * short_len
    key_counts = item_lengths // 3
    full_at = seq_index * full_rows + jnp.arange(full_rows)
    live = (full_at[None, :] < item_lengths[:, None]).astype(jnp.float32)[:, :, None]

    def grad_rows(array_in):
        return own_slice(array_in, item_count, short_len, own_short, seq_index)

    def heads_of(array_in):
        return array_in.reshape(item_count, short_len, head_count, head_width).transpose(0, 2, 1, 3)

    def rows_of(array_in):
        return array_in.transpose(0, 2, 1, 3).reshape(row_total, width)

    tail_rows = byte_rows[:, full_rows - 2 :, :]
    carried = shifted_2(tail_rows, "seq", 1)
    shifted = jnp.concatenate([carried, byte_rows[:, : full_rows - 2, :]], axis=1)
    grouped = shifted.reshape(item_count * own_short, 3 * width)
    pooled = jnp.dot(grouped, pool_weight, preferred_element_type=jnp.float32).astype(jnp.bfloat16)
    short_all = lax.all_gather(
        pooled.reshape(item_count, own_short, width), "seq", axis=1, tiled=True
    )
    short_rows = short_all.reshape(row_total, width).astype(jnp.float32)
    normed1, inverse1 = norm_forward(short_rows)
    attn_in = (normed1 * norm1_gain + norm1_bias).astype(jnp.bfloat16)
    queries = jnp.dot(attn_in, query_weight, preferred_element_type=jnp.float32)
    content_q = heads_of((queries + content_bias.reshape(-1)).astype(jnp.bfloat16))
    position_q = heads_of((queries + position_bias.reshape(-1)).astype(jnp.bfloat16))
    keys = heads_of(
        jnp.dot(attn_in, key_weight, preferred_element_type=jnp.float32).astype(jnp.bfloat16)
    )
    values = heads_of(
        jnp.dot(attn_in, value_weight, preferred_element_type=jnp.float32).astype(jnp.bfloat16)
    )
    table = relative_table(table_rows, short_len, width).astype(jnp.bfloat16)
    position_indices = jnp.dot(table, position_weight, preferred_element_type=jnp.float32).astype(
        jnp.bfloat16
    )
    position_heads = position_indices.reshape(table_rows, head_count, head_width).transpose(1, 0, 2)

    def forward_item(packed):
        return attend_forward(packed[0], packed[1], packed[2], packed[3], packed[4], position_heads)

    attended_heads, log_totals = lax.map(
        forward_item, (content_q, position_q, keys, values, key_counts)
    )
    attended = rows_of(attended_heads).astype(jnp.bfloat16)
    hidden = short_rows + jnp.dot(attended, output_weight, preferred_element_type=jnp.float32)
    normed2, inverse2 = norm_forward(hidden)
    ffn_in = (normed2 * norm2_gain + norm2_bias).astype(jnp.bfloat16)
    inner = jnp.dot(ffn_in, inner_weight, preferred_element_type=jnp.float32)
    activated = jax.nn.gelu(inner, approximate=False).astype(jnp.bfloat16)
    summed = hidden + jnp.dot(activated, outer_weight, preferred_element_type=jnp.float32)
    own_summed = own_slice(summed, item_count, short_len, own_short, seq_index).astype(jnp.bfloat16)
    upsampled = jnp.dot(own_summed, upsample_weight, preferred_element_type=jnp.float32).reshape(
        item_count, full_rows, width
    )
    block_out = (byte_rows.astype(jnp.float32) + upsampled * live).astype(jnp.bfloat16)
    up_grad = (out_grad.astype(jnp.float32) * live).astype(jnp.bfloat16)
    up_rows = up_grad.reshape(item_count * own_short, 3 * width)
    upsample_grad = transposed_product(own_summed, up_rows)
    summed_grad = back_product(up_rows, upsample_weight).astype(jnp.bfloat16)
    summed_all = lax.all_gather(
        summed_grad.reshape(item_count, own_short, width), "seq", axis=1, tiled=True
    )
    summed_all = summed_all.reshape(row_total, width)
    outer_grad = transposed_product(grad_rows(activated), grad_rows(summed_all))
    act_grad = back_product(summed_all, outer_weight)
    inner_grad = (act_grad * gelu_slope(inner)).astype(jnp.bfloat16)
    inner_wgrad = transposed_product(grad_rows(ffn_in), grad_rows(inner_grad))
    ffn_grad = back_product(inner_grad, inner_weight)
    ffn_share = grad_rows(ffn_grad)
    norm2_gain_grad = jnp.sum(ffn_share * grad_rows(normed2), axis=0)
    norm2_bias_grad = jnp.sum(ffn_share, axis=0)
    hidden_grad = summed_all.astype(jnp.float32) + norm_backward(
        ffn_grad, normed2, inverse2, norm2_gain
    )
    branch_grad = hidden_grad.astype(jnp.bfloat16)
    output_wgrad = transposed_product(grad_rows(attended), grad_rows(branch_grad))
    attended_grad = heads_of(back_product(branch_grad, output_weight).astype(jnp.bfloat16))

    def backward_item(packed):
        return attend_backward(
            packed[0],
            packed[1],
            packed[2],
            packed[3],
            packed[4],
            packed[5],
            packed[6],
            position_heads,
        )

    content_grad, position_grad, key_part, value_part, table_part = lax.map(
        backward_item, (content_q, position_q, keys, values, attended_grad, key_counts, log_totals)
    )
    content_bias_grad = jnp.sum(content_grad, axis=(0, 2))
    position_bias_grad = jnp.sum(position_grad, axis=(0, 2))
    query_grad = rows_of(content_grad + position_grad).astype(jnp.bfloat16)
    key_grad = rows_of(key_part).astype(jnp.bfloat16)
    value_grad = rows_of(value_part).astype(jnp.bfloat16)
    table_grad = (
        table_part.transpose(0, 2, 1, 3).reshape(item_count, table_rows, width).astype(jnp.bfloat16)
    )
    position_wgrad = jnp.zeros((width, width), jnp.float32)
    for item_index in range(item_count):
        position_wgrad = position_wgrad + transposed_product(table, table_grad[item_index])
    attn_rows = grad_rows(attn_in)
    query_wgrad = transposed_product(attn_rows, grad_rows(query_grad))
    key_wgrad = transposed_product(attn_rows, grad_rows(key_grad))
    value_wgrad = transposed_product(attn_rows, grad_rows(value_grad))
    attn_grad = (
        back_product(query_grad, query_weight)
        + back_product(key_grad, key_weight)
        + back_product(value_grad, value_weight)
    )
    attn_share = grad_rows(attn_grad)
    norm1_gain_grad = jnp.sum(attn_share * grad_rows(normed1), axis=0)
    norm1_bias_grad = jnp.sum(attn_share, axis=0)
    short_grad = hidden_grad + norm_backward(attn_grad, normed1, inverse1, norm1_gain)
    own_grad = own_slice(short_grad, item_count, short_len, own_short, seq_index).astype(
        jnp.bfloat16
    )
    pool_grad = transposed_product(grouped, own_grad)
    shifted_grad = back_product(own_grad, pool_weight).reshape(item_count, full_rows, width)
    next_rows = shifted_2(shifted_grad[:, :2, :], "seq", -1)
    input_grad = out_grad.astype(jnp.float32) + jnp.concatenate(
        [shifted_grad[:, 2:, :], next_rows], axis=1
    )
    summed_dense = lax.psum(
        (
            pool_grad,
            upsample_grad,
            norm1_gain_grad,
            norm1_bias_grad,
            query_wgrad,
            key_wgrad,
            value_wgrad,
            output_wgrad,
            norm2_gain_grad,
            norm2_bias_grad,
            inner_wgrad,
            outer_grad,
        ),
        ("batch", "seq"),
    )
    summed_relative = (
        lax.psum(position_wgrad.astype(jnp.bfloat16), "batch").astype(jnp.float32),
        lax.psum(content_bias_grad.astype(jnp.bfloat16), "batch").astype(jnp.float32),
        lax.psum(position_bias_grad.astype(jnp.bfloat16), "batch").astype(jnp.float32),
    )
    (
        pool_total,
        upsample_total,
        gain1_total,
        bias1_total,
        query_total,
        key_total,
        value_total,
        output_total,
        gain2_total,
        bias2_total,
        inner_total,
        outer_total,
    ) = summed_dense
    position_total, content_total, posbias_total = summed_relative
    return (
        block_out,
        input_grad,
        pool_total,
        gain1_total,
        bias1_total,
        query_total,
        key_total,
        value_total,
        position_total,
        content_total,
        posbias_total,
        output_total,
        gain2_total,
        bias2_total,
        inner_total,
        outer_total,
        upsample_total,
    )


def solution(mesh):
    in_specs = (
        P("batch", "seq", None),
        P("batch"),
        P("batch", "seq", None),
        P(),
        P(),
        P(),
        P(),
        P(),
        P(),
        P(),
        P(),
        P(),
        P(),
        P(),
        P(),
        P(),
        P(),
        P(),
    )
    out_specs = (
        P("batch", "seq", None),
        P("batch", "seq", None),
        P(),
        P(),
        P(),
        P(),
        P(),
        P(),
        P(),
        P(),
        P(),
        P(),
        P(),
        P(),
        P(),
        P(),
        P(),
    )
    return jax.shard_map(body, mesh=mesh, in_specs=in_specs, out_specs=out_specs, check_vma=False)
```

profile of v0, /device:TPU:0, one launch (start us, length us, event | category | flops | bytes accessed | tf_op | source)
XLA Modules:
  0.0 1270.5 jit_solution(16590751689694703133)
XLA Ops:
  29.6 31.0 %all-gather.3.cloned.1.call-done = bf16[2,512,512]{2,1,0:T(8,128)(2,1)} async-done(((bf16[2,64,512]{2,1,0:T(8,128)(2,1)}), bf16[2,512,512]{2,1,0:T(8,128)(2,1)}) %all-gather.3.cloned.1.call-update) | async-done | bytes 1048592 | tf_op jit(solution)/shard_map/all_gather | solution.py:266
  104.4 229.1 %while.41 = (s32[]{:T(128)}, bf16[2,8,512,64]{2,3,1,0:T(8,128)(2,1)}, f32[2,8,512]{2,1,0:T(8,128)S(1)}, s32[2]{0:T(128)S(1)}, bf16[2,8,512,64]{2,3,1,0:T(8,128)(...) while((s32[]{:T(128)}, ...), condition=%wide.region_5.6_spmd.clone, body=%wide.region_2.5_spmd.sunk.clone | while | flops 1090515456 | bytes 268814528 | solution.py:290
  106.0 9.2 fusion.263
  115.1 16.0 %reshape.603 = f32[4190208]{0:T(1024)} reshape(f32[8,512,1023]{2,1,0:T(8,128)} %fusion.263) | data formatting | bytes 33521664 | tf_op jit(solution)/shard_map/while
  131.1 16.4 %reshape.604 = f32[8,523776]{1,0:T(8,128)} reshape(f32[4190208]{0:T(1024)} %reshape.603) | data formatting | bytes 33521664 | tf_op jit(solution)/shard_map/while/body/eval_jaxpr/reshape | solution.py:27
  147.6 12.9 %slice.121 = f32[8,523264]{1,0:T(8,128)} slice(f32[8,523776]{1,0:T(8,128)} %reshape.604), slice={[0:8], [511:523775]} | slice | bytes 33488896 | tf_op jit(solution)/shard_map/while/body/eval_jaxpr/slice | solution.py:28
  160.5 13.9 %reshape.605 = f32[4186112]{0:T(1024)} reshape(f32[8,523264]{1,0:T(8,128)} %slice.121) | data formatting | bytes 33488896 | tf_op jit(solution)/shard_map/while
  174.4 18.3 %reshape.606 = f32[8,512,1022]{2,1,0:T(8,128)} reshape(f32[4186112]{0:T(1024)} %reshape.605) | data formatting | bytes 33488896 | tf_op jit(solution)/shard_map/while/body/eval_jaxpr/reshape | solution.py:31
  200.3 9.1 copy.100
  220.2 9.2 fusion.263
  229.4 16.0 %reshape.603 = f32[4190208]{0:T(1024)} reshape(f32[8,512,1023]{2,1,0:T(8,128)} %fusion.263) | data formatting | bytes 33521664 | tf_op jit(solution)/shard_map/while
  245.4 16.4 %reshape.604 = f32[8,523776]{1,0:T(8,128)} reshape(f32[4190208]{0:T(1024)} %reshape.603) | data formatting | bytes 33521664 | tf_op jit(solution)/shard_map/while/body/eval_jaxpr/reshape | solution.py:27
  261.8 12.9 %slice.121 = f32[8,523264]{1,0:T(8,128)} slice(f32[8,523776]{1,0:T(8,128)} %reshape.604), slice={[0:8], [511:523775]} | slice | bytes 33488896 | tf_op jit(solution)/shard_map/while/body/eval_jaxpr/slice | solution.py:28
  274.8 13.9 %reshape.605 = f32[4186112]{0:T(1024)} reshape(f32[8,523264]{1,0:T(8,128)} %slice.121) | data formatting | bytes 33488896 | tf_op jit(solution)/shard_map/while
  288.7 18.3 %reshape.606 = f32[8,512,1022]{2,1,0:T(8,128)} reshape(f32[4186112]{0:T(1024)} %reshape.605) | data formatting | bytes 33488896 | tf_op jit(solution)/shard_map/while/body/eval_jaxpr/reshape | solution.py:31
  314.6 9.1 copy.100
  339.4 20.7 %fusion.81 = (bf16[1024,2048]{1,0:T(8,128)(2,1)S(1)}, f32[1024,2048]{1,0:T(8,128)}) fusion(bf16[1024,512]{1,0:T(8,128)(2,1)S(1)} %get-tuple-element.460, bf16[512,2048]{1,0:T(8,128)(2,1)S(1)} %copy-done), kind=kOutput, calls=%fused_computation.81 | convolution fusion | flops 2283798528 | bytes 15728640 | tf_op jit(solution)/shard_map/dot_general | solution.py:297
  381.3 30.7 %all-gather.5.cloned.1.call-done = bf16[2,512,512]{2,1,0:T(8,128)(2,1)} async-done(((bf16[2,64,512]{2,1,0:T(8,128)(2,1)}), bf16[2,512,512]{2,1,0:T(8,128)(2,1)}) %all-gather.5.cloned.1.call-update) | async-done | bytes 1048592 | tf_op jit(solution)/shard_map/all_gather | solution.py:309
  434.3 458.4 %while.42 = (s32[]{:T(128)}, f32[2,8,512,64]{2,3,1,0:T(8,128)}, f32[2,8,512,64]{2,3,1,0:T(8,128)}, bf16[2,8,512,64]{2,3,1,0:T(8,128)(2,1)}, bf16[2,8,512,64]{2,3...) while((s32[]{:T(128)}, f32[2,8,512,64]{2,3,1,0:T(8,128)}, ...), condition=%wide.region_12.13_spmd.clone, body=%wide.region_10.12_spmd.sunk.clone | while | flops 3243250688 | bytes 513669440 | solution.py:340
  436.0 8.1 fusion.287
  444.1 15.9 %reshape.607 = f32[4190208]{0:T(1024)} reshape(f32[8,512,1023]{2,1,0:T(8,128)} %fusion.287) | data formatting | bytes 33521664 | tf_op jit(solution)/shard_map/while
  460.0 16.4 %reshape.608 = f32[8,523776]{1,0:T(8,128)} reshape(f32[4190208]{0:T(1024)} %reshape.607) | data formatting | bytes 33521664 | tf_op jit(solution)/shard_map/while/body/eval_jaxpr/reshape | solution.py:27
  476.5 12.9 %slice.123 = f32[8,523264]{1,0:T(8,128)} slice(f32[8,523776]{1,0:T(8,128)} %reshape.608), slice={[0:8], [511:523775]} | slice | bytes 33488896 | tf_op jit(solution)/shard_map/while/body/eval_jaxpr/slice | solution.py:28
  489.4 13.9 %reshape.609 = f32[4186112]{0:T(1024)} reshape(f32[8,523264]{1,0:T(8,128)} %slice.123) | data formatting | bytes 33488896 | tf_op jit(solution)/shard_map/while
  503.3 18.2 %reshape.610 = f32[8,512,1022]{2,1,0:T(8,128)} reshape(f32[4186112]{0:T(1024)} %reshape.609) | data formatting | bytes 33488896 | tf_op jit(solution)/shard_map/while/body/eval_jaxpr/reshape | solution.py:31
  529.3 9.1 copy.101
  549.5 11.2 multiply_convert_fusion.3
  580.1 14.2 %reshape.611 = bf16[4186112]{0:T(1024)(128)(2,1)} reshape(bf16[8,512,1022]{2,1,0:T(8,128)(2,1)} %pad.23.clone.3) | data formatting | bytes 16744448 | tf_op jit(solution)/shard_map/while
  594.4 10.2 reshape.612
  604.5 8.0 pad.45
  612.5 19.3 %reshape.613 = bf16[4190208]{0:T(1024)(128)(2,1)} reshape(bf16[8,523776]{1,0:T(8,128)(2,1)} %pad.45) | data formatting | bytes 16760832 | tf_op jit(solution)/shard_map/while
  631.8 17.2 %reshape.614 = bf16[8,512,1023]{2,1,0:T(8,128)(2,1)} reshape(bf16[4190208]{0:T(1024)(128)(2,1)} %reshape.613) | data formatting | bytes 16760832 | tf_op jit(solution)/shard_map/while/body/eval_jaxpr/reshape | solution.py:39
  661.5 8.1 fusion.287
  669.7 15.9 %reshape.607 = f32[4190208]{0:T(1024)} reshape(f32[8,512,1023]{2,1,0:T(8,128)} %fusion.287) | data formatting | bytes 33521664 | tf_op jit(solution)/shard_map/while
  685.6 16.4 %reshape.608 = f32[8,523776]{1,0:T(8,128)} reshape(f32[4190208]{0:T(1024)} %reshape.607) | data formatting | bytes 33521664 | tf_op jit(solution)/shard_map/while/body/eval_jaxpr/reshape | solution.py:27
  702.0 12.9 %slice.123 = f32[8,523264]{1,0:T(8,128)} slice(f32[8,523776]{1,0:T(8,128)} %reshape.608), slice={[0:8], [511:523775]} | slice | bytes 33488896 | tf_op jit(solution)/shard_map/while/body/eval_jaxpr/slice | solution.py:28
  714.9 13.9 %reshape.609 = f32[4186112]{0:T(1024)} reshape(f32[8,523264]{1,0:T(8,128)} %slice.123) | data formatting | bytes 33488896 | tf_op jit(solution)/shard_map/while
  728.9 18.2 %reshape.610 = f32[8,512,1022]{2,1,0:T(8,128)} reshape(f32[4186112]{0:T(1024)} %reshape.609) | data formatting | bytes 33488896 | tf_op jit(solution)/shard_map/while/body/eval_jaxpr/reshape | solution.py:31
  747.1 7.7 slice.124
  754.8 9.1 copy.101
  774.8 11.0 multiply_convert_fusion.3
  805.3 14.2 %reshape.611 = bf16[4186112]{0:T(1024)(128)(2,1)} reshape(bf16[8,512,1022]{2,1,0:T(8,128)(2,1)} %pad.23.clone.3) | data formatting | bytes 16744448 | tf_op jit(solution)/shard_map/while
  819.5 10.2 reshape.612
  829.7 8.0 pad.45
  837.7 19.5 %reshape.613 = bf16[4190208]{0:T(1024)(128)(2,1)} reshape(bf16[8,523776]{1,0:T(8,128)(2,1)} %pad.45) | data formatting | bytes 16760832 | tf_op jit(solution)/shard_map/while
  857.2 17.2 %reshape.614 = bf16[8,512,1023]{2,1,0:T(8,128)(2,1)} reshape(bf16[4190208]{0:T(1024)(128)(2,1)} %reshape.613) | data formatting | bytes 16760832 | tf_op jit(solution)/shard_map/while/body/eval_jaxpr/reshape | solution.py:39
  938.3 42.7 %all-reduce.2 = (f32[512]{0:T(512)}, f32[512]{0:T(512)}, f32[512]{0:T(512)}, f32[512]{0:T(512)}) all-reduce(f32[512]{0:T(512)S(1)} %get-tuple-element.395, f32[512]{0:T(512)S(1)} %get-tuple-element.394, f32[512]{0:T(512)S(1)} %get-tuple-element.393, f32[512]{0:T(512)S(1)} %get-tuple-element.392), channel_id=1, replica_groups=mesh['batch'=4,'seq'=8] {'batch','seq'}, use_global_device_ids=true, to_apply=%region_17.18 | all-reduce | flops 2048 | bytes 16384 | tf_op jit(solution)/shard_map/psum | solution.py:376
  984.1 262.7 %all-reduce.10.cloned.1.call-done = (f32[1536,512]{1,0:T(8,128)}, f32[512,512]{1,0:T(8,128)}, f32[512,512]{1,0:T(8,128)}, f32[512,512]{1,0:T(8,128)}, f32[512,51...) async-done(((f32[1536,512]{1,0:T(8,128)}, f32[512,512]{1,0:T(8,128)}, f32[512,512]{1,0:T(8,128)}, f32[512,512]{1,0:T(8,128)}, ...) | async-done | bytes 18874384 | tf_op jit(solution)/shard_map/psum | solution.py:376
  (323 shorter events, 309.7 us)
Async XLA Ops:
  7.2 332.2 %copy-start = (bf16[512,2048]{1,0:T(8,128)(2,1)S(1)}, bf16[512,2048]{1,0:T(8,128)(2,1)}, u32[]{:S(2)}) copy-start(bf16[512,2048]{1,0:T(8,128)(2,1)} %param.49) | copy-start | bytes 6291460
  7.2 14.7 %copy-start.67 = (s32[2]{0:T(128)S(1)}, s32[2]{0:T(128)}, u32[]{:S(2)}) copy-start(s32[2]{0:T(128)} %param.35) | copy-start | bytes 28
  7.2 53.4 %all-gather.3.cloned.1.call-start = ((), (), s32[]{:S(2)}) async-start(), calls=%async_computation | async-start | bytes 1179648 | tf_op jit(solution)/shard_map/all_gather | solution.py:266
  8.1 6.2 collective-permute-start
  15.6 11.2 copy-start.21
  18.2 393.8 %all-gather.5.cloned.1.call-start = ((), (), s32[]{:S(2)}) async-start(), calls=%async_computation.1 | async-start | bytes 1179648 | tf_op jit(solution)/shard_map/all_gather | solution.py:309
  20.9 43.5 %copy-start.60 = (f32[512]{0:T(512)S(1)}, f32[512]{0:T(512)}, u32[]{:S(2)}) copy-start(f32[512]{0:T(512)} %param.38) | copy-start | bytes 6148
  20.9 43.5 %copy-start.64 = (f32[512]{0:T(512)S(1)}, f32[512]{0:T(512)}, u32[]{:S(2)}) copy-start(f32[512]{0:T(512)} %param.39) | copy-start | bytes 6148
  60.6 6.5 copy-start.42
  62.1 11.5 copy-start.52
  64.4 9.2 copy-start.54
  333.5 3.6 copy-start.50
  333.5 3.6 copy-start.69
  339.4 20.7 %copy-start.33 = (bf16[1024,512]{1,0:T(8,128)(2,1)}, bf16[1024,512]{1,0:T(8,128)(2,1)S(1)}, u32[]{:S(2)}) copy-start(bf16[1024,512]{1,0:T(8,128)(2,1)S(1)} %get-tuple-element.460) | copy-start | bytes 3145732
  339.4 20.7 %copy-start.68 = (bf16[2048,512]{1,0:T(8,128)(2,1)S(1)}, bf16[2048,512]{1,0:T(8,128)(2,1)}, u32[]{:S(2)}) copy-start(bf16[2048,512]{1,0:T(8,128)(2,1)} %param.50) | copy-start | bytes 6291460
  362.4 4.2 copy-start.29
  364.4 10.8 copy-start.59
  364.4 10.8 copy-start.62
  372.9 609.1 %all-reduce.8.cloned.1.call-start = ((), (), s32[]{:S(2)}) async-start(), calls=%async_computation.2 | async-start | bytes 1048576 | tf_op jit(solution)/shard_map/psum | solution.py:394
  412.0 7.4 copy-start.13
  425.2 9.1 copy-start.5
  425.2 9.1 copy-start.6
  425.2 9.1 copy-start.51
  425.2 9.1 copy-start.70
  538.4 8.9 copy-start.12
  544.0 3.2 copy-start.4
  560.6 4.6 copy-start.3
  649.0 6.1 copy-start.2
  649.0 6.7 copy-start.25
  763.9 8.6 copy-start.12
  769.3 3.2 copy-start.4
  785.8 4.6 copy-start.3
  874.4 6.1 copy-start.2
  874.4 6.7 copy-start.25
  895.4 4.3 copy-start.10
  897.1 349.8 %all-reduce.10.cloned.1.call-start = ((), (), s32[]{:S(2)}) async-start(), calls=%async_computation.3 | async-start | bytes 37748736 | tf_op jit(solution)/shard_map/psum | solution.py:376
  897.1 4.0 copy-start.40
  906.5 6.5 copy-start.14
  918.1 6.3 copy-start.22
  928.1 52.8 %copy-start.30 = (bf16[2,192,512]{2,1,0:T(8,128)(2,1)S(1)}, bf16[2,192,512]{2,1,0:T(8,128)(2,1)}, u32[]{:S(2)}) copy-start(bf16[2,192,512]{2,1,0:T(8,128)(2,1)} %param.36) | copy-start | bytes 1179652
  935.9 45.0 %collective-permute-start.1 = (f32[2,2,512]{2,1,0:T(2,128)S(1)}, f32[2,2,512]{2,1,0:T(2,128)S(1)}, u32[]{:S(2)}, u32[]{:S(2)}) collective-permute-start(f32[2,2,512]{2,1,0:T(2,128)S(1)} %slice.108), channel_id=1, source_target_pairs={{1,0},{2,1},{3,2},{4,3},{5,4},{6,5},{7,6},{9,8},{10,9},{11,10},{12... | collective-permute-start | bytes 24584 | tf_op jit(solution)/shard_map/ppermute | solution.py:13
  1246.8 4.0 copy-start.38
  1246.8 5.0 copy-start.37
  1246.8 6.0 copy-start.36
  1250.9 3.9 copy-start.20
  1254.8 3.7 copy-start.19
  1258.5 3.4 copy-start.23
  1258.5 5.1 copy-start.1
  (38 other events, 69.5 us)
Sparse Core Ops, SparseCore 0:
  18.3 42.2 all-gather.2
  373.0 38.9 all-gather.4
  897.2 31.8 all-reduce.7
  937.0 309.7 all-reduce.9
where the time goes:
time: 1280 us; the launch traced here: 1270 us
  local copies, waits for them, and re-layouts  635 us (50%)
  waiting for transfers between devices  326 us (25%)
  matrix products  196 us (15%)
  blocking collectives  48.3 us (4%)
  other arithmetic  34.9 us (3%)
  between operations  15.1 us (1%)
    psum x1, waiting for transfers between devices, body(): lax.psum((pool_grad, upsample_grad, norm1_gain_grad, norm1_bias_grad, que...  263 us
    while x54, local copies, waits for them, and re-layouts  249 us
    reshape x4, local copies, waits for them, and re-layouts, skew_scores(): flattened.reshape(head_count, block_rows, extent_length - 1)  73 us
    reshape x4, local copies, waits for them, and re-layouts, skew_scores(): flattened = scattered_rows.reshape(head_count, block_rows * extent_length)  65.8 us
    slice x4, local copies, waits for them, and re-layouts, skew_scores(): lax.slice_in_dim(flattened, block_rows - 1, block_rows - 1 + block_rows *...  51.6 us
    psum x1, blocking collectives, body(): lax.psum((pool_grad, upsample_grad, norm1_gain_grad, norm1_bias_grad, que...  42.7 us
    dot_general x4, matrix products, block_logits(): jnp.einsum('hnd,hed->hne', query_location[:, leading_index:key_total], po...  34.6 us
    reshape x2, local copies, waits for them, and re-layouts, unskew_scores(): return flattened.reshape(head_count, block_rows, extent_length)  34.4 us
  transfers between devices with their start and end apart: 6, of which 4 were waited for; matrix products, arithmetic and copies ran while one was open for 4% of the time, Pallas kernels for 0%

commit v1 on v0

v1 whole, which is shorter than its diff:
```python
import functools

import jax
import jax.numpy as jnp
import numpy as np
from jax import lax
from jax.experimental import pallas as pl
from jax.experimental.pallas import tpu as pltpu
from jax.sharding import PartitionSpec as P

MESH = pl.DeviceIdType.MESH
epsilon = 1e-05
masked_value = -1e30
BLOCK = 128
LANES = 128
VMEM = pl.BlockSpec(memory_space=pltpu.VMEM)
SMEM = pl.BlockSpec(memory_space=pltpu.SMEM)
ANY = pl.BlockSpec(memory_space=pl.ANY)


def dot(left, right):
    return jnp.dot(left, right, preferred_element_type=jnp.float32)


def dot_nt(left, right):
    return lax.dot_general(
        left, right, (((1,), (1,)), ((), ())), preferred_element_type=jnp.float32
    )


def dot_tn(left, right):
    return lax.dot_general(
        left, right, (((0,), (0,)), ((), ())), preferred_element_type=jnp.float32
    )


def low(value):
    return value.astype(jnp.bfloat16)


def distance_table(short_len, width):
    distance = (short_len - 1 - np.arange(short_len)).astype(np.float32)
    steps_in = np.arange(0, width, 2).astype(np.float32)
    frequency = np.exp(-np.log(np.float32(10000.0)) * steps_in / np.float32(width))
    angles = distance[:, None] * frequency[None, :].astype(np.float32)
    both = np.concatenate([np.sin(angles), np.cos(angles)], axis=1)
    return jnp.asarray(both.astype(jnp.bfloat16))


def norm_rows(rows):
    mean = jnp.mean(rows, axis=-1, keepdims=True)
    centered = rows - mean
    inverse = lax.rsqrt(jnp.mean(centered * centered, axis=-1, keepdims=True) + epsilon)
    return centered * inverse, inverse


def norm_backward(gradient, normed, inverse, gain):
    scaled = gradient * gain
    return inverse * (
        scaled
        - jnp.mean(scaled, axis=-1, keepdims=True)
        - normed * jnp.mean(scaled * normed, axis=-1, keepdims=True)
    )


class Sizes:
    def __init__(self, n, items, full_rows, width, heads):
        self.n = n
        self.items = items
        self.r = full_rows // 3
        self.width = width
        self.heads = heads
        self.hd = width // heads
        self.units = items * heads // n
        self.length = n * self.r
        self.rows = items * self.r
        assert n % heads == 0 and self.units * self.hd <= LANES


def greet(n, me):
    barrier = pltpu.get_barrier_semaphore()
    for step in range(1, n):
        pl.semaphore_signal(
            barrier, inc=1, device_id={"seq": lax.rem(me + step, n)}, device_id_type=MESH
        )
    pl.semaphore_wait(barrier, n - 1)


def send_all(n, me, source, target, send_sem, recv_sem):
    copies = []
    for step in range(1, n):
        peer = lax.rem(me + step, n)
        copies.append(
            pltpu.make_async_remote_copy(
                src_ref=source(peer),
                dst_ref=target.at[me],
                send_sem=send_sem.at[step],
                recv_sem=recv_sem.at[step],
                device_id={"seq": peer},
                device_id_type=MESH,
            )
        )
        copies[-1].start()
    return copies


def rows_by_three(z, x_ref, xf_ref):
    for item in range(z.items):
        for slab in range(z.width // LANES):
            xf_ref[item, slab, 8:, :] = x_ref[item, :, slab * LANES : (slab + 1) * LANES].astype(
                jnp.float32
            )


def every_third(z, xf_ref, first):
    items = []
    for item in range(z.items):
        slabs = [
            xf_ref[item, slab, pl.ds(first, z.r, stride=3), :] for slab in range(z.width // LANES)
        ]
        items.append(jnp.concatenate(slabs, axis=1))
    return jnp.concatenate(items, axis=0)


def set_every_third(z, xf_ref, first, value):
    for item in range(z.items):
        for slab in range(z.width // LANES):
            xf_ref[item, slab, pl.ds(first, z.r, stride=3), :] = value[
                item * z.r : (item + 1) * z.r, slab * LANES : (slab + 1) * LANES
            ]


def forward_kernel(
    z,
    counts_ref,
    x_ref,
    pool_w,
    gain_ref,
    bias_ref,
    query_w,
    key_w,
    value_w,
    position_w,
    cb_ref,
    pb_ref,
    table_ref,
    pooled_ref,
    recv_ref,
    attn_in_ref,
    qc_ref,
    qp_ref,
    k_ref,
    v_ref,
    pos_ref,
    probs_ref,
    xf_ref,
    tail_ref,
    halo_ref,
    gather_ref,
    out_ref,
    halo_sems,
    gather_send,
    gather_recv,
    out_send,
    out_recv,
    own_sem,
):
    n, r, width, hd = z.n, z.r, z.width, z.hd
    me = lax.axis_index("seq")
    head = lax.rem(me, z.heads)
    group = lax.div(me, z.heads)
    greet(n, me)
    tail_ref[...] = x_ref[:, 3 * r - 16 :, :]
    halo = pltpu.make_async_remote_copy(
        src_ref=tail_ref,
        dst_ref=halo_ref,
        send_sem=halo_sems.at[0],
        recv_sem=halo_sems.at[1],
        device_id={"seq": lax.rem(me + 1, n)},
        device_id_type=MESH,
    )
    halo.start()
    rows_by_three(z, x_ref, xf_ref)
    halo.wait()
    for item in range(z.items):
        before = jnp.where(me > 0, halo_ref[item].astype(jnp.float32), 0.0)
        for slab in range(width // LANES):
            xf_ref[item, slab, 0:8, :] = before[8:16, slab * LANES : (slab + 1) * LANES]
    pooled = jnp.zeros((z.rows, width), jnp.float32)
    for part in range(3):
        pooled += dot(
            low(every_third(z, xf_ref, 6 + part)), pool_w[part * width : (part + 1) * width, :]
        )
    pooled_ref[...] = low(pooled).reshape(z.items, r, width)

    def items_of(peer):
        return pooled_ref.at[pl.ds(lax.div(peer, z.heads) * z.units, z.units)]

    copies = send_all(n, me, items_of, gather_ref, gather_send, gather_recv)
    gather_ref[me] = pooled_ref[pl.ds(group * z.units, z.units)]
    lane_pair = pl.multiple_of(lax.div(head * hd, LANES) * LANES, LANES)
    pair = pl.ds(lane_pair, LANES)
    turn = lax.rem(head * hd, LANES)

    def own_half(value):
        return pltpu.roll(value, LANES - turn, 1)[:, :hd]

    pos_ref[...] = low(own_half(dot(table_ref[...], position_w[:, pair])))
    for copy in copies:
        copy.wait()
    weights = jnp.concatenate([query_w[:, pair], key_w[:, pair], value_w[:, pair]], axis=1)
    content_bias = cb_ref[pl.ds(head, 1), :]
    position_bias = pb_ref[pl.ds(head, 1), :]
    for unit in range(z.units):
        normed, _ = norm_rows(gather_ref[:, unit].reshape(z.length, width).astype(jnp.float32))
        attn_in_ref[unit] = low(normed * gain_ref[...] + bias_ref[...])
        qkv = dot(attn_in_ref[unit], weights)
        queries = own_half(qkv[:, :LANES])
        qc_ref[unit] = low(queries + content_bias)
        qp_ref[unit] = low(queries + position_bias)
        k_ref[unit] = low(own_half(qkv[:, LANES : 2 * LANES]))
        v_ref[unit] = low(own_half(qkv[:, 2 * LANES :]))
    for block in range(z.length // BLOCK):
        lo, hi = block * BLOCK, (block + 1) * BLOCK
        sides = []
        for unit in range(z.units):
            count = counts_ref[group * z.units + unit]
            content = dot_nt(qc_ref[unit, lo:hi, :], k_ref[unit, :hi, :])
            by_distance = dot_nt(qp_ref[unit, lo:hi, :], pos_ref[z.length - hi :, :])
            placed = pltpu.roll(by_distance, lo + 1, 1, stride=1, stride_axis=0)
            query_at = lo + lax.broadcasted_iota(jnp.int32, (BLOCK, hi), 0)
            key_at = lax.broadcasted_iota(jnp.int32, (BLOCK, hi), 1)
            valid = (key_at <= query_at) & (key_at < count)
            logits = jnp.where(valid, (content + placed) * hd**-0.5, masked_value)
            raised = jnp.exp(logits - jnp.max(logits, axis=-1, keepdims=True))
            probs = raised / jnp.sum(raised, axis=-1, keepdims=True)
            probs_ref[unit, lo:hi, :hi] = probs
            sides.append(low(dot(low(probs), v_ref[unit, :hi, :])))
        sides += [jnp.zeros((BLOCK, hd), jnp.bfloat16)] * (LANES // hd - z.units)
        per = BLOCK // r
        out_ref[block * per : (block + 1) * per] = jnp.concatenate(sides, axis=1).reshape(
            per, r, LANES
        )
    copies = send_all(n, me, lambda peer: out_ref.at[peer], recv_ref, out_send, out_recv)
    own = pltpu.make_async_copy(out_ref.at[me], recv_ref.at[me], own_sem)
    own.start()
    for copy in copies:
        copy.wait()
    own.wait()


def live_rows(z, me, length, part):
    at = lax.broadcasted_iota(jnp.int32, (z.r, 1), 0) * 3 + part + me * 3 * z.r
    return (at < length).astype(jnp.float32)


def middle_kernel(
    z,
    lengths_ref,
    att_recv_ref,
    pooled_ref,
    x_ref,
    og_ref,
    output_w,
    gain_ref,
    bias_ref,
    inner_w,
    outer_w,
    up_w,
    block_ref,
    recv_ref,
    hidden_grad_ref,
    up_grad_ref,
    outer_grad_ref,
    inner_grad_ref,
    output_grad_ref,
    norm_grad_ref,
    xf_ref,
    att_ref,
    act_ref,
    slope_ref,
    inner_low_ref,
    up_rows_ref,
    out_ref,
    out_send,
    out_recv,
    own_sem,
):
    n, r, width, hd = z.n, z.r, z.width, z.hd
    me = lax.axis_index("seq")
    greet(n, me)
    ff = inner_w.shape[1]
    step = min(512, ff)

    def live(part):
        return jnp.concatenate(
            [live_rows(z, me, lengths_ref[item], part) for item in range(z.items)], axis=0
        )

    rows_by_three(z, og_ref, xf_ref)
    for part in range(3):
        up_rows_ref[:, part * width : (part + 1) * width] = low(
            every_third(z, xf_ref, 8 + part) * live(part)
        )
    summed_grad = low(dot_nt(up_rows_ref[...], up_w[...]))
    for source in range(n):
        for unit in range(z.units):
            item = source // z.heads * z.units + unit
            head = source % z.heads
            att_ref[item * r : (item + 1) * r, head * hd : (head + 1) * hd] = att_recv_ref[
                source, :, unit * hd : (unit + 1) * hd
            ]
    short = pooled_ref[...].reshape(z.rows, width).astype(jnp.float32)
    hidden = short + dot(att_ref[...], output_w[...])
    normed, inverse = norm_rows(hidden)
    ffn_in = low(normed * gain_ref[...] + bias_ref[...])
    for lo in range(0, ff, step):
        inner = dot(ffn_in, inner_w[:, lo : lo + step])
        normal_cdf = 0.5 * (1.0 + lax.erf(inner * 0.7071067811865476))
        density = jnp.exp(-0.5 * inner * inner) * 0.3989422804014327
        act_ref[:, lo : lo + step] = low(inner * normal_cdf)
        slope_ref[:, lo : lo + step] = normal_cdf + inner * density
    for lo in range(0, ff, step):
        inner_low_ref[:, lo : lo + step] = low(
            dot_nt(summed_grad, outer_w[lo : lo + step, :]) * slope_ref[:, lo : lo + step]
        )
    ffn_grad = dot_nt(inner_low_ref[...], inner_w[...])
    norm_grad_ref[0:1, :] = jnp.sum(ffn_grad * normed, axis=0, keepdims=True)
    norm_grad_ref[1:2, :] = jnp.sum(ffn_grad, axis=0, keepdims=True)
    hidden_grad = summed_grad.astype(jnp.float32) + norm_backward(
        ffn_grad, normed, inverse, gain_ref[...]
    )
    hidden_grad_ref[...] = hidden_grad
    branch = low(hidden_grad)
    att_grad = low(dot_nt(branch, output_w[...]))
    for target in range(n):
        head = target % z.heads
        sides = []
        for unit in range(z.units):
            item = target // z.heads * z.units + unit
            sides.append(att_grad[item * r : (item + 1) * r, head * hd : (head + 1) * hd])
        sides += [jnp.zeros((r, hd), jnp.bfloat16)] * (LANES // hd - z.units)
        out_ref[target] = jnp.concatenate(sides, axis=1)
    copies = send_all(n, me, lambda peer: out_ref.at[peer], recv_ref, out_send, out_recv)
    own = pltpu.make_async_copy(out_ref.at[me], recv_ref.at[me], own_sem)
    own.start()
    summed = low(hidden + dot(act_ref[...], outer_w[...]))
    rows_by_three(z, x_ref, xf_ref)
    for part in range(3):
        up = dot(summed, up_w[:, part * width : (part + 1) * width])
        set_every_third(
            z, xf_ref, 8 + part, every_third(z, xf_ref, 8 + part) + up * live(part)
        )
    for item in range(z.items):
        for slab in range(width // LANES):
            block_ref[item, :, slab * LANES : (slab + 1) * LANES] = low(xf_ref[item, slab, 8:, :])
    for part in range(3):
        cut = slice(part * width, (part + 1) * width)
        up_grad_ref[:, cut] = low(dot_tn(summed, up_rows_ref[:, cut]))
    for lo in range(0, ff, step):
        cut = slice(lo, lo + step)
        outer_grad_ref[cut, :] = low(dot_tn(act_ref[:, cut], summed_grad))
        inner_grad_ref[:, cut] = low(dot_tn(ffn_in, inner_low_ref[:, cut]))
    output_grad_ref[...] = low(dot_tn(att_ref[...], branch))
    for copy in copies:
        copy.wait()
    own.wait()


def reversal():
    at = lax.broadcasted_iota(jnp.int32, (BLOCK, BLOCK), 0)
    across = lax.broadcasted_iota(jnp.int32, (BLOCK, BLOCK), 1)
    return low((at + across == BLOCK - 1).astype(jnp.float32))


def backward_kernel(
    z,
    grad_recv_ref,
    attn_in_ref,
    qc_ref,
    qp_ref,
    k_ref,
    v_ref,
    pos_ref,
    probs_ref,
    table_ref,
    recv_ref,
    head_grad_ref,
    bias_grad_ref,
    query_grad_ref,
    key_t_ref,
    value_t_ref,
    table_t_ref,
    out_ref,
    out_send,
    out_recv,
    own_sem,
):
    n, r, hd = z.n, z.r, z.hd
    length = z.length
    me = lax.axis_index("seq")
    greet(n, me)
    flip = reversal()
    content_sum = jnp.zeros((1, hd), jnp.float32)
    position_sum = jnp.zeros((1, hd), jnp.float32)
    key_t_ref[...] = jnp.zeros_like(key_t_ref)
    value_t_ref[...] = jnp.zeros_like(value_t_ref)
    table_t_ref[...] = jnp.zeros_like(table_t_ref)
    for unit in range(z.units):
        att_grad = grad_recv_ref[:, :, unit * hd : (unit + 1) * hd].reshape(length, hd)
        for block in range(length // BLOCK):
            lo, hi = block * BLOCK, (block + 1) * BLOCK
            block_grad = att_grad[lo:hi]
            probs = probs_ref[unit, lo:hi, :hi]
            prob_grad = dot_nt(block_grad, v_ref[unit, :hi, :])
            delta = jnp.sum(probs * prob_grad, axis=-1, keepdims=True)
            raw = low(probs * (prob_grad - delta) * hd**-0.5)
            content = dot(raw, k_ref[unit, :hi, :])
            key_t_ref[unit, :, :hi] += dot_tn(qc_ref[unit, lo:hi, :], raw)
            value_t_ref[unit, :, :hi] += dot_tn(block_grad, low(probs))
            by_distance = low(pltpu.roll(dot(flip, raw), 0, 1, stride=1, stride_axis=0))
            position = dot(by_distance, pos_ref[length - hi :, :])
            upper = low(position)
            lower = low(position - upper.astype(jnp.float32))
            position = dot(flip, upper) + dot(flip, lower)
            flipped_q = low(dot(flip, qp_ref[unit, lo:hi, :]))
            table_t_ref[unit, :, length - hi :] += dot_tn(flipped_q, by_distance)
            content_sum += jnp.sum(content, axis=0, keepdims=True)
            position_sum += jnp.sum(position, axis=0, keepdims=True)
            query_grad_ref[unit, lo:hi, :] = low(content + position)
    bias_grad_ref[0:1, :] = content_sum
    bias_grad_ref[1:2, :] = position_sum
    pad = [jnp.zeros((length, hd), jnp.bfloat16)] * (LANES // hd - z.units)
    sides = [query_grad_ref[unit] for unit in range(z.units)] + pad
    sides += [low(key_t_ref[unit].T) for unit in range(z.units)] + pad
    sides += [low(value_t_ref[unit].T) for unit in range(z.units)] + pad
    out_ref[...] = jnp.concatenate(sides, axis=1).reshape(n, r, 3 * LANES)
    copies = send_all(n, me, lambda peer: out_ref.at[peer], recv_ref, out_send, out_recv)
    own = pltpu.make_async_copy(out_ref.at[me], recv_ref.at[me], own_sem)
    own.start()
    query_sum = key_sum = value_sum = table_sum = 0.0
    for unit in range(z.units):
        query_sum += dot_tn(query_grad_ref[unit], attn_in_ref[unit])
        key_sum += dot(low(key_t_ref[unit]), attn_in_ref[unit])
        value_sum += dot(low(value_t_ref[unit]), attn_in_ref[unit])
        table_sum += dot(low(table_t_ref[unit]), table_ref[...])
    head_grad_ref[...] = jnp.concatenate([query_sum, key_sum, value_sum, table_sum], axis=0)
    for copy in copies:
        copy.wait()
    own.wait()


def last_kernel(
    z,
    recv_ref,
    hidden_grad_ref,
    pooled_ref,
    x_ref,
    og_ref,
    gain_ref,
    query_w,
    key_w,
    value_w,
    pool_w,
    input_grad_ref,
    pool_grad_ref,
    norm_grad_ref,
    xf_ref,
    of_ref,
    dq_ref,
    grad_ref,
    head_ref,
    halo_ref,
    halo_sems,
):
    n, r, width, hd = z.n, z.r, z.width, z.hd
    me = lax.axis_index("seq")
    greet(n, me)
    for source in range(n):
        for unit in range(z.units):
            item = source // z.heads * z.units + unit
            head = source % z.heads
            for which in range(3):
                dq_ref[which, item * r : (item + 1) * r, head * hd : (head + 1) * hd] = recv_ref[
                    source, :, which * LANES + unit * hd : which * LANES + (unit + 1) * hd
                ]
    attn_grad = (
        dot_nt(dq_ref[0], query_w[...])
        + dot_nt(dq_ref[1], key_w[...])
        + dot_nt(dq_ref[2], value_w[...])
    )
    normed, inverse = norm_rows(pooled_ref[...].reshape(z.rows, width).astype(jnp.float32))
    norm_grad_ref[0:1, :] = jnp.sum(attn_grad * normed, axis=0, keepdims=True)
    norm_grad_ref[1:2, :] = jnp.sum(attn_grad, axis=0, keepdims=True)
    short_grad = low(
        hidden_grad_ref[...] + norm_backward(attn_grad, normed, inverse, gain_ref[...])
    )
    for item in range(z.items):
        head_ref[item] = short_grad[item * r : item * r + 16, :]
        grad_ref[item, 0:r, :] = short_grad[item * r : (item + 1) * r, :].astype(jnp.float32)
    halo = pltpu.make_async_remote_copy(
        src_ref=head_ref,
        dst_ref=halo_ref,
        send_sem=halo_sems.at[0],
        recv_sem=halo_sems.at[1],
        device_id={"seq": lax.rem(me + n - 1, n)},
        device_id_type=MESH,
    )
    halo.start()
    rows_by_three(z, x_ref, xf_ref)
    rows_by_three(z, og_ref, of_ref)
    pool_grad_ref[2 * width :, :] = low(dot_tn(low(every_third(z, xf_ref, 8)), short_grad))
    own = dot_nt(short_grad, pool_w[2 * width :, :])
    set_every_third(z, of_ref, 8, every_third(z, of_ref, 8) + own)
    halo.wait()
    for item in range(z.items):
        after = jnp.where(me < n - 1, halo_ref[item].astype(jnp.float32), 0.0)
        grad_ref[item, r : r + 8, :] = after[0:8, :]
    later = low(
        jnp.concatenate([grad_ref[item, 1 : r + 1, :] for item in range(z.items)], axis=0)
    )
    for part in range(2):
        cut = slice(part * width, (part + 1) * width)
        first = 9 + part
        pool_grad_ref[cut, :] = low(dot_tn(low(every_third(z, xf_ref, first)), later))
        back = dot_nt(later, pool_w[cut, :])
        set_every_third(z, of_ref, first, every_third(z, of_ref, first) + back)
    for item in range(z.items):
        for slab in range(width // LANES):
            input_grad_ref[item, :, slab * LANES : (slab + 1) * LANES] = of_ref[item, slab, 8:, :]


def call(kernel, z, collective_id, ins, outs, scratch, args):
    return pl.pallas_call(
        functools.partial(kernel, z),
        out_shape=[jax.ShapeDtypeStruct(shape, dtype) for shape, dtype, _ in outs],
        in_specs=ins,
        out_specs=[space for _, _, space in outs],
        scratch_shapes=scratch,
        compiler_params=pltpu.CompilerParams(
            collective_id=collective_id, has_side_effects=True, vmem_limit_bytes=50 * 2**20
        ),
    )(*args)


def body(
    byte_rows,
    item_lengths,
    out_grad,
    pool_weight,
    norm1_gain,
    norm1_bias,
    query_weight,
    key_weight,
    value_weight,
    position_weight,
    content_bias,
    position_bias,
    output_weight,
    norm2_gain,
    norm2_bias,
    inner_weight,
    outer_weight,
    upsample_weight,
):
    items, full_rows, width = byte_rows.shape
    heads, hd = content_bias.shape
    n = lax.axis_size("seq")
    ff = inner_weight.shape[1]
    z = Sizes(n, items, full_rows, width, heads)
    r, units, length, rows = z.r, z.units, z.length, z.rows
    bf, f4 = jnp.bfloat16, jnp.float32
    slabs = width // LANES
    dma = pltpu.SemaphoreType.DMA
    counts = item_lengths // 3
    table = distance_table(length, width)
    gain1, bias1 = norm1_gain.reshape(1, width), norm1_bias.reshape(1, width)
    gain2, bias2 = norm2_gain.reshape(1, width), norm2_bias.reshape(1, width)
    xf = pltpu.VMEM((items, slabs, 3 * r + 8, LANES), f4)
    (pooled, att_recv, attn_in, qc, qp, keys, values, positions, probs) = call(
        forward_kernel,
        z,
        0,
        [SMEM] + [VMEM] * 11,
        [
            ((items, r, width), bf, VMEM),
            ((n, r, LANES), bf, ANY),
            ((units, length, width), bf, VMEM),
            ((units, length, hd), bf, VMEM),
            ((units, length, hd), bf, VMEM),
            ((units, length, hd), bf, VMEM),
            ((units, length, hd), bf, VMEM),
            ((length, hd), bf, VMEM),
            ((units, length, length), f4, VMEM),
        ],
        [
            xf,
            pltpu.VMEM((items, 16, width), bf),
            pltpu.VMEM((items, 16, width), bf),
            pltpu.VMEM((n, units, r, width), bf),
            pltpu.VMEM((n, r, LANES), bf),
            dma((2,)),
            dma((n,)),
            dma((n,)),
            dma((n,)),
            dma((n,)),
            dma,
        ],
        (
            counts,
            byte_rows,
            pool_weight,
            gain1,
            bias1,
            query_weight,
            key_weight,
            value_weight,
            position_weight,
            content_bias,
            position_bias,
            table,
        ),
    )
    (block_out, grad_recv, hidden_grad, up_g, outer_g, inner_g, output_g, norm2_g) = call(
        middle_kernel,
        z,
        1,
        [SMEM] + [VMEM] * 10,
        [
            ((items, full_rows, width), bf, VMEM),
            ((n, r, LANES), bf, ANY),
            ((rows, width), f4, VMEM),
            ((width, 3 * width), bf, VMEM),
            ((ff, width), bf, VMEM),
            ((width, ff), bf, VMEM),
            ((width, width), bf, VMEM),
            ((2, width), f4, VMEM),
        ],
        [
            xf,
            pltpu.VMEM((rows, width), bf),
            pltpu.VMEM((rows, ff), bf),
            pltpu.VMEM((rows, ff), f4),
            pltpu.VMEM((rows, ff), bf),
            pltpu.VMEM((rows, 3 * width), bf),
            pltpu.VMEM((n, r, LANES), bf),
            dma((n,)),
            dma((n,)),
            dma,
        ],
        (
            item_lengths,
            att_recv,
            pooled,
            byte_rows,
            out_grad,
            output_weight,
            gain2,
            bias2,
            inner_weight,
            outer_weight,
            upsample_weight,
        ),
    )
    qkv_recv, head_g, head_bias_g = call(
        backward_kernel,
        z,
        2,
        [VMEM] * 9,
        [
            ((n, r, 3 * LANES), bf, ANY),
            ((4 * hd, width), f4, VMEM),
            ((2, hd), f4, VMEM),
        ],
        [
            pltpu.VMEM((units, length, hd), bf),
            pltpu.VMEM((units, hd, length), f4),
            pltpu.VMEM((units, hd, length), f4),
            pltpu.VMEM((units, hd, length), f4),
            pltpu.VMEM((n, r, 3 * LANES), bf),
            dma((n,)),
            dma((n,)),
            dma,
        ],
        (grad_recv, attn_in, qc, qp, keys, values, positions, probs, table),
    )
    input_grad, pool_g, norm1_g = call(
        last_kernel,
        z,
        3,
        [VMEM] * 10,
        [
            ((items, full_rows, width), f4, VMEM),
            ((3 * width, width), bf, VMEM),
            ((2, width), f4, VMEM),
        ],
        [
            xf,
            xf,
            pltpu.VMEM((3, rows, width), bf),
            pltpu.VMEM((items, r + 8, width), f4),
            pltpu.VMEM((items, 16, width), bf),
            pltpu.VMEM((items, 16, width), bf),
            dma((2,)),
        ],
        (
            qkv_recv,
            hidden_grad,
            pooled,
            byte_rows,
            out_grad,
            gain1,
            query_weight,
            key_weight,
            value_weight,
            pool_weight,
        ),
    )
    dense = lax.psum((pool_g, up_g, outer_g, inner_g, output_g), ("batch", "seq"))
    pool_t, up_t, outer_t, inner_t, output_t = (value.astype(f4) for value in dense)
    norm_t = lax.psum(jnp.concatenate([norm1_g, norm2_g]), ("batch", "seq"))
    head_t = lax.all_gather(lax.psum(head_g.astype(bf), "batch"), "seq", axis=0)
    head_t = jnp.sum(head_t.reshape(n // heads, heads, 4, hd, width).astype(f4), axis=0)
    head_t = head_t.transpose(1, 3, 0, 2).reshape(4, width, width)
    bias_t = lax.all_gather(lax.psum(head_bias_g, "batch"), "seq", axis=0)
    bias_t = jnp.sum(bias_t.reshape(n // heads, heads, 2, hd), axis=0)
    return (
        block_out,
        input_grad,
        pool_t,
        norm_t[0],
        norm_t[1],
        head_t[0],
        head_t[1],
        head_t[2],
        head_t[3],
        bias_t[:, 0],
        bias_t[:, 1],
        output_t,
        norm_t[2],
        norm_t[3],
        inner_t,
        outer_t,
        up_t,
    )


def solution(mesh):
    split = P("batch", "seq", None)
    in_specs = (split, P("batch"), split) + (P(),) * 15
    out_specs = (split, split) + (P(),) * 15
    return jax.shard_map(body, mesh=mesh, in_specs=in_specs, out_specs=out_specs, check_vma=False)
```

time: 1280 us -> 359 us (0.28)
  local copies, waits for them, and re-layouts: 635 us -> 24 us
  matrix products: 196 us -> 0 us
  waiting for transfers between devices: 326 us -> 149 us
  Pallas kernels: 0 us -> 87.5 us
  other arithmetic: 34.9 us -> 15.6 us
  blocking collectives: 48.3 us -> 65.9 us
    while x59 -> x0, local copies, waits for them, and re-layouts: 261 us -> none
    reshape x21 -> x0, local copies, waits for them, and re-layouts: 210 us -> none  [the longest x4 73 us: skew_scores(): flattened.reshape(head_count, block_rows, extent_length - 1)]
    dot_general x47 -> x0, matrix products: 173 us -> none  [the longest x4 34.6 us: block_logits(): jnp.einsum('hnd,hed->hne', query_location[:, leading_index:key_total], po...]
    psum x2, waiting for transfers between devices: 263 us -> 149 us  [the longest x1 116 us: body(): lax.psum((pool_g, up_g, outer_g, inner_g, output_g), ('batch', 'seq'))]
    pallas_call x0 -> x4, Pallas kernels: none -> 87.5 us  [call(): pl.pallas_call(functools.partial(kernel, z), out_shape=[jax.ShapeDtypeStr...]
    slice x12 -> x3, local copies, waits for them, and re-layouts: 85.1 us -> 3.17 us  [the longest x1 1.98 us: body(): head_t[3]]
    all_gather x2 -> x1, waiting for transfers between devices: 61.7 us -> 0.01 us  [body(): head_t = lax.all_gather(lax.psum(head_g.astype(bf), 'batch'), 'seq', axis=0)]
    pad x4 -> x0, local copies, waits for them, and re-layouts: 29.2 us -> none  [the longest x2 16.1 us: unskew_scores(): flattened = jnp.pad(flattened, ((0, 0), (block_rows - 1, 1)))]
  transfers between devices with their start and end apart: 6 -> 3, of which waited for: 4 -> 2; matrix products, arithmetic and copies ran while one was open for 4% -> 4% of each run, Pallas kernels for 0% -> 3%
where the time goes in v1:
time: 359 us; the launch traced here: 358 us
  waiting for transfers between devices  149 us (42%)
  Pallas kernels  87.5 us (24%)
  blocking collectives  65.9 us (18%)
  local copies, waits for them, and re-layouts  24 us (7%)
  between operations  15.7 us (4%)
  other arithmetic  15.6 us (4%)
    psum x1, waiting for transfers between devices, body(): lax.psum((pool_g, up_g, outer_g, inner_g, output_g), ('batch', 'seq'))  116 us
    pallas_call x4, Pallas kernels, call(): pl.pallas_call(functools.partial(kernel, z), out_shape=[jax.ShapeDtypeStr...  87.5 us
    psum x1, blocking collectives, body(): norm_t = lax.psum(jnp.concatenate([norm1_g, norm2_g]), ('batch', 'seq'))  39.1 us
    psum x1, waiting for transfers between devices, body(): head_t = lax.all_gather(lax.psum(head_g.astype(bf), 'batch'), 'seq', axis=0)  33.6 us
    all_gather x1, blocking collectives, body(): bias_t = lax.all_gather(lax.psum(head_bias_g, 'batch'), 'seq', axis=0)  20.8 us
    unnamed x66, local copies, waits for them, and re-layouts  20.8 us
    convert_element_type x5, other arithmetic, body(): value.astype(f4)  12 us
  transfers between devices with their start and end apart: 3, of which 2 were waited for; matrix products, arithmetic and copies ran while one was open for 4% of the time, Pallas kernels for 3%

profile of v1, /device:TPU:0, one launch (start us, length us, event | category | flops | bytes accessed | tf_op | source)
XLA Modules:
  0.0 358.2 jit_solution(5266484524500949425)
XLA Ops:
  8.0 0.0 all-reduce.4.cloned.1.call-start
  8.1 0.7 and_select_fusion.counts_ref
  8.7 1.0 copy-done
  9.7 1.0 copy-done.2
  10.8 1.0 copy-done.4
  11.8 1.0 copy-done.6
  12.9 1.0 copy-done.12
  13.9 0.7 copy-done.18
  14.6 0.7 copy-done.20
  15.3 0.7 copy-done.21
  16.0 0.7 copy-done.22
  16.6 0.0 copy-start.24
  16.7 46.5 %shard_map.314 = (bf16[2,64,512]{2,1,0:T(8,128)(2,1)S(1)}, bf16[8,64,128]{2,1,0:T(8,128)(2,1)S(1)}, bf16[2,512,512]{2,1,0:T(8,128)(2,1)}, bf16[2,512,64]{2,1,0:T...) custom-call(s32[2]{0:T(128)S(1)} %and_select_fusion.counts_ref, ...), custom_call_target="tpu_custom_call" | custom-call | tf_op jit(solution)/shard_map/pallas_call | solution.py:534
  63.3 0.0 copy-start.8
  63.3 15.1 %shard_map.315 = (bf16[2,192,512]{2,1,0:T(8,128)(2,1)S(1)}, bf16[8,64,128]{2,1,0:T(8,128)(2,1)S(1)}, f32[128,512]{1,0:T(8,128)S(1)}, bf16[512,1536]{1,0:T(8,128)...) custom-call(s32[2]{0:T(128)S(1)} %copy-done.25, ...), custom_call_target="tpu_custom_call" | custom-call | tf_op jit(solution)/shard_map/pallas_call | solution.py:534
  78.4 0.0 copy-start.13
  78.4 0.8 copy-done.13
  79.2 0.7 copy-done.16
  80.0 15.2 %shard_map.316 = (bf16[8,64,384]{2,1,0:T(8,128)(2,1)S(1)}, f32[256,512]{1,0:T(8,128)S(1)}, f32[2,64]{1,0:T(2,128)S(1)}) custom-call(bf16[8,64,128]{2,1,0:T(8,128)(2,1)S(1)} %get-tuple-element.43.grad_recv_ref, bf16[2,512,512]{2,1,0:T(8,128)(2,1)S(1)} %copy-done.10, bf16[2,512,64]{2,1,0:T(8,128)(2,1)S(1)} %get-tuple-element.45.qc_ref, ...), custom_call_target="tpu_custom_call" | custom-call | tf_op jit(solution)/shard_map/pallas_call | solution.py:534
  95.2 0.7 copy-done.14
  95.9 0.7 convert_bitcast_fusion.1
  96.7 0.0 all-reduce.4.cloned.1.call-update
  96.7 0.0 all-gather.2.cloned.1.call-start
  96.7 33.6 %all-reduce.4.cloned.1.call-done = bf16[1,256,512]{2,1,0:T(8,128)(2,1)} async-done(((bf16[1,256,512]{2,1,0:T(8,128)(2,1)}), bf16[1,256,512]{2,1,0:T(8,128)(2,1)}) %all-reduce.4.cloned.1.call-update) | async-done | bytes 262160 | tf_op jit(solution)/shard_map/psum | solution.py:722
  130.4 0.0 all-gather.2.cloned.1.call-update
  130.4 0.0 all-reduce.6.cloned.1.call-start
  130.5 1.0 copy-done.15
  131.5 10.6 %shard_map.317 = (f32[2,192,512]{2,1,0:T(8,128)S(1)}, bf16[1536,512]{1,0:T(8,128)(2,1)}, f32[2,512]{1,0:T(2,128)S(1)}) custom-call(bf16[8,64,384]{2,1,0:T(8,128)(2,1)S(1)} %copy-done.15, f32[128,512]{1,0:T(8,128)S(1)} %get-tuple-element.52.hidden_grad_ref, bf16[2,64,512]{2,1,0:T(8,128)(2,1)S(1)} %get-tuple-element.41.pooled_ref, ...), custom_call_target="tpu_custom_call" | custom-call | tf_op jit(solution)/shard_map/pallas_call | solution.py:534
  142.1 0.0 all-reduce.6.cloned.1.call-update
  142.2 6.1 %psum.59 = f32[1,2,64]{2,1,0:T(2,128)S(1)} all-reduce(f32[1,2,64]{2,1,0:T(2,128)S(1)} %bitcast.26), channel_id=1, replica_groups=mesh['batch'=4,'seq'=8] {'batch'}, use_global_device_ids=true, to_apply=%region_3.4 | all-reduce | flops 128 | bytes 1024 | tf_op jit(solution)/shard_map/psum | solution.py:725
  148.2 20.8 %all_gather.15 = f32[8,2,64]{2,1,0:T(2,128)S(1)} all-gather(f32[1,2,64]{2,1,0:T(2,128)S(1)} %psum.59), channel_id=1, replica_groups=mesh['batch'=4,'seq'=8] {'seq'}, dimensions={0}, use_global_device_ids=true | all-gather | bytes 4608 | tf_op jit(solution)/shard_map/all_gather | solution.py:725
  169.1 39.1 %psum.57 = f32[4,512]{1,0:T(4,128)S(1)} all-reduce(f32[4,512]{1,0:T(4,128)S(1)} %pad_maximum_fusion), channel_id=1, replica_groups=mesh['batch'=4,'seq'=8] {'batch','seq'}, use_global_device_ids=true, to_apply=%region_1.2 | all-reduce | flops 2048 | bytes 16384 | tf_op jit(solution)/shard_map/psum | solution.py:721
  208.1 0.6 fusion.1
  208.7 0.6 fusion.2
  209.3 2.2 convert_bitcast_fusion
  211.5 2.0 fusion
  213.5 2.8 copy.49
  216.3 2.5 copy.50
  218.8 1.3 copy.51
  220.1 1.3 copy.52
  221.4 115.7 %all-reduce.6.cloned.1.call-done = (bf16[1536,512]{1,0:T(8,128)(2,1)}, bf16[512,512]{1,0:T(8,128)(2,1)}, bf16[512,2048]{1,0:T(8,128)(2,1)}, bf16[2048,512]{1,0:T(8,128)(2,1)}, bf16[512,1536]{1,0:T(8,128)(2,1)}) async-done(((bf16[1536,512]{1,0:T(8,128)(2,1)}, bf16[512,512]{1,0:T(8,128)(2,1)}, bf16[512,2048]{1,0:T(8,128)(2,1)}, bf16[2048,512]{1,0:T(8,128)(2,1)}, bf16[512,1536]{1,0:T(8,128)(2,1)}), ...) | async-done | bytes 7864336 | tf_op jit(solution)/shard_map/psum | solution.py:719
  337.1 3.7 %convert_element_type.25 = f32[1536,512]{1,0:T(8,128)} convert(bf16[1536,512]{1,0:T(8,128)(2,1)} %get-tuple-element.114) | non-fusion elementwise | flops 786432 | bytes 4718592 | tf_op jit(solution)/shard_map/convert_element_type | solution.py:720
  340.7 1.1 convert_element_type.28
  341.9 2.5 convert_element_type.29
  344.4 2.6 convert_element_type.30
  347.0 2.1 convert_element_type.31
  349.1 0.7 copy.61
  349.8 0.9 copy.62
  (46 shorter events, 0.1 us)
Async XLA Ops:
  8.0 122.4 %all-reduce.4.cloned.1.call-start = ((), (), s32[]{:S(2)}) async-start(), calls=%async_computation | async-start | bytes 524288 | tf_op jit(solution)/shard_map/psum | solution.py:722
  8.7 1.0 copy-start
  9.7 1.0 copy-start.2
  10.8 1.0 copy-start.4
  11.8 1.0 copy-start.6
  12.9 1.0 copy-start.12
  13.9 0.7 copy-start.18
  14.6 0.7 copy-start.20
  15.3 0.7 copy-start.21
  16.0 0.7 copy-start.22
  16.6 46.6 %copy-start.1 = (bf16[2,192,512]{2,1,0:T(8,128)(2,1)S(1)}, bf16[2,192,512]{2,1,0:T(8,128)(2,1)}, u32[]{:S(2)}) copy-start(bf16[2,192,512]{2,1,0:T(8,128)(2,1)} %x_ref.5) | copy-start | bytes 1179652
  16.6 46.6 %copy-start.9 = (bf16[2,192,512]{2,1,0:T(8,128)(2,1)S(1)}, bf16[2,192,512]{2,1,0:T(8,128)(2,1)}, u32[]{:S(2)}) copy-start(bf16[2,192,512]{2,1,0:T(8,128)(2,1)} %og_ref.3) | copy-start | bytes 1179652
  16.6 46.6 %copy-start.11 = (bf16[512,512]{1,0:T(8,128)(2,1)S(1)}, bf16[512,512]{1,0:T(8,128)(2,1)}, u32[]{:S(2)}) copy-start(bf16[512,512]{1,0:T(8,128)(2,1)} %output_w.1) | copy-start | bytes 1572868
  16.6 46.6 %copy-start.23 = (f32[512]{0:T(512)S(1)}, f32[512]{0:T(512)}, u32[]{:S(2)}) copy-start(f32[512]{0:T(512)} %param.32) | copy-start | bytes 6148
  16.6 46.6 %copy-start.24 = (f32[512]{0:T(512)S(1)}, f32[512]{0:T(512)}, u32[]{:S(2)}) copy-start(f32[512]{0:T(512)} %param.33) | copy-start | bytes 6148
  16.7 46.6 %copy-start.25 = (s32[2]{0:T(128)S(1)}, s32[2]{0:T(128)}, u32[]{:S(2)}) copy-start(s32[2]{0:T(128)} %lengths_ref.1) | copy-start | bytes 28
  63.3 16.6 %copy-start.8 = (bf16[512,512]{1,0:T(8,128)(2,1)S(1)}, bf16[512,512]{1,0:T(8,128)(2,1)}, u32[]{:S(2)}) copy-start(bf16[512,512]{1,0:T(8,128)(2,1)} %constant.14.clone.table_ref) | copy-start | bytes 1572868
  63.3 16.6 %copy-start.10 = (bf16[2,512,512]{2,1,0:T(8,128)(2,1)S(1)}, bf16[2,512,512]{2,1,0:T(8,128)(2,1)}, u32[]{:S(2)}) copy-start(bf16[2,512,512]{2,1,0:T(8,128)(2,1)} %get-tuple-element.44.attn_in_ref) | copy-start | bytes 3145732
  78.4 0.8 copy-start.13
  79.2 0.7 copy-start.16
  79.9 50.5 %copy-start.3 = (bf16[512,512]{1,0:T(8,128)(2,1)S(1)}, bf16[512,512]{1,0:T(8,128)(2,1)}, u32[]{:S(2)}) copy-start(bf16[512,512]{1,0:T(8,128)(2,1)} %query_w.3) | copy-start | bytes 1572868
  79.9 50.5 %copy-start.5 = (bf16[512,512]{1,0:T(8,128)(2,1)S(1)}, bf16[512,512]{1,0:T(8,128)(2,1)}, u32[]{:S(2)}) copy-start(bf16[512,512]{1,0:T(8,128)(2,1)} %key_w.3) | copy-start | bytes 1572868
  79.9 50.5 %copy-start.7 = (bf16[512,512]{1,0:T(8,128)(2,1)S(1)}, bf16[512,512]{1,0:T(8,128)(2,1)}, u32[]{:S(2)}) copy-start(bf16[512,512]{1,0:T(8,128)(2,1)} %value_w.3) | copy-start | bytes 1572868
  79.9 50.5 %copy-start.19 = (f32[512]{0:T(512)S(1)}, f32[512]{0:T(512)}, u32[]{:S(2)}) copy-start(f32[512]{0:T(512)} %param.23) | copy-start | bytes 6148
  95.2 0.7 copy-start.14
  96.7 112.6 %all-gather.2.cloned.1.call-start = ((), (), s32[]{:S(2)}) async-start(), calls=%async_computation.1 | async-start | bytes 2359296 | tf_op jit(solution)/shard_map/all_gather | solution.py:722
  130.4 206.7 %all-reduce.6.cloned.1.call-start = ((), (), s32[]{:S(2)}) async-start(), calls=%async_computation.2 | async-start | bytes 15728640 | tf_op jit(solution)/shard_map/psum | solution.py:719
  130.5 1.0 copy-start.15
  337.1 3.7 %copy-start.29 = (bf16[512,512]{1,0:T(8,128)(2,1)S(1)}, bf16[512,512]{1,0:T(8,128)(2,1)}, u32[]{:S(2)}) copy-start(bf16[512,512]{1,0:T(8,128)(2,1)} %get-tuple-element.115) | copy-start | bytes 1572868
  337.1 4.8 %copy-start.27 = (bf16[512,2048]{1,0:T(8,128)(2,1)S(1)}, bf16[512,2048]{1,0:T(8,128)(2,1)}, u32[]{:S(2)}) copy-start(bf16[512,2048]{1,0:T(8,128)(2,1)} %get-tuple-element.116) | copy-start | bytes 6291460
  341.9 2.5 copy-start.26
  344.4 2.6 copy-start.28
  347.0 2.1 copy-start.17
Sparse Core Ops, SparseCore 0:
  96.8 33.5 all-reduce.3
  132.7 70.4 all-gather.1
Sparse Core Ops, SparseCore 1:
  142.3 194.8 all-reduce.5

commit v2 on v1

--- a/solution.py
+++ b/solution.py
@@ -11,6 +11,8 @@
 MESH = pl.DeviceIdType.MESH
 epsilon = 1e-05
 masked_value = -1e30
+CHAIN_ROWS = [1024, 1536, 512, 512, 512, 1536, 512, 512, 512, 512, 512, 512, 512]
+CHAIN_ORDER = [2, 1, 0, 8, 4, 0, 1, 3, 1, 0, 4, 9, 5]
 BLOCK = 128
 LANES = 128
 VMEM = pl.BlockSpec(memory_space=pltpu.VMEM)
@@ -146,7 +148,6 @@
     table_ref,
     pooled_ref,
     recv_ref,
-    attn_in_ref,
     qc_ref,
     qp_ref,
     k_ref,
@@ -156,11 +157,12 @@
     xf_ref,
     tail_ref,
     halo_ref,
-    gather_ref,
+    qkv_out_ref,
+    qkv_ref,
     out_ref,
     halo_sems,
-    gather_send,
-    gather_recv,
+    qkv_send,
+    qkv_recv,
     out_send,
     out_recv,
     own_sem,
@@ -191,35 +193,42 @@
         pooled += dot(
             low(every_third(z, xf_ref, 6 + part)), pool_w[part * width : (part + 1) * width, :]
         )
-    pooled_ref[...] = low(pooled).reshape(z.items, r, width)
-
-    def items_of(peer):
-        return pooled_ref.at[pl.ds(lax.div(peer, z.heads) * z.units, z.units)]
-
-    copies = send_all(n, me, items_of, gather_ref, gather_send, gather_recv)
-    gather_ref[me] = pooled_ref[pl.ds(group * z.units, z.units)]
+    short = low(pooled)
+    pooled_ref[...] = short.reshape(z.items, r, width)
+    normed, _ = norm_rows(short.astype(jnp.float32))
+    attn_in = low(normed * gain_ref[...] + bias_ref[...])
+    qkv = [low(dot(attn_in, w[...])) for w in (query_w, key_w, value_w)]
+    pad = [jnp.zeros((r, hd), jnp.bfloat16)] * (LANES // hd - z.units)
+    for target in range(n):
+        sides = []
+        lanes = slice(target % z.heads * hd, (target % z.heads + 1) * hd)
+        for value in qkv:
+            for unit in range(z.units):
+                item = target // z.heads * z.units + unit
+                sides.append(value[item * r : (item + 1) * r, lanes])
+            sides += pad
+        qkv_out_ref[target] = jnp.concatenate(sides, axis=1)
+    copies = send_all(n, me, lambda peer: qkv_out_ref.at[peer], qkv_ref, qkv_send, qkv_recv)
+    qkv_ref[me] = qkv_out_ref[me]
     lane_pair = pl.multiple_of(lax.div(head * hd, LANES) * LANES, LANES)
-    pair = pl.ds(lane_pair, LANES)
     turn = lax.rem(head * hd, LANES)
-
-    def own_half(value):
-        return pltpu.roll(value, LANES - turn, 1)[:, :hd]
-
-    pos_ref[...] = low(own_half(dot(table_ref[...], position_w[:, pair])))
+    both = dot(table_ref[...], position_w[:, pl.ds(lane_pair, LANES)])
+    pos_ref[...] = low(pltpu.roll(both, LANES - turn, 1)[:, :hd])
+    content_bias = cb_ref[pl.ds(head, 1), :]
+    position_bias = pb_ref[pl.ds(head, 1), :]
     for copy in copies:
         copy.wait()
-    weights = jnp.concatenate([query_w[:, pair], key_w[:, pair], value_w[:, pair]], axis=1)
-    content_bias = cb_ref[pl.ds(head, 1), :]
-    position_bias = pb_ref[pl.ds(head, 1), :]
     for unit in range(z.units):
-        normed, _ = norm_rows(gather_ref[:, unit].reshape(z.length, width).astype(jnp.float32))
-        attn_in_ref[unit] = low(normed * gain_ref[...] + bias_ref[...])
-        qkv = dot(attn_in_ref[unit], weights)
-        queries = own_half(qkv[:, :LANES])
-        qc_ref[unit] = low(queries + content_bias)
-        qp_ref[unit] = low(queries + position_bias)
-        k_ref[unit] = low(own_half(qkv[:, LANES : 2 * LANES]))
-        v_ref[unit] = low(own_half(qkv[:, 2 * LANES :]))
+        queries, keys, values = (
+            qkv_ref[:, :, which * LANES + unit * hd : which * LANES + (unit + 1) * hd].reshape(
+                z.length, hd
+            )
+            for which in range(3)
+        )
+        qc_ref[unit] = low(queries.astype(jnp.float32) + content_bias)
+        qp_ref[unit] = low(queries.astype(jnp.float32) + position_bias)
+        k_ref[unit] = keys
+        v_ref[unit] = values
     for block in range(z.length // BLOCK):
         lo, hi = block * BLOCK, (block + 1) * BLOCK
         sides = []
@@ -270,10 +279,7 @@
     block_ref,
     recv_ref,
     hidden_grad_ref,
-    up_grad_ref,
-    outer_grad_ref,
-    inner_grad_ref,
-    output_grad_ref,
+    early_ref,
     norm_grad_ref,
     xf_ref,
     att_ref,
@@ -356,12 +362,14 @@
             block_ref[item, :, slab * LANES : (slab + 1) * LANES] = low(xf_ref[item, slab, 8:, :])
     for part in range(3):
         cut = slice(part * width, (part + 1) * width)
-        up_grad_ref[:, cut] = low(dot_tn(summed, up_rows_ref[:, cut]))
-    for lo in range(0, ff, step):
-        cut = slice(lo, lo + step)
-        outer_grad_ref[cut, :] = low(dot_tn(act_ref[:, cut], summed_grad))
-        inner_grad_ref[:, cut] = low(dot_tn(ffn_in, inner_low_ref[:, cut]))
-    output_grad_ref[...] = low(dot_tn(att_ref[...], branch))
+        early_ref[cut, :] = low(dot_tn(summed, up_rows_ref[:, cut]))
+    for lo in range(0, ff, width):
+        cut = slice(lo, lo + width)
+        at = 3 * width + lo
+        early_ref[at : at + width, :] = low(dot_tn(act_ref[:, cut], summed_grad))
+        at += ff
+        early_ref[at : at + width, :] = low(dot_tn(ffn_in, inner_low_ref[:, cut]))
+    early_ref[3 * width + 2 * ff :, :] = low(dot_tn(att_ref[...], branch))
     for copy in copies:
         copy.wait()
     own.wait()
@@ -376,7 +384,6 @@
 def backward_kernel(
     z,
     grad_recv_ref,
-    attn_in_ref,
     qc_ref,
     qp_ref,
     k_ref,
@@ -438,13 +445,10 @@
     copies = send_all(n, me, lambda peer: out_ref.at[peer], recv_ref, out_send, out_recv)
     own = pltpu.make_async_copy(out_ref.at[me], recv_ref.at[me], own_sem)
     own.start()
-    query_sum = key_sum = value_sum = table_sum = 0.0
+    table_sum = 0.0
     for unit in range(z.units):
-        query_sum += dot_tn(query_grad_ref[unit], attn_in_ref[unit])
-        key_sum += dot(low(key_t_ref[unit]), attn_in_ref[unit])
-        value_sum += dot(low(value_t_ref[unit]), attn_in_ref[unit])
         table_sum += dot(low(table_t_ref[unit]), table_ref[...])
-    head_grad_ref[...] = jnp.concatenate([query_sum, key_sum, value_sum, table_sum], axis=0)
+    head_grad_ref[...] = low(table_sum)
     for copy in copies:
         copy.wait()
     own.wait()
@@ -458,12 +462,13 @@
     x_ref,
     og_ref,
     gain_ref,
+    bias_ref,
     query_w,
     key_w,
     value_w,
     pool_w,
     input_grad_ref,
-    pool_grad_ref,
+    late_ref,
     norm_grad_ref,
     xf_ref,
     of_ref,
@@ -507,9 +512,13 @@
         device_id_type=MESH,
     )
     halo.start()
+    attn_in = low(normed * gain_ref[...] + bias_ref[...])
+    for which in range(3):
+        at = (3 + which) * width
+        late_ref[at : at + width, :] = low(dot_tn(attn_in, dq_ref[which]))
     rows_by_three(z, x_ref, xf_ref)
     rows_by_three(z, og_ref, of_ref)
-    pool_grad_ref[2 * width :, :] = low(dot_tn(low(every_third(z, xf_ref, 8)), short_grad))
+    late_ref[2 * width : 3 * width, :] = low(dot_tn(low(every_third(z, xf_ref, 8)), short_grad))
     own = dot_nt(short_grad, pool_w[2 * width :, :])
     set_every_third(z, of_ref, 8, every_third(z, of_ref, 8) + own)
     halo.wait()
@@ -522,12 +531,333 @@
     for part in range(2):
         cut = slice(part * width, (part + 1) * width)
         first = 9 + part
-        pool_grad_ref[cut, :] = low(dot_tn(low(every_third(z, xf_ref, first)), later))
+        late_ref[cut, :] = low(dot_tn(low(every_third(z, xf_ref, first)), later))
         back = dot_nt(later, pool_w[cut, :])
         set_every_third(z, of_ref, first, every_third(z, of_ref, first) + back)
     for item in range(z.items):
         for slab in range(width // LANES):
             input_grad_ref[item, :, slab * LANES : (slab + 1) * LANES] = of_ref[item, slab, 8:, :]
+
+
+class Copies:
+    def __init__(self, batch_size, seq_size):
+        self.core = [("batch", 1)]
+        self.chips = [("batch", 1 << k) for k in range(1, batch_size.bit_length() - 1)]
+        self.line = [("seq", 1 << k) for k in range(seq_size.bit_length() - 1)]
+        self.bits = self.core + self.chips + self.line
+
+    def cost(self, bit, size):
+        axis, mask = bit
+        if bit in self.core:
+            return {"core": size / 428e3}
+        near = 2 * size / 92e3
+        if bit in self.line[:1] or axis == "batch":
+            return {bit: near}
+        return {"line": near, bit: near * (mask // 2)}
+
+    def orders(self):
+        if len(self.bits) != 5:
+            links = self.chips + self.line
+            return [self.core + links[k:] + links[:k] for k in range(len(links))] * 4
+        c, x, y, z0, z1 = self.bits
+        names = (
+            "xyz0z1",
+            "yxz0z1",
+            "yz0xz1",
+            "z0xyz1",
+            "z1xz0y",
+            "yxz1z0",
+            "xyz1z0",
+            "yz0z1x",
+            "xz0yz1",
+            "z0z1xy",
+        )
+        found = []
+        for name in names:
+            order = [c]
+            while name:
+                for key, bit in (("x", x), ("y", y), ("z0", z0), ("z1", z1)):
+                    if name.startswith(key):
+                        order.append(bit)
+                        name = name[len(key) :]
+            found.append(order)
+        return found
+
+    def halving(self, rows, order, base):
+        down, up = [], []
+        for bit in order:
+            if rows % 32 == 0:
+                rows //= 2
+                down.append(("sum", bit, rows, rows))
+                up.append(("spread", bit, rows, rows))
+            else:
+                down.append(("sum", bit, 0, rows))
+        return {"base": base, "fixed": [], "steps": down + up[::-1], "rows": rows}
+
+    def by_head(self, heads, hd, base):
+        head_bits = self.line[: heads.bit_length() - 1]
+        batch_bits = self.core + self.chips
+        rest = self.line[len(head_bits) :]
+        rows, parts = hd, []
+        for bit in batch_bits + rest:
+            if rows % 32 == 0:
+                rows //= 2
+                parts.append((bit, rows))
+            else:
+                parts.append((bit, 0))
+        split = [bit for bit, size in parts if size]
+        inner = split[1:]
+        stride, strides = rows, {}
+        for bit in inner[::-1] + head_bits + split[:1]:
+            strides[bit] = stride
+            stride *= 2
+        down = [("sum", bit, strides.get(bit, 0), size or rows) for bit, size in parts]
+        up = [("spread", bit, strides[bit], strides[bit]) for bit in strides]
+        fixed = [(bit, strides[bit]) for bit in head_bits]
+        return {"base": base, "fixed": fixed, "steps": down + up, "rows": rows, "strides": strides}
+
+    def schedule(self, chains, width):
+        chains = [(chain, start) for chain, start in chains]
+        left = []
+        for chain, _ in chains:
+            total = [0.0]
+            for _, bit, _, rows in chain["steps"][::-1]:
+                busy = max(self.cost(bit, 2 * rows * width).values())
+                total.append(total[-1] + busy + 2.0)
+            left.append(total[::-1])
+        free, ready = {}, [start for _, start in chains]
+        at = [0] * len(chains)
+        plan = []
+        while True:
+            best = None
+            for c, (chain, _) in enumerate(chains):
+                if at[c] < len(chain["steps"]):
+                    _, bit, _, rows = chain["steps"][at[c]]
+                    cost = self.cost(bit, 2 * rows * width)
+                    start = max([ready[c]] + [free.get(link, 0.0) for link in cost])
+                    key = (round(start, 1), -left[c][at[c]], c)
+                    if best is None or key < best[0]:
+                        best = (key, c, cost, start)
+            if best is None:
+                return plan
+            _, c, cost, start = best
+            for link, busy in cost.items():
+                free[link] = start + busy
+            step = chains[c][0]["steps"][at[c]]
+            lag = 0.7 if step[1] in self.core else 2.0
+            lag += 1e-6 * 2 * step[3] * width if step[0] == "sum" else 0.0
+            ready[c] = start + max(cost.values()) + lag
+            plan.append((start, c, at[c]))
+            at[c] += 1
+
+
+class Sums:
+    def __init__(self, chains, work, landing, total, send_sems, recv_sems):
+        self.chains = chains
+        self.work, self.landing, self.total = work, landing, total
+        self.send_sems, self.recv_sems = send_sems, recv_sems
+        self.index = {"batch": lax.axis_index("batch"), "seq": lax.axis_index("seq")}
+        self.open = {}
+        self.offset = {}
+        sem = land = 0
+        self.sem, self.land = {}, {}
+        for c, chain in enumerate(chains):
+            self.offset[c] = chain["base"] + sum(
+                self.bit(bit) * stride for bit, stride in chain["fixed"]
+            )
+            for k, (phase, _, _, rows) in enumerate(chain["steps"]):
+                self.sem[c, k] = sem
+                sem += 1
+                if phase == "sum":
+                    self.land[c, k] = land
+                    land += rows
+
+    @staticmethod
+    def needs(chains):
+        steps = [step for chain in chains for step in chain["steps"]]
+        return len(steps), sum(step[3] for step in steps if step[0] == "sum")
+
+    def bit(self, bit):
+        axis, mask = bit
+        return lax.rem(lax.div(self.index[axis], mask), 2)
+
+    def partner(self, bit):
+        axis, mask = bit
+        return {axis: self.index[axis] + mask - 2 * mask * self.bit(bit)}
+
+    def start(self, c, k):
+        if k:
+            self.finish(c, k - 1)
+        phase, bit, stride, rows = self.chains[c]["steps"][k]
+        side = self.bit(bit)
+        offset = self.offset[c]
+        if phase == "sum":
+            other = offset + (1 - side) * stride if stride else offset
+            source = self.work.at[pl.ds(pl.multiple_of(other, 16), rows)]
+            target = self.landing.at[pl.ds(self.land[c, k], rows)]
+            if stride:
+                self.offset[c] = offset + side * stride
+        else:
+            here = pl.ds(pl.multiple_of(offset, 16), rows)
+            source, target = self.total.at[here], self.total.at[here]
+            self.offset[c] = offset - side * stride
+        copy = pltpu.make_async_remote_copy(
+            src_ref=source,
+            dst_ref=target,
+            send_sem=self.send_sems.at[self.sem[c, k]],
+            recv_sem=self.recv_sems.at[self.sem[c, k]],
+            device_id=self.partner(bit),
+            device_id_type=MESH,
+        )
+        copy.start()
+        self.open[c] = copy
+
+    def finish(self, c, k):
+        self.open.pop(c).wait()
+        steps = self.chains[c]["steps"]
+        phase, _, _, rows = steps[k]
+        if phase == "sum":
+            last = k + 1 == len(steps) or steps[k + 1][0] == "spread"
+            held = pl.ds(pl.multiple_of(self.offset[c], 16), rows)
+            landed = self.landing[self.land[c, k] : self.land[c, k] + rows, :]
+            both = self.work[held, :].astype(jnp.float32) + landed.astype(jnp.float32)
+            (self.total if last else self.work)[held, :] = low(both)
+
+
+def sum_kernel(
+    z,
+    plan,
+    chains,
+    bits,
+    terms_ref,
+    small_ref,
+    total_ref,
+    small_total_ref,
+    work,
+    landing,
+    total,
+    small_work,
+    small_landing,
+    send_sems,
+    recv_sems,
+    small_send,
+    small_recv,
+    load_sems,
+    store_sems,
+):
+    sums = Sums(chains, work, landing, total, send_sems, recv_sems)
+    loads = []
+    for c, chain in enumerate(chains):
+        at, size = chain["base"], chain["all"]
+        loads.append(
+            pltpu.make_async_copy(
+                terms_ref.at[at : at + size], work.at[at : at + size], load_sems.at[c]
+            )
+        )
+        loads[-1].start()
+    barrier = pltpu.get_barrier_semaphore()
+    for bit in bits:
+        pl.semaphore_signal(barrier, inc=1, device_id=sums.partner(bit), device_id_type=MESH)
+    pl.semaphore_wait(barrier, len(bits))
+    small_work[0] = small_ref[...]
+    small = []
+
+    def small_start(k):
+        copy = pltpu.make_async_remote_copy(
+            src_ref=small_work.at[k],
+            dst_ref=small_landing.at[k],
+            send_sem=small_send.at[k],
+            recv_sem=small_recv.at[k],
+            device_id=sums.partner(bits[k]),
+            device_id_type=MESH,
+        )
+        copy.start()
+        small.append(copy)
+
+    def small_finish(k):
+        small[k].wait()
+        small_work[k + 1] = small_work[k] + small_landing[k]
+
+    stores = []
+    small_start(0)
+    small_at = [plan[len(plan) * (k + 1) // (len(bits) + 1)][1:] for k in range(len(bits))]
+    for _, c, k in plan:
+        if k == 0:
+            loads[c].wait()
+        sums.start(c, k)
+        if (c, k) in small_at:
+            done = small_at.index((c, k))
+            small_finish(done)
+            if done + 1 < len(bits):
+                small_start(done + 1)
+    small_total_ref[...] = small_work[len(bits)]
+    ends = {}
+    for order, (_, c, k) in enumerate(plan):
+        ends[c] = order
+    for c in sorted(ends, key=ends.get):
+        sums.finish(c, len(chains[c]["steps"]) - 1)
+        at, size = chains[c]["base"], chains[c]["all"]
+        stores.append(
+            pltpu.make_async_copy(
+                total.at[at : at + size], total_ref.at[at : at + size], store_sems.at[c]
+            )
+        )
+        stores[-1].start()
+    for store in stores:
+        store.wait()
+
+
+def sum_all(z, nb, terms, head_term, small, early_rows):
+    width = z.width
+    copies = Copies(nb, z.n)
+    orders = copies.orders()
+    chains, base = [], 0
+    sizes = CHAIN_ROWS if sum(CHAIN_ROWS) == terms.shape[0] else [512] * (terms.shape[0] // 512)
+    for c, rows in enumerate(sizes):
+        chains.append(copies.halving(rows, orders[CHAIN_ORDER[c % len(CHAIN_ORDER)] % len(orders)], base))
+        chains[-1]["all"] = rows
+        base += rows
+    total_rows = base + z.heads * z.hd
+    chains.append(copies.by_head(z.heads, z.hd, base))
+    chains[-1]["all"] = z.heads * z.hd
+    half = z.hd // 2
+    head = lax.rem(lax.axis_index("seq"), z.heads)
+    placed = jnp.zeros((2, z.heads, half, width), jnp.bfloat16)
+    placed = lax.dynamic_update_slice(
+        placed, head_term.reshape(2, 1, half, width), (0, head, 0, 0)
+    )
+    terms = jnp.concatenate([terms, placed.reshape(z.heads * z.hd, width)], axis=0)
+    plan = copies.schedule([(chain, 0.0) for chain in chains], width)
+    count, landing = Sums.needs(chains)
+    bits = copies.bits
+    bf, f4, dma = jnp.bfloat16, jnp.float32, pltpu.SemaphoreType.DMA
+    total, small_total = pl.pallas_call(
+        functools.partial(sum_kernel, z, plan, chains, bits),
+        out_shape=[
+            jax.ShapeDtypeStruct((total_rows, width), bf),
+            jax.ShapeDtypeStruct(small.shape, f4),
+        ],
+        in_specs=[ANY, VMEM],
+        out_specs=[ANY, VMEM],
+        scratch_shapes=[
+            pltpu.VMEM((total_rows, width), bf),
+            pltpu.VMEM((landing, width), bf),
+            pltpu.VMEM((total_rows, width), bf),
+            pltpu.VMEM((len(bits) + 1,) + small.shape, f4),
+            pltpu.VMEM((len(bits),) + small.shape, f4),
+            dma((count,)),
+            dma((count,)),
+            dma((len(bits),)),
+            dma((len(bits),)),
+            dma((len(chains),)),
+            dma((len(chains),)),
+        ],
+        compiler_params=pltpu.CompilerParams(
+            collective_id=4, has_side_effects=True, vmem_limit_bytes=58 * 2**20
+        ),
+    )(terms, small)
+    heads_total = total[base:].reshape(2, z.heads, half, width).transpose(1, 0, 2, 3)
+    return total, heads_total.reshape(z.heads * z.hd, width).T, small_total
 
 
 def call(kernel, z, collective_id, ins, outs, scratch, args):
@@ -577,7 +907,7 @@
     gain1, bias1 = norm1_gain.reshape(1, width), norm1_bias.reshape(1, width)
     gain2, bias2 = norm2_gain.reshape(1, width), norm2_bias.reshape(1, width)
     xf = pltpu.VMEM((items, slabs, 3 * r + 8, LANES), f4)
-    (pooled, att_recv, attn_in, qc, qp, keys, values, positions, probs) = call(
+    (pooled, att_recv, qc, qp, keys, values, positions, probs) = call(
         forward_kernel,
         z,
         0,
@@ -585,7 +915,6 @@
         [
             ((items, r, width), bf, VMEM),
             ((n, r, LANES), bf, ANY),
-            ((units, length, width), bf, VMEM),
             ((units, length, hd), bf, VMEM),
             ((units, length, hd), bf, VMEM),
             ((units, length, hd), bf, VMEM),
@@ -597,7 +926,8 @@
             xf,
             pltpu.VMEM((items, 16, width), bf),
             pltpu.VMEM((items, 16, width), bf),
-            pltpu.VMEM((n, units, r, width), bf),
+            pltpu.VMEM((n, r, 3 * LANES), bf),
+            pltpu.VMEM((n, r, 3 * LANES), bf),
             pltpu.VMEM((n, r, LANES), bf),
             dma((2,)),
             dma((n,)),
@@ -621,7 +951,8 @@
             table,
         ),
     )
-    (block_out, grad_recv, hidden_grad, up_g, outer_g, inner_g, output_g, norm2_g) = call(
+    early_rows = 3 * width + 2 * ff + width
+    block_out, grad_recv, hidden_grad, early, norm2_g = call(
         middle_kernel,
         z,
         1,
@@ -630,10 +961,7 @@
             ((items, full_rows, width), bf, VMEM),
             ((n, r, LANES), bf, ANY),
             ((rows, width), f4, VMEM),
-            ((width, 3 * width), bf, VMEM),
-            ((ff, width), bf, VMEM),
-            ((width, ff), bf, VMEM),
-            ((width, width), bf, VMEM),
+            ((early_rows, width), bf, VMEM),
             ((2, width), f4, VMEM),
         ],
         [
@@ -666,10 +994,10 @@
         backward_kernel,
         z,
         2,
-        [VMEM] * 9,
+        [VMEM] * 8,
         [
             ((n, r, 3 * LANES), bf, ANY),
-            ((4 * hd, width), f4, VMEM),
+            ((hd, width), bf, VMEM),
             ((2, hd), f4, VMEM),
         ],
         [
@@ -682,16 +1010,16 @@
             dma((n,)),
             dma,
         ],
-        (grad_recv, attn_in, qc, qp, keys, values, positions, probs, table),
-    )
-    input_grad, pool_g, norm1_g = call(
+        (grad_recv, qc, qp, keys, values, positions, probs, table),
+    )
+    input_grad, late, norm1_g = call(
         last_kernel,
         z,
         3,
-        [VMEM] * 10,
+        [VMEM] * 11,
         [
             ((items, full_rows, width), f4, VMEM),
-            ((3 * width, width), bf, VMEM),
+            ((6 * width, width), bf, VMEM),
             ((2, width), f4, VMEM),
         ],
         [
@@ -710,35 +1038,58 @@
             byte_rows,
             out_grad,
             gain1,
+            bias1,
             query_weight,
             key_weight,
             value_weight,
             pool_weight,
         ),
     )
-    dense = lax.psum((pool_g, up_g, outer_g, inner_g, output_g), ("batch", "seq"))
-    pool_t, up_t, outer_t, inner_t, output_t = (value.astype(f4) for value in dense)
-    norm_t = lax.psum(jnp.concatenate([norm1_g, norm2_g]), ("batch", "seq"))
-    head_t = lax.all_gather(lax.psum(head_g.astype(bf), "batch"), "seq", axis=0)
-    head_t = jnp.sum(head_t.reshape(n // heads, heads, 4, hd, width).astype(f4), axis=0)
-    head_t = head_t.transpose(1, 3, 0, 2).reshape(4, width, width)
-    bias_t = lax.all_gather(lax.psum(head_bias_g, "batch"), "seq", axis=0)
-    bias_t = jnp.sum(bias_t.reshape(n // heads, heads, 2, hd), axis=0)
+    own_head = lax.rem(lax.axis_index("seq"), heads)
+    mine = (lax.broadcasted_iota(jnp.int32, (1, heads, 1), 1) == own_head).astype(f4)
+    small = jnp.concatenate(
+        [norm1_g, norm2_g, (head_bias_g[:, None, :] * mine).reshape(2, width)], axis=0
+    )
+    small = jnp.concatenate([small, jnp.zeros((2, width), f4)], axis=0)
+    total, position_t, small_t = sum_all(
+        z,
+        lax.axis_size("batch"),
+        jnp.concatenate([early, late], axis=0),
+        head_g,
+        small,
+        early_rows,
+    )
+
+    def rows_at(first, count):
+        return total[first * width : (first + count) * width].astype(f4)
+
+    def side_by_side(first, count):
+        stacked = rows_at(first, count).reshape(count, width, width)
+        return stacked.transpose(1, 0, 2).reshape(width, count * width)
+
+    wide = ff // width
+    up_t = side_by_side(0, 3)
+    outer_t = rows_at(3, wide)
+    inner_t = side_by_side(3 + wide, wide)
+    output_t = rows_at(3 + 2 * wide, 1)
+    pool_t = rows_at(4 + 2 * wide, 3)
+    query_t, key_t, value_t = (rows_at(7 + 2 * wide + which, 1) for which in range(3))
+    bias_t = small_t[4:6].reshape(2, heads, hd)
     return (
         block_out,
         input_grad,
         pool_t,
-        norm_t[0],
-        norm_t[1],
-        head_t[0],
-        head_t[1],
-        head_t[2],
-        head_t[3],
-        bias_t[:, 0],
-        bias_t[:, 1],
+        small_t[0],
+        small_t[1],
+        query_t,
+        key_t,
+        value_t,
+        position_t.astype(f4),
+        bias_t[0],
+        bias_t[1],
         output_t,
-        norm_t[2],
-        norm_t[3],
+        small_t[2],
+        small_t[3],
         inner_t,
         outer_t,
         up_t,

time: 359 us -> 229 us (0.64)
  waiting for transfers between devices: 149 us -> 0 us
  Pallas kernels: 87.5 us -> 165 us
  blocking collectives: 65.9 us -> 0 us
  other arithmetic: 15.6 us -> 35.6 us
  between operations: 15.7 us -> 0.98 us
    psum x2 -> x0, waiting for transfers between devices: 149 us -> none  [the longest x1 116 us: body(): lax.psum((pool_g, up_g, outer_g, inner_g, output_g), ('batch', 'seq'))]
    pallas_call x0 -> x1, Pallas kernels: none -> 90.7 us  [sum_all(): pl.pallas_call(functools.partial(sum_kernel, z, plan, chains, bits), out_...]
    psum x2 -> x0, blocking collectives: 45.1 us -> none  [the longest x1 39.1 us: body(): norm_t = lax.psum(jnp.concatenate([norm1_g, norm2_g]), ('batch', 'seq'))]
    concatenate x1 -> x2, other arithmetic: 0.01 us -> 20.9 us  [the longest x1 20.2 us: sum_all(): jnp.concatenate([terms, placed.reshape(z.heads * z.hd, width)], axis=0)]
    all_gather x1 -> x0, blocking collectives: 20.8 us -> none  [body(): bias_t = lax.all_gather(lax.psum(head_bias_g, 'batch'), 'seq', axis=0)]
    pallas_call x4, Pallas kernels: 87.5 us -> 74.6 us  [call(): pl.pallas_call(functools.partial(kernel, z), out_shape=[jax.ShapeDtypeStr...]
    reshape x0 -> x2, local copies, waits for them, and re-layouts: none -> 5.73 us  [side_by_side(): return stacked.transpose(1, 0, 2).reshape(width, count * width)]
    slice x0 -> x1, other arithmetic: none -> 4.58 us  [rows_at(): return total[first * width:(first + count) * width].astype(f4)]
  transfers between devices with their start and end apart: 3 -> 0, of which waited for: 2 -> 0; matrix products, arithmetic and copies ran while one was open for 4% -> 0% of each run, Pallas kernels for 3% -> 0%
where the time goes in v2:
time: 229 us; the launch traced here: 228 us
  Pallas kernels  165 us (72%)
  other arithmetic  35.6 us (16%)
  local copies, waits for them, and re-layouts  26.1 us (11%)
    pallas_call x1, Pallas kernels, sum_all(): pl.pallas_call(functools.partial(sum_kernel, z, plan, chains, bits), out_...  90.7 us
    pallas_call x4, Pallas kernels, call(): pl.pallas_call(functools.partial(kernel, z), out_shape=[jax.ShapeDtypeStr...  74.6 us
    concatenate x1, other arithmetic, sum_all(): jnp.concatenate([terms, placed.reshape(z.heads * z.hd, width)], axis=0)  20.2 us
    unnamed x60, local copies, waits for them, and re-layouts  17 us
    convert_element_type x2, other arithmetic, rows_at(): return total[first * width:(first + count) * width].astype(f4)  8.89 us
    reshape x2, local copies, waits for them, and re-layouts, side_by_side(): return stacked.transpose(1, 0, 2).reshape(width, count * width)  5.73 us
    slice x1, other arithmetic, rows_at(): return total[first * width:(first + count) * width].astype(f4)  4.58 us

profile of v2, /device:TPU:0, one launch (start us, length us, event | category | flops | bytes accessed | tf_op | source)
XLA Modules:
  0.0 227.9 jit_solution(812168128495111182)
XLA Ops:
  0.7 0.7 and_select_fusion.counts_ref
  1.4 0.1 pad.3.clone
  1.4 0.1 mul.22
  1.5 0.1 mul.23
  1.6 1.0 copy-done
  2.6 1.0 copy-done.3
  3.6 1.0 copy-done.5
  4.7 1.0 copy-done.7
  5.7 1.0 copy-done.12
  6.7 0.7 copy-done.17
  7.4 0.7 copy-done.19
  8.1 0.7 copy-done.21
  8.8 0.7 copy-done.22
  9.5 0.0 copy-start.24
  9.5 0.0 copy-start.25
  9.5 31.0 %shard_map.314 = (bf16[2,64,512]{2,1,0:T(8,128)(2,1)S(1)}, bf16[8,64,128]{2,1,0:T(8,128)(2,1)S(1)}, bf16[2,512,64]{2,1,0:T(8,128)(2,1)S(1)}, bf16[2,512,64]{2,1,...) custom-call(s32[2]{0:T(128)S(1)} %and_select_fusion.counts_ref, ...), custom_call_target="tpu_custom_call" | custom-call | tf_op jit(solution)/shard_map/pallas_call | solution.py:864
  40.5 0.0 copy-start.2
  40.6 0.0 copy-start.4
  40.6 0.0 copy-start.6
  40.6 0.0 copy-start.8
  40.6 0.0 copy-start.18
  40.7 0.0 copy-start.20
  40.7 14.8 %shard_map.315 = (bf16[2,192,512]{2,1,0:T(8,128)(2,1)S(1)}, bf16[8,64,128]{2,1,0:T(8,128)(2,1)S(1)}, f32[128,512]{1,0:T(8,128)S(1)}, bf16[6144,512]{1,0:T(8,128)(2,1)}, f32[2,512]{1,0:T(2,128)S(1)}) custom-call(s32[2]{0:T(128)S(1)} %copy-done.25, bf16[8,64,128]{2,1,0:T(8,128)(2,1)S(1)} %get-tuple-element.38.att_recv_ref, ...), custom_call_target="tpu_custom_call" | custom-call | tf_op jit(solution)/shard_map/pallas_call | solution.py:864
  55.4 0.0 copy-start.13
  55.5 16.4 %shard_map.316 = (bf16[8,64,384]{2,1,0:T(8,128)(2,1)S(1)}, bf16[64,512]{1,0:T(8,128)(2,1)S(1)}, f32[2,64]{1,0:T(2,128)S(1)}) custom-call(bf16[8,64,128]{2,1,0:T(8,128)(2,1)S(1)} %get-tuple-element.41.grad_recv_ref, bf16[2,512,64]{2,1,0:T(8,128)(2,1)S(1)} %get-tuple-element.42.qc_ref, bf16[2,512,64]{2,1,0:T(8,128)(2,1)S(1)} %get-tuple-element.43.qp_ref, ...), custom_call_target="tpu_custom_call" | custom-call | tf_op jit(solution)/shard_map/pallas_call | solution.py:864
  71.9 0.0 copy-start.15
  71.9 0.7 copy-done.15
  72.7 0.8 copy-done.26
  73.5 0.1 mul.21
  73.6 1.0 copy-done.16
  74.6 12.4 %shard_map.317 = (f32[2,192,512]{2,1,0:T(8,128)S(1)}, bf16[3072,512]{1,0:T(8,128)(2,1)}, f32[2,512]{1,0:T(2,128)S(1)}) custom-call(bf16[8,64,384]{2,1,0:T(8,128)(2,1)S(1)} %copy-done.16, f32[128,512]{1,0:T(8,128)S(1)} %get-tuple-element.49.hidden_grad_ref, bf16[2,64,512]{2,1,0:T(8,128)(2,1)S(1)} %get-tuple-element.39.pooled_ref, ...), custom_call_target="tpu_custom_call" | custom-call | tf_op jit(solution)/shard_map/pallas_call | solution.py:864
  87.0 0.7 maximum_maximum_fusion.small_ref
  87.7 20.2 %pad_maximum_fusion.terms_ref = bf16[9728,512]{1,0:T(8,128)(2,1)} fusion(bf16[512,512]{1,0:T(8,128)(2,1)S(1)} %bitcast.43, bf16[3072,512]{1,0:T(8,128)(2,1)} %get-tuple-element.52, bf16[6144,512]{1,0:T(8,128)(2,1)} %get-tuple-element.51), kind=kLoop, calls=%fused_computation | loop fusion | flops 29884416 | bytes 19922944 | tf_op jit(solution)/shard_map/concatenate | solution.py:829
  107.9 90.7 %shard_map.318 = (bf16[9728,512]{1,0:T(8,128)(2,1)}, f32[8,512]{1,0:T(8,128)}) custom-call(bf16[9728,512]{1,0:T(8,128)(2,1)} %pad_maximum_fusion.terms_ref, f32[8,512]{1,0:T(8,128)} %maximum_maximum_fusion.small_ref), custom_call_target="tpu_custom_call" | custom-call | tf_op jit(solution)/shard_map/pallas_call | solution.py:834
  198.6 1.5 fusion.1
  200.2 0.7 squeeze.20
  200.8 0.7 squeeze.21
  201.5 3.9 %slice_convert_fusion.2 = (f32[512,512]{1,0:T(8,128)}, bf16[512,512]{1,0:T(8,128)(2,1)S(1)}, f32[512,512]{1,0:T(8,128)}, f32[512,512]{1,0:T(8,128)}, f32[512,512]{1,0:T(8,128)}) fusion(bf16[9728,512]{1,0:T(8,128)(2,1)} %get-tuple-element.57), kind=kLoop, calls=%fused_computation.4 | loop fusion | flops 1048576 | bytes 7340032 | tf_op jit(solution)/shard_map/convert_element_type | solution.py:1064
  205.4 0.1 copy.41
  205.6 1.3 copy.44
  206.9 4.6 %fusion = (bf16[1536,512]{1,0:T(8,128)(2,1)}, f32[1536,512]{1,0:T(8,128)}) fusion(bf16[9728,512]{1,0:T(8,128)(2,1)} %get-tuple-element.57), kind=kLoop, calls=%fused_computation.15 | loop fusion | flops 786432 | bytes 7864320 | tf_op jit(solution)/shard_map/slice | solution.py:1064
  211.5 5.0 %slice_convert_fusion = (f32[2048,512]{1,0:T(8,128)}, bf16[2048,512]{1,0:T(8,128)(2,1)S(1)}) fusion(bf16[9728,512]{1,0:T(8,128)(2,1)} %get-tuple-element.57), kind=kLoop, calls=%fused_computation.2 | loop fusion | flops 1048576 | bytes 10485760 | tf_op jit(solution)/shard_map/convert_element_type | solution.py:1064
  216.4 3.1 %copy.43 = f32[3,512,512]{1,2,0:T(8,128)} copy(bf16[3,512,512]{2,1,0:T(8,128)(2,1)} %bitcast.39) | data formatting | bytes 4718592 | tf_op jit(solution)/shard_map/reshape | solution.py:1068
  219.5 3.5 %copy.45 = f32[512,1536]{1,0:T(8,128)} copy(f32[512,1536]{0,1:T(8,128)} %bitcast.37) | data formatting | bytes 6291456
  223.0 0.6 convert_bitcast_fusion
  223.6 2.7 %copy.46 = f32[4,64,8,512]{3,2,0,1:T(8,128)} copy(f32[4,64,8,512]{3,2,1,0:T(8,128)S(1)} %convert_bitcast_fusion) | data formatting | bytes 8388608 | tf_op jit(solution)/shard_map/reshape | solution.py:1068
  226.3 0.7 copy.50
  227.0 0.9 copy.51
  (40 shorter events, 0.1 us)
Async XLA Ops:
  0.7 39.9 %copy-start.23 = (f32[512]{0:T(512)S(1)}, f32[512]{0:T(512)}, u32[]{:S(2)}) copy-start(f32[512]{0:T(512)} %param.32) | copy-start | bytes 6148
  1.6 1.0 copy-start
  2.6 1.0 copy-start.3
  3.6 1.0 copy-start.5
  4.7 1.0 copy-start.7
  5.7 1.0 copy-start.12
  6.7 0.7 copy-start.17
  7.4 0.7 copy-start.19
  8.1 0.7 copy-start.21
  8.8 0.7 copy-start.22
  9.5 31.1 %copy-start.1 = (bf16[2,192,512]{2,1,0:T(8,128)(2,1)S(1)}, bf16[2,192,512]{2,1,0:T(8,128)(2,1)}, u32[]{:S(2)}) copy-start(bf16[2,192,512]{2,1,0:T(8,128)(2,1)} %x_ref.5) | copy-start | bytes 1179652
  9.5 31.1 %copy-start.9 = (bf16[512,1536]{1,0:T(8,128)(2,1)S(1)}, bf16[512,1536]{1,0:T(8,128)(2,1)}, u32[]{:S(2)}) copy-start(bf16[512,1536]{1,0:T(8,128)(2,1)} %up_w.1) | copy-start | bytes 4718596
  9.5 31.1 %copy-start.10 = (bf16[2,192,512]{2,1,0:T(8,128)(2,1)S(1)}, bf16[2,192,512]{2,1,0:T(8,128)(2,1)}, u32[]{:S(2)}) copy-start(bf16[2,192,512]{2,1,0:T(8,128)(2,1)} %og_ref.3) | copy-start | bytes 1179652
  9.5 31.1 %copy-start.11 = (bf16[512,512]{1,0:T(8,128)(2,1)S(1)}, bf16[512,512]{1,0:T(8,128)(2,1)}, u32[]{:S(2)}) copy-start(bf16[512,512]{1,0:T(8,128)(2,1)} %output_w.1) | copy-start | bytes 1572868
  9.5 31.1 %copy-start.24 = (f32[512]{0:T(512)S(1)}, f32[512]{0:T(512)}, u32[]{:S(2)}) copy-start(f32[512]{0:T(512)} %param.33) | copy-start | bytes 6148
  9.5 31.1 %copy-start.25 = (s32[2]{0:T(128)S(1)}, s32[2]{0:T(128)}, u32[]{:S(2)}) copy-start(s32[2]{0:T(128)} %lengths_ref.1) | copy-start | bytes 28
  40.5 14.9 %copy-start.2 = (bf16[512,512]{1,0:T(8,128)(2,1)S(1)}, bf16[512,512]{1,0:T(8,128)(2,1)}, u32[]{:S(2)}) copy-start(bf16[512,512]{1,0:T(8,128)(2,1)} %constant.27.clone.table_ref) | copy-start | bytes 1572868
  40.6 33.0 %copy-start.4 = (bf16[512,512]{1,0:T(8,128)(2,1)S(1)}, bf16[512,512]{1,0:T(8,128)(2,1)}, u32[]{:S(2)}) copy-start(bf16[512,512]{1,0:T(8,128)(2,1)} %query_w.3) | copy-start | bytes 1572868
  40.6 33.0 %copy-start.6 = (bf16[512,512]{1,0:T(8,128)(2,1)S(1)}, bf16[512,512]{1,0:T(8,128)(2,1)}, u32[]{:S(2)}) copy-start(bf16[512,512]{1,0:T(8,128)(2,1)} %key_w.3) | copy-start | bytes 1572868
  40.6 33.0 %copy-start.8 = (bf16[512,512]{1,0:T(8,128)(2,1)S(1)}, bf16[512,512]{1,0:T(8,128)(2,1)}, u32[]{:S(2)}) copy-start(bf16[512,512]{1,0:T(8,128)(2,1)} %value_w.3) | copy-start | bytes 1572868
  40.6 33.0 %copy-start.18 = (f32[512]{0:T(512)S(1)}, f32[512]{0:T(512)}, u32[]{:S(2)}) copy-start(f32[512]{0:T(512)} %param.23) | copy-start | bytes 6148
  40.7 33.0 %copy-start.20 = (f32[512]{0:T(512)S(1)}, f32[512]{0:T(512)}, u32[]{:S(2)}) copy-start(f32[512]{0:T(512)} %param.24) | copy-start | bytes 6148
  55.4 16.4 %copy-start.13 = (bf16[2,192,512]{2,1,0:T(8,128)(2,1)}, bf16[2,192,512]{2,1,0:T(8,128)(2,1)S(1)}, u32[]{:S(2)}) copy-start(bf16[2,192,512]{2,1,0:T(8,128)(2,1)S(1)} %get-tuple-element.110) | copy-start | bytes 1179652
  71.9 0.7 copy-start.15
  72.7 0.8 copy-start.26
  73.6 1.0 copy-start.16
  74.6 13.1 %copy-start.27 = (bf16[2,8,32,512]{3,2,1,0:T(8,128)(2,1)S(1)}, bf16[2,8,32,512]{3,2,1,0:T(8,128)(2,1)}, u32[]{:S(2)}) copy-start(bf16[2,8,32,512]{3,2,1,0:T(8,128)(2,1)} %copy-done.26) | copy-start | bytes 1572868
  223.6 2.7 %copy-start.14 = (bf16[2,192,512]{2,1,0:T(8,128)(2,1)S(1)}, bf16[2,192,512]{2,1,0:T(8,128)(2,1)}, u32[]{:S(2)}) copy-start(bf16[2,192,512]{2,1,0:T(8,128)(2,1)} %copy-done.13) | copy-start | bytes 1179652

commit v3 on v2

--- a/solution.py
+++ b/solution.py
@@ -729,7 +729,9 @@
     plan,
     chains,
     bits,
-    terms_ref,
+    early_ref,
+    late_ref,
+    head_ref,
     small_ref,
     total_ref,
     small_total_ref,
@@ -749,12 +751,28 @@
     loads = []
     for c, chain in enumerate(chains):
         at, size = chain["base"], chain["all"]
+        early_rows = early_ref.shape[0]
+        if "strides" in chain:
+            half = z.hd // 2
+            head = lax.rem(lax.axis_index("seq"), z.heads)
+            parts = []
+            for side in range(2):
+                to = pl.multiple_of(at + side * z.heads * half + head * half, 16)
+                parts.append((head_ref.at[side * half : (side + 1) * half], to, half))
+        elif at < early_rows:
+            parts = [(early_ref.at[at : at + size], at, size)]
+        else:
+            parts = [(late_ref.at[at - early_rows : at - early_rows + size], at, size)]
         loads.append(
-            pltpu.make_async_copy(
-                terms_ref.at[at : at + size], work.at[at : at + size], load_sems.at[c]
-            )
-        )
-        loads[-1].start()
+            [
+                pltpu.make_async_copy(
+                    source, work.at[pl.ds(to, count)], load_sems.at[c, which]
+                )
+                for which, (source, to, count) in enumerate(parts)
+            ]
+        )
+        for load in loads[-1]:
+            load.start()
     barrier = pltpu.get_barrier_semaphore()
     for bit in bits:
         pl.semaphore_signal(barrier, inc=1, device_id=sums.partner(bit), device_id_type=MESH)
@@ -783,7 +801,8 @@
     small_at = [plan[len(plan) * (k + 1) // (len(bits) + 1)][1:] for k in range(len(bits))]
     for _, c, k in plan:
         if k == 0:
-            loads[c].wait()
+            for load in loads[c]:
+                load.wait()
         sums.start(c, k)
         if (c, k) in small_at:
             done = small_at.index((c, k))
@@ -807,12 +826,13 @@
         store.wait()
 
 
-def sum_all(z, nb, terms, head_term, small, early_rows):
+def sum_all(z, nb, early, late, head_term, small):
     width = z.width
     copies = Copies(nb, z.n)
     orders = copies.orders()
     chains, base = [], 0
-    sizes = CHAIN_ROWS if sum(CHAIN_ROWS) == terms.shape[0] else [512] * (terms.shape[0] // 512)
+    term_rows = early.shape[0] + late.shape[0]
+    sizes = CHAIN_ROWS if sum(CHAIN_ROWS) == term_rows else [512] * (term_rows // 512)
     for c, rows in enumerate(sizes):
         chains.append(copies.halving(rows, orders[CHAIN_ORDER[c % len(CHAIN_ORDER)] % len(orders)], base))
         chains[-1]["all"] = rows
@@ -820,13 +840,6 @@
     total_rows = base + z.heads * z.hd
     chains.append(copies.by_head(z.heads, z.hd, base))
     chains[-1]["all"] = z.heads * z.hd
-    half = z.hd // 2
-    head = lax.rem(lax.axis_index("seq"), z.heads)
-    placed = jnp.zeros((2, z.heads, half, width), jnp.bfloat16)
-    placed = lax.dynamic_update_slice(
-        placed, head_term.reshape(2, 1, half, width), (0, head, 0, 0)
-    )
-    terms = jnp.concatenate([terms, placed.reshape(z.heads * z.hd, width)], axis=0)
     plan = copies.schedule([(chain, 0.0) for chain in chains], width)
     count, landing = Sums.needs(chains)
     bits = copies.bits
@@ -837,7 +850,7 @@
             jax.ShapeDtypeStruct((total_rows, width), bf),
             jax.ShapeDtypeStruct(small.shape, f4),
         ],
-        in_specs=[ANY, VMEM],
+        in_specs=[ANY, ANY, ANY, VMEM],
         out_specs=[ANY, VMEM],
         scratch_shapes=[
             pltpu.VMEM((total_rows, width), bf),
@@ -849,15 +862,91 @@
             dma((count,)),
             dma((len(bits),)),
             dma((len(bits),)),
-            dma((len(chains),)),
+            dma((len(chains), 2)),
             dma((len(chains),)),
         ],
         compiler_params=pltpu.CompilerParams(
             collective_id=4, has_side_effects=True, vmem_limit_bytes=58 * 2**20
         ),
-    )(terms, small)
-    heads_total = total[base:].reshape(2, z.heads, half, width).transpose(1, 0, 2, 3)
-    return total, heads_total.reshape(z.heads * z.hd, width).T, small_total
+    )(early, late, head_term, small)
+    return total, small_total
+
+
+def result_kernel(
+    z,
+    ff,
+    total_ref,
+    small_ref,
+    block_in_ref,
+    input_in_ref,
+    block_ref,
+    input_ref,
+    pool_ref,
+    gain1_ref,
+    bias1_ref,
+    query_ref,
+    key_ref,
+    value_ref,
+    position_ref,
+    content_bias_ref,
+    position_bias_ref,
+    output_ref,
+    gain2_ref,
+    bias2_ref,
+    inner_ref,
+    outer_ref,
+    up_ref,
+    held,
+    wide,
+    load_sems,
+    store_sems,
+    pass_sems,
+):
+    width = z.width
+    through = [
+        pltpu.make_async_copy(block_in_ref, block_ref, pass_sems.at[0]),
+        pltpu.make_async_copy(input_in_ref, input_ref, pass_sems.at[1]),
+    ]
+    blocks = held.shape[0]
+    loads = [
+        pltpu.make_async_copy(
+            total_ref.at[k * width : (k + 1) * width], held.at[k], load_sems.at[k]
+        )
+        for k in range(blocks)
+    ]
+    for copy in loads + through:
+        copy.start()
+    places = [up_ref.at[:, k * width : (k + 1) * width] for k in range(3)]
+    places += [outer_ref.at[k * width : (k + 1) * width] for k in range(ff // width)]
+    places += [inner_ref.at[:, k * width : (k + 1) * width] for k in range(ff // width)]
+    places += [output_ref]
+    places += [pool_ref.at[k * width : (k + 1) * width] for k in range(3)]
+    places += [query_ref, key_ref, value_ref, position_ref]
+    gain1_ref[...] = small_ref[0:1, :]
+    bias1_ref[...] = small_ref[1:2, :]
+    gain2_ref[...] = small_ref[2:3, :]
+    bias2_ref[...] = small_ref[3:4, :]
+    for head in range(z.heads):
+        lanes = slice(head * z.hd, (head + 1) * z.hd)
+        content_bias_ref[head : head + 1, :] = small_ref[4:5, lanes]
+        position_bias_ref[head : head + 1, :] = small_ref[5:6, lanes]
+    stores = []
+    for k in range(blocks):
+        loads[k].wait()
+        if k + 1 < blocks:
+            wide[k] = held[k].astype(jnp.float32)
+        else:
+            half = z.hd // 2
+            for head in range(z.heads):
+                rows = [
+                    held[k, side * z.heads * half + head * half :][:half] for side in range(2)
+                ]
+                both = jnp.concatenate(rows, axis=0).astype(jnp.float32)
+                wide[k, :, head * z.hd : (head + 1) * z.hd] = both.T
+        stores.append(pltpu.make_async_copy(wide.at[k], places[k], store_sems.at[k]))
+        stores[-1].start()
+    for copy in stores + through:
+        copy.wait()
 
 
 def call(kernel, z, collective_id, ins, outs, scratch, args):
@@ -1051,48 +1140,43 @@
         [norm1_g, norm2_g, (head_bias_g[:, None, :] * mine).reshape(2, width)], axis=0
     )
     small = jnp.concatenate([small, jnp.zeros((2, width), f4)], axis=0)
-    total, position_t, small_t = sum_all(
-        z,
-        lax.axis_size("batch"),
-        jnp.concatenate([early, late], axis=0),
-        head_g,
-        small,
-        early_rows,
-    )
-
-    def rows_at(first, count):
-        return total[first * width : (first + count) * width].astype(f4)
-
-    def side_by_side(first, count):
-        stacked = rows_at(first, count).reshape(count, width, width)
-        return stacked.transpose(1, 0, 2).reshape(width, count * width)
-
-    wide = ff // width
-    up_t = side_by_side(0, 3)
-    outer_t = rows_at(3, wide)
-    inner_t = side_by_side(3 + wide, wide)
-    output_t = rows_at(3 + 2 * wide, 1)
-    pool_t = rows_at(4 + 2 * wide, 3)
-    query_t, key_t, value_t = (rows_at(7 + 2 * wide + which, 1) for which in range(3))
-    bias_t = small_t[4:6].reshape(2, heads, hd)
-    return (
-        block_out,
-        input_grad,
-        pool_t,
-        small_t[0],
-        small_t[1],
-        query_t,
-        key_t,
-        value_t,
-        position_t.astype(f4),
-        bias_t[0],
-        bias_t[1],
-        output_t,
-        small_t[2],
-        small_t[3],
-        inner_t,
-        outer_t,
-        up_t,
+    total, small_t = sum_all(z, lax.axis_size("batch"), early, late, head_g, small)
+    blocks = total.shape[0] // width
+    shapes = [
+        ((items, full_rows, width), bf, ANY),
+        ((items, full_rows, width), f4, ANY),
+        ((3 * width, width), f4, ANY),
+        ((1, width), f4, VMEM),
+        ((1, width), f4, VMEM),
+        ((width, width), f4, ANY),
+        ((width, width), f4, ANY),
+        ((width, width), f4, ANY),
+        ((width, width), f4, ANY),
+        ((heads, hd), f4, VMEM),
+        ((heads, hd), f4, VMEM),
+        ((width, width), f4, ANY),
+        ((1, width), f4, VMEM),
+        ((1, width), f4, VMEM),
+        ((width, ff), f4, ANY),
+        ((ff, width), f4, ANY),
+        ((width, 3 * width), f4, ANY),
+    ]
+    results = pl.pallas_call(
+        functools.partial(result_kernel, z, ff),
+        out_shape=[jax.ShapeDtypeStruct(shape, dtype) for shape, dtype, _ in shapes],
+        in_specs=[ANY, VMEM, ANY, ANY],
+        out_specs=[space for _, _, space in shapes],
+        scratch_shapes=[
+            pltpu.VMEM((blocks, width, width), bf),
+            pltpu.VMEM((blocks, width, width), f4),
+            dma((blocks,)),
+            dma((blocks,)),
+            dma((2,)),
+        ],
+        compiler_params=pltpu.CompilerParams(vmem_limit_bytes=50 * 2**20),
+    )(total, small_t, block_out, input_grad)
+    return tuple(
+        value.reshape(width) if value.shape == (1, width) else value for value in results
     )
 
 

time: 229 us -> 193 us (0.84)
  other arithmetic: 35.6 us -> 2.72 us
  local copies, waits for them, and re-layouts: 26.1 us -> 12 us
  Pallas kernels: 165 us -> 177 us
    concatenate x1 -> x0, other arithmetic: 20.2 us -> none  [sum_all(): jnp.concatenate([terms, placed.reshape(z.heads * z.hd, width)], axis=0)]
    pallas_call x0 -> x1, Pallas kernels: none -> 11.3 us  [body(): pl.pallas_call(functools.partial(result_kernel, z, ff), out_shape=[jax.Sh...]
    convert_element_type x2 -> x0, other arithmetic: 8.89 us -> none  [rows_at(): return total[first * width:(first + count) * width].astype(f4)]
    unnamed x60 -> x48, local copies, waits for them, and re-layouts: 17 us -> 9.3 us
    reshape x2 -> x0, local copies, waits for them, and re-layouts: 5.73 us -> none  [side_by_side(): return stacked.transpose(1, 0, 2).reshape(width, count * width)]
    slice x1 -> x0, other arithmetic: 4.58 us -> none  [rows_at(): return total[first * width:(first + count) * width].astype(f4)]
where the time goes in v3:
time: 193 us
  Pallas kernels  177 us (92%)
  local copies, waits for them, and re-layouts  12 us (6%)
  other arithmetic  2.72 us (1%)
    pallas_call x1, Pallas kernels, sum_all(): pl.pallas_call(functools.partial(sum_kernel, z, plan, chains, bits), out_...  91.1 us
    pallas_call x4, Pallas kernels, call(): pl.pallas_call(functools.partial(kernel, z), out_shape=[jax.ShapeDtypeStr...  74.4 us
    pallas_call x1, Pallas kernels, body(): pl.pallas_call(functools.partial(result_kernel, z, ff), out_shape=[jax.Sh...  11.3 us
    unnamed x48, local copies, waits for them, and re-layouts  9.3 us

profile of v3, /device:TPU:0, one launch (start us, length us, event | category | flops | bytes accessed | tf_op | source)
XLA Modules:
  0.0 192.6 jit_solution(7828094171600780536)
XLA Ops:
  0.7 0.0 copy-start.23
  0.7 0.0 copy-start.22
  0.7 0.0 copy-start.21
  0.7 0.7 and_select_fusion.counts_ref
  1.4 0.6 pad.3.clone
  2.0 0.1 mul.22
  2.1 0.7 mul.23
  2.7 1.0 copy-done
  3.7 1.0 copy-done.3
  4.8 1.0 copy-done.5
  5.8 1.0 copy-done.7
  6.8 1.0 copy-done.12
  7.9 0.7 copy-done.15
  8.6 0.7 copy-done.17
  9.2 0.7 copy-done.19
  9.9 0.7 copy-done.20
  10.6 31.0 %shard_map.314 = (bf16[2,64,512]{2,1,0:T(8,128)(2,1)S(1)}, bf16[8,64,128]{2,1,0:T(8,128)(2,1)S(1)}, bf16[2,512,64]{2,1,0:T(8,128)(2,1)S(1)}, bf16[2,512,64]{2,1,...) custom-call(s32[2]{0:T(128)S(1)} %and_select_fusion.counts_ref, ...), custom_call_target="tpu_custom_call" | custom-call | tf_op jit(solution)/shard_map/pallas_call | solution.py:953
  41.6 0.0 copy-done.23
  41.6 0.0 copy-done.22
  41.7 0.0 copy-done.21
  41.7 0.0 copy-done.1
  41.7 0.0 copy-done.9
  41.7 0.0 copy-done.10
  41.7 0.0 copy-done.11
  41.7 0.0 copy-start.2
  41.7 14.7 %shard_map.315 = (bf16[2,192,512]{2,1,0:T(8,128)(2,1)S(1)}, bf16[8,64,128]{2,1,0:T(8,128)(2,1)S(1)}, f32[128,512]{1,0:T(8,128)S(1)}, bf16[6144,512]{1,0:T(8,128)(2,1)}, f32[2,512]{1,0:T(2,128)S(1)}) custom-call(s32[2]{0:T(128)S(1)} %copy-done.23, bf16[8,64,128]{2,1,0:T(8,128)(2,1)S(1)} %get-tuple-element.55.att_recv_ref, ...), custom_call_target="tpu_custom_call" | custom-call | tf_op jit(solution)/shard_map/pallas_call | solution.py:953
  56.4 0.0 copy-start.4
  56.5 0.0 copy-start.6
  56.5 0.0 copy-start.8
  56.5 0.0 copy-start.16
  56.5 0.0 copy-start.18
  56.5 0.0 copy-done.2
  56.5 16.4 %shard_map.316 = (bf16[8,64,384]{2,1,0:T(8,128)(2,1)S(1)}, bf16[64,512]{1,0:T(8,128)(2,1)S(1)}, f32[2,64]{1,0:T(2,128)S(1)}) custom-call(bf16[8,64,128]{2,1,0:T(8,128)(2,1)S(1)} %get-tuple-element.58.grad_recv_ref, bf16[2,512,64]{2,1,0:T(8,128)(2,1)S(1)} %get-tuple-element.59.qc_ref, bf16[2,512,64]{2,1,0:T(8,128)(2,1)S(1)} %get-tuple-element.60.qp_ref, ...), custom_call_target="tpu_custom_call" | custom-call | tf_op jit(solution)/shard_map/pallas_call | solution.py:953
  72.9 0.0 copy-start.13
  72.9 0.6 copy-done.13
  73.5 0.6 mul.20
  74.1 0.8 mul.21
  74.9 0.7 broadcast_multiply_fusion
  75.6 0.0 copy-done.4
  75.6 0.0 copy-done.6
  75.6 0.0 copy-done.8
  75.6 0.0 copy-done.16
  75.6 0.0 copy-done.18
  75.6 12.3 %shard_map.317 = (f32[2,192,512]{2,1,0:T(8,128)S(1)}, bf16[3072,512]{1,0:T(8,128)(2,1)}, f32[2,512]{1,0:T(2,128)S(1)}) custom-call(bf16[8,64,384]{2,1,0:T(8,128)(2,1)S(1)} %get-tuple-element.65.recv_ref, f32[128,512]{1,0:T(8,128)S(1)} %get-tuple-element.66.hidden_grad_ref, bf16[2,64,512]{2,1,0:T(8,128)(2,1)S(1)} %get-tuple-element.56.pooled_ref, ...), custom_call_target="tpu_custom_call" | custom-call | tf_op jit(solution)/shard_map/pallas_call | solution.py:953
  88.0 1.3 maximum_maximum_fusion.small_ref
  89.3 91.1 %shard_map.318 = (bf16[9728,512]{1,0:T(8,128)(2,1)}, f32[8,512]{1,0:T(8,128)}) custom-call(bf16[6144,512]{1,0:T(8,128)(2,1)} %get-tuple-element.57.early_ref, bf16[3072,512]{1,0:T(8,128)(2,1)} %get-tuple-element.67.late_ref, bf16[64,512]{1,0:T(8,128)(2,1)} %copy-done.13, f32[8,512]{1,0:T(8,128)} %maximum_maximum_fusion.small_ref), custom_call_target="tpu_custom_call" | custom-call | tf_op jit(solution)/shard_map/pallas_call | solution.py:847
  180.4 0.7 copy-done.14
  181.1 11.3 %shard_map.319 = (bf16[2,192,512]{2,1,0:T(8,128)(2,1)}, f32[2,192,512]{2,1,0:T(8,128)}, f32[1536,512]{1,0:T(8,128)}, f32[1,512]{1,0:T(1,128)}, f32[1,512]{1,0:T(...) custom-call(bf16[9728,512]{1,0:T(8,128)(2,1)} %get-tuple-element.72., ...), custom_call_target="tpu_custom_call" | custom-call | tf_op jit(solution)/shard_map/pallas_call | solution.py:1164
  (16 shorter events, 0.0 us)
Async XLA Ops:
  0.7 41.0 %copy-start.23 = (s32[2]{0:T(128)S(1)}, s32[2]{0:T(128)}, u32[]{:S(2)}) copy-start(s32[2]{0:T(128)} %lengths_ref.1) | copy-start | bytes 28
  0.7 41.0 %copy-start.22 = (f32[512]{0:T(512)S(1)}, f32[512]{0:T(512)}, u32[]{:S(2)}) copy-start(f32[512]{0:T(512)} %param.33) | copy-start | bytes 6148
  0.7 41.0 %copy-start.21 = (f32[512]{0:T(512)S(1)}, f32[512]{0:T(512)}, u32[]{:S(2)}) copy-start(f32[512]{0:T(512)} %param.32) | copy-start | bytes 6148
  2.7 1.0 copy-start
  3.7 1.0 copy-start.3
  4.8 1.0 copy-start.5
  5.8 1.0 copy-start.7
  6.8 1.0 copy-start.12
  7.9 0.7 copy-start.15
  8.6 0.7 copy-start.17
  9.2 0.7 copy-start.19
  9.9 0.7 copy-start.20
  10.6 31.1 %copy-start.1 = (bf16[2,192,512]{2,1,0:T(8,128)(2,1)S(1)}, bf16[2,192,512]{2,1,0:T(8,128)(2,1)}, u32[]{:S(2)}) copy-start(bf16[2,192,512]{2,1,0:T(8,128)(2,1)} %x_ref.5) | copy-start | bytes 1179652
  10.6 31.1 %copy-start.9 = (bf16[512,1536]{1,0:T(8,128)(2,1)S(1)}, bf16[512,1536]{1,0:T(8,128)(2,1)}, u32[]{:S(2)}) copy-start(bf16[512,1536]{1,0:T(8,128)(2,1)} %up_w.1) | copy-start | bytes 4718596
  10.6 31.1 %copy-start.10 = (bf16[2,192,512]{2,1,0:T(8,128)(2,1)S(1)}, bf16[2,192,512]{2,1,0:T(8,128)(2,1)}, u32[]{:S(2)}) copy-start(bf16[2,192,512]{2,1,0:T(8,128)(2,1)} %og_ref.3) | copy-start | bytes 1179652
  10.6 31.1 %copy-start.11 = (bf16[512,512]{1,0:T(8,128)(2,1)S(1)}, bf16[512,512]{1,0:T(8,128)(2,1)}, u32[]{:S(2)}) copy-start(bf16[512,512]{1,0:T(8,128)(2,1)} %output_w.1) | copy-start | bytes 1572868
  41.7 14.8 %copy-start.2 = (bf16[512,512]{1,0:T(8,128)(2,1)S(1)}, bf16[512,512]{1,0:T(8,128)(2,1)}, u32[]{:S(2)}) copy-start(bf16[512,512]{1,0:T(8,128)(2,1)} %constant.23.clone.table_ref) | copy-start | bytes 1572868
  56.4 19.1 %copy-start.4 = (bf16[512,512]{1,0:T(8,128)(2,1)S(1)}, bf16[512,512]{1,0:T(8,128)(2,1)}, u32[]{:S(2)}) copy-start(bf16[512,512]{1,0:T(8,128)(2,1)} %query_w.3) | copy-start | bytes 1572868
  56.5 19.1 %copy-start.6 = (bf16[512,512]{1,0:T(8,128)(2,1)S(1)}, bf16[512,512]{1,0:T(8,128)(2,1)}, u32[]{:S(2)}) copy-start(bf16[512,512]{1,0:T(8,128)(2,1)} %key_w.3) | copy-start | bytes 1572868
  56.5 19.1 %copy-start.8 = (bf16[512,512]{1,0:T(8,128)(2,1)S(1)}, bf16[512,512]{1,0:T(8,128)(2,1)}, u32[]{:S(2)}) copy-start(bf16[512,512]{1,0:T(8,128)(2,1)} %value_w.3) | copy-start | bytes 1572868
  56.5 19.1 %copy-start.16 = (f32[512]{0:T(512)S(1)}, f32[512]{0:T(512)}, u32[]{:S(2)}) copy-start(f32[512]{0:T(512)} %param.23) | copy-start | bytes 6148
  56.5 19.1 %copy-start.18 = (f32[512]{0:T(512)S(1)}, f32[512]{0:T(512)}, u32[]{:S(2)}) copy-start(f32[512]{0:T(512)} %param.24) | copy-start | bytes 6148
  72.9 0.6 copy-start.13
  180.4 0.7 copy-start.14

commit v4 on v3

v4 whole, which is shorter than its diff:
```python
import functools

import jax
import jax.numpy as jnp
import numpy as np
from jax import lax
from jax.experimental import pallas as pl
from jax.experimental.pallas import tpu as pltpu
from jax.sharding import PartitionSpec as P

MESH = pl.DeviceIdType.MESH
epsilon = 1e-05
masked_value = -1e30
CHAINS = [(2, 0), (2, 1), (1, 2), (1, 3), (2, 0), (1, 1), (1, 8), (1, 4), (1, 5), (1, 0), (1, 1), (1, 3), (1, 9), (1, 2), (1, 4)]
EARLY_DONE = 9.0
BACK_DONE = 21.0
LATE = (31.0, 34.0)
BLOCK = 128
LANES = 128
VMEM = pl.BlockSpec(memory_space=pltpu.VMEM)
SMEM = pl.BlockSpec(memory_space=pltpu.SMEM)
ANY = pl.BlockSpec(memory_space=pl.ANY)


def dot(left, right):
    return jnp.dot(left, right, preferred_element_type=jnp.float32)


def dot_nt(left, right):
    return lax.dot_general(
        left, right, (((1,), (1,)), ((), ())), preferred_element_type=jnp.float32
    )


def dot_tn(left, right):
    return lax.dot_general(
        left, right, (((0,), (0,)), ((), ())), preferred_element_type=jnp.float32
    )


def low(value):
    return value.astype(jnp.bfloat16)


def distance_table(short_len, width):
    distance = (short_len - 1 - np.arange(short_len)).astype(np.float32)
    steps_in = np.arange(0, width, 2).astype(np.float32)
    frequency = np.exp(-np.log(np.float32(10000.0)) * steps_in / np.float32(width))
    angles = distance[:, None] * frequency[None, :].astype(np.float32)
    both = np.concatenate([np.sin(angles), np.cos(angles)], axis=1)
    return jnp.asarray(both.astype(jnp.bfloat16))


def norm_rows(rows):
    mean = jnp.mean(rows, axis=-1, keepdims=True)
    centered = rows - mean
    inverse = lax.rsqrt(jnp.mean(centered * centered, axis=-1, keepdims=True) + epsilon)
    return centered * inverse, inverse


def norm_backward(gradient, normed, inverse, gain):
    scaled = gradient * gain
    return inverse * (
        scaled
        - jnp.mean(scaled, axis=-1, keepdims=True)
        - normed * jnp.mean(scaled * normed, axis=-1, keepdims=True)
    )


class Sizes:
    def __init__(self, n, items, full_rows, width, heads):
        self.n = n
        self.items = items
        self.r = full_rows // 3
        self.width = width
        self.heads = heads
        self.hd = width // heads
        self.units = items * heads // n
        self.length = n * self.r
        self.rows = items * self.r
        assert n % heads == 0 and self.units * self.hd <= LANES


def send_all(n, me, source, target, send_sem, recv_sem):
    copies = []
    for step in range(1, n):
        peer = lax.rem(me + step, n)
        copies.append(
            pltpu.make_async_remote_copy(
                src_ref=source(peer),
                dst_ref=target.at[me],
                send_sem=send_sem.at[step],
                recv_sem=recv_sem.at[step],
                device_id={"seq": peer},
                device_id_type=MESH,
            )
        )
        copies[-1].start()
    return copies


def rows_by_three(z, x_ref, xf_ref):
    for item in range(z.items):
        for slab in range(z.width // LANES):
            xf_ref[item, slab, 8:, :] = x_ref[item, :, slab * LANES : (slab + 1) * LANES].astype(
                jnp.float32
            )


def every_third(z, xf_ref, first):
    items = []
    for item in range(z.items):
        slabs = [
            xf_ref[item, slab, pl.ds(first, z.r, stride=3), :] for slab in range(z.width // LANES)
        ]
        items.append(jnp.concatenate(slabs, axis=1))
    return jnp.concatenate(items, axis=0)


def set_every_third(z, xf_ref, first, value):
    for item in range(z.items):
        for slab in range(z.width // LANES):
            xf_ref[item, slab, pl.ds(first, z.r, stride=3), :] = value[
                item * z.r : (item + 1) * z.r, slab * LANES : (slab + 1) * LANES
            ]


def live_rows(z, me, length, part):
    at = lax.broadcasted_iota(jnp.int32, (z.r, 1), 0) * 3 + part + me * 3 * z.r
    return (at < length).astype(jnp.float32)


def reversal():
    at = lax.broadcasted_iota(jnp.int32, (BLOCK, BLOCK), 0)
    across = lax.broadcasted_iota(jnp.int32, (BLOCK, BLOCK), 1)
    return low((at + across == BLOCK - 1).astype(jnp.float32))


class Copies:
    def __init__(self, batch_size, seq_size):
        self.core = [("batch", 1)]
        self.chips = [("batch", 1 << k) for k in range(1, batch_size.bit_length() - 1)]
        self.line = [("seq", 1 << k) for k in range(seq_size.bit_length() - 1)]
        self.bits = self.core + self.chips + self.line

    def cost(self, bit, size):
        axis, mask = bit
        if bit in self.core:
            return {"core": size / 428e3}
        near = 2 * size / 92e3
        if bit in self.line[:1] or axis == "batch":
            return {bit: near}
        return {"line": near, bit: near * (mask // 2)}

    def orders(self):
        if len(self.bits) != 5:
            links = self.chips + self.line
            return [self.core + links[k:] + links[:k] for k in range(len(links))] * 4
        c, x, y, z0, z1 = self.bits
        names = (
            "xyz0z1",
            "yxz0z1",
            "yz0xz1",
            "z0xyz1",
            "z1xz0y",
            "yxz1z0",
            "xyz1z0",
            "yz0z1x",
            "xz0yz1",
            "z0z1xy",
        )
        found = []
        for name in names:
            order = [c]
            while name:
                for key, bit in (("x", x), ("y", y), ("z0", z0), ("z1", z1)):
                    if name.startswith(key):
                        order.append(bit)
                        name = name[len(key) :]
            found.append(order)
        return found

    def halving(self, rows, order, base):
        down, up = [], []
        for bit in order:
            if rows % 32 == 0:
                rows //= 2
                down.append(("sum", bit, rows, rows))
                up.append(("spread", bit, rows, rows))
            else:
                down.append(("sum", bit, 0, rows))
        return {"base": base, "fixed": [], "steps": down + up[::-1], "rows": rows}

    def by_head(self, heads, hd, base):
        head_bits = self.line[: heads.bit_length() - 1]
        batch_bits = self.core + self.chips
        rest = self.line[len(head_bits) :]
        rows, parts = hd, []
        for bit in batch_bits + rest:
            if rows % 32 == 0:
                rows //= 2
                parts.append((bit, rows))
            else:
                parts.append((bit, 0))
        split = [bit for bit, size in parts if size]
        inner = split[1:]
        stride, strides = rows, {}
        for bit in inner[::-1] + head_bits + split[:1]:
            strides[bit] = stride
            stride *= 2
        down = [("sum", bit, strides.get(bit, 0), size or rows) for bit, size in parts]
        up = [("spread", bit, strides[bit], strides[bit]) for bit in strides]
        fixed = [(bit, strides[bit]) for bit in head_bits]
        return {"base": base, "fixed": fixed, "steps": down + up, "rows": rows, "strides": strides}

    def schedule(self, chains, width, holds=()):
        left = []
        for chain in chains:
            total = [0.0]
            for _, bit, _, rows in chain["steps"][::-1]:
                busy = max(self.cost(bit, 2 * rows * width).values())
                total.append(total[-1] + busy + 2.0)
            left.append(total[::-1])
        free, ready = {}, [chain["ready"] for chain in chains]
        at = [0] * len(chains)
        plan, holds = [], sorted(holds, key=lambda hold: hold[0])
        self.end = 0.0
        while True:
            best = None
            for c, chain in enumerate(chains):
                if at[c] < len(chain["steps"]):
                    _, bit, _, rows = chain["steps"][at[c]]
                    cost = self.cost(bit, 2 * rows * width)
                    start = max([ready[c]] + [free.get(link, 0.0) for link in cost])
                    key = (round(start, 1), -left[c][at[c]], c)
                    if best is None or key < best[0]:
                        best = (key, c, cost, start)
            if best is None:
                return sorted(plan)
            _, c, cost, start = best
            if holds and start >= holds[0][0]:
                since, taken = holds.pop(0)
                for link, busy in taken.items():
                    free[link] = max(free.get(link, 0.0), since) + busy
                continue
            for link, busy in cost.items():
                free[link] = start + busy
            step = chains[c]["steps"][at[c]]
            lag = 0.7 if step[1] in self.core else 2.0
            lag += 1e-6 * 2 * step[3] * width if step[0] == "sum" else 0.0
            ready[c] = start + max(cost.values()) + lag
            self.end = max(self.end, ready[c])
            plan.append((start, c, at[c]))
            at[c] += 1


class Sums:
    def __init__(self, chains, work, landing, total, send_sems, recv_sems):
        self.chains = chains
        self.work, self.landing, self.total = work, landing, total
        self.send_sems, self.recv_sems = send_sems, recv_sems
        self.index = {"batch": lax.axis_index("batch"), "seq": lax.axis_index("seq")}
        self.open = {}
        self.offset = {}
        sem = land = 0
        self.sem, self.land = {}, {}
        for c, chain in enumerate(chains):
            self.offset[c] = chain["base"] + sum(
                self.bit(bit) * stride for bit, stride in chain["fixed"]
            )
            for k, (phase, _, _, rows) in enumerate(chain["steps"]):
                self.sem[c, k] = sem
                sem += 1
                if phase == "sum":
                    self.land[c, k] = land
                    land += rows

    @staticmethod
    def needs(chains):
        steps = [step for chain in chains for step in chain["steps"]]
        return len(steps), sum(step[3] for step in steps if step[0] == "sum")

    def bit(self, bit):
        axis, mask = bit
        return lax.rem(lax.div(self.index[axis], mask), 2)

    def partner(self, bit):
        axis, mask = bit
        return {axis: self.index[axis] + mask - 2 * mask * self.bit(bit)}

    def start(self, c, k):
        if k:
            self.finish(c, k - 1)
        phase, bit, stride, rows = self.chains[c]["steps"][k]
        side = self.bit(bit)
        offset = self.offset[c]
        if phase == "sum":
            other = offset + (1 - side) * stride if stride else offset
            source = self.work.at[pl.ds(pl.multiple_of(other, 16), rows)]
            target = self.landing.at[pl.ds(self.land[c, k], rows)]
            if stride:
                self.offset[c] = offset + side * stride
        else:
            here = pl.ds(pl.multiple_of(offset, 16), rows)
            source, target = self.total.at[here], self.total.at[here]
            self.offset[c] = offset - side * stride
        copy = pltpu.make_async_remote_copy(
            src_ref=source,
            dst_ref=target,
            send_sem=self.send_sems.at[self.sem[c, k]],
            recv_sem=self.recv_sems.at[self.sem[c, k]],
            device_id=self.partner(bit),
            device_id_type=MESH,
        )
        copy.start()
        self.open[c] = copy

    def finish(self, c, k):
        self.open.pop(c).wait()
        steps = self.chains[c]["steps"]
        phase, _, _, rows = steps[k]
        if phase == "sum":
            last = k + 1 == len(steps) or steps[k + 1][0] == "spread"
            held = pl.ds(pl.multiple_of(self.offset[c], 16), rows)
            landed = self.landing[self.land[c, k] : self.land[c, k] + rows, :]
            both = self.work[held, :].astype(jnp.float32) + landed.astype(jnp.float32)
            (self.total if last else self.work)[held, :] = low(both)


OPERANDS = (
    "x",
    "pool_w",
    "gain1",
    "bias1",
    "query_w",
    "key_w",
    "value_w",
    "og",
    "up_w",
    "outer_w",
    "table",
    "position_w",
    "content_bias",
    "position_bias",
    "output_w",
    "gain2",
    "bias2",
    "inner_w",
)


class Pass:
    def __init__(self, z, plan, chains, bits, names, refs):
        self.z = z
        self.__dict__.update(zip(names, refs))
        self.plan, self.chains, self.bits = plan, chains, bits
        self.me = lax.axis_index("seq")
        self.head = lax.rem(self.me, z.heads)
        self.group = lax.div(self.me, z.heads)
        self.sums = Sums(
            chains, self.work, self.landing, self.total, self.sum_send, self.sum_recv
        )
        self.at = 0
        self.loads = {}

    def run(self):
        self.enter()
        self.project()
        self.attend()
        self.feed_forward()
        self.attend_back()
        self.finish_rows()
        self.finish_sums()

    def enter(self):
        z, me = self.z, self.me
        for k, name in enumerate(OPERANDS):
            self.loads[name] = pltpu.make_async_copy(
                getattr(self, name), getattr(self, name + "_v"), self.load_sems.at[k]
            )
            self.loads[name].start()
        barrier = pltpu.get_barrier_semaphore()
        batch = [bit for bit in self.bits if bit[0] == "batch"]
        for step in range(1, z.n):
            pl.semaphore_signal(
                barrier,
                inc=1,
                device_id={"seq": lax.rem(me + step, z.n)},
                device_id_type=MESH,
            )
        for bit in batch:
            pl.semaphore_signal(
                barrier, inc=1, device_id=self.sums.partner(bit), device_id_type=MESH
            )
        self.have("x")
        rows_by_three(z, self.x_v, self.xf)
        pl.semaphore_wait(barrier, z.n - 1 + len(batch))

    def have(self, *names):
        for name in names:
            if name in self.loads:
                self.loads.pop(name).wait()

    def neighbour(self, source, target, sems, step):
        copy = pltpu.make_async_remote_copy(
            src_ref=source,
            dst_ref=target,
            send_sem=sems.at[0],
            recv_sem=sems.at[1],
            device_id={"seq": lax.rem(self.me + step, self.z.n)},
            device_id_type=MESH,
        )
        copy.start()
        return copy

    def exchange(self, source, target, send, recv):
        copies = send_all(self.z.n, self.me, lambda peer: source.at[peer], target, send, recv)
        target[self.me] = source[self.me]
        return copies

    def by_head(self, target, values):
        z = self.z
        pad = [jnp.zeros((z.r, z.hd), jnp.bfloat16)] * (LANES // z.hd - z.units)
        lanes = slice(target % z.heads * z.hd, (target % z.heads + 1) * z.hd)
        sides = []
        for value in values:
            for unit in range(z.units):
                item = target // z.heads * z.units + unit
                sides.append(value[item * z.r : (item + 1) * z.r, lanes])
            sides += pad
        return jnp.concatenate(sides, axis=1)

    def to_rows(self, source_ref, which, target_ref):
        z = self.z
        for source in range(z.n):
            for unit in range(z.units):
                item = source // z.heads * z.units + unit
                head = source % z.heads
                first = which * LANES + unit * z.hd
                target_ref[item * z.r : (item + 1) * z.r, head * z.hd : (head + 1) * z.hd] = (
                    source_ref[source, :, first : first + z.hd]
                )

    def live(self, part):
        z = self.z
        rows = [live_rows(z, self.me, self.lengths[item], part) for item in range(z.items)]
        return jnp.concatenate(rows, axis=0)

    def project(self):
        z, me, r, width = self.z, self.me, self.z.r, self.z.width
        halo = self.neighbour(
            self.x_v.at[:, 3 * r - 16 :, :], self.halo, self.halo_sems, 1
        )
        self.have("pool_w")
        pooled = dot(low(every_third(z, self.xf, 8)), self.pool_w_v[2 * width :, :])
        halo.wait()
        for item in range(z.items):
            before = jnp.where(me > 0, self.halo[item].astype(jnp.float32), 0.0)
            for slab in range(width // LANES):
                self.xf[item, slab, 0:8, :] = before[8:16, slab * LANES : (slab + 1) * LANES]
        for part in range(2):
            pooled += dot(
                low(every_third(z, self.xf, 6 + part)),
                self.pool_w_v[part * width : (part + 1) * width, :],
            )
        self.short[...] = low(pooled)
        normed, inverse = norm_rows(self.short[...].astype(jnp.float32))
        self.normed1[...] = normed
        self.inverse1[...] = inverse
        self.have("gain1", "bias1", "query_w", "key_w", "value_w")
        self.attn_in[...] = low(normed * self.gain1_v[...] + self.bias1_v[...])
        attn_in = self.attn_in[...]
        qkv = [low(dot(attn_in, w[...])) for w in (self.query_w_v, self.key_w_v, self.value_w_v)]
        for target in range(z.n):
            self.qkv_out[target] = self.by_head(target, qkv)
        copies = self.exchange(self.qkv_out, self.qkv_in, self.qkv_send, self.qkv_recv)
        self.have("og", "up_w", "outer_w")
        rows_by_three(z, self.og_v, self.of)
        for part in range(3):
            self.up_rows[:, part * width : (part + 1) * width] = low(
                every_third(z, self.of, 8 + part) * self.live(part)
            )
        self.summed_grad[...] = low(dot_nt(self.up_rows[...], self.up_w_v[...]))
        ff = self.outer_w_v.shape[0]
        for lo in range(0, ff, width):
            self.act_grad[:, lo : lo + width] = dot_nt(
                self.summed_grad[...], self.outer_w_v[lo : lo + width, :]
            )
        self.have("table", "position_w", "content_bias", "position_bias")
        first = self.head * z.hd
        pair = pl.ds(pl.multiple_of(lax.div(first, LANES) * LANES, LANES), LANES)
        both = dot(self.table_v[...], self.position_w_v[:, pair])
        self.pos[...] = low(pltpu.roll(both, LANES - lax.rem(first, LANES), 1)[:, : z.hd])
        for copy in copies:
            copy.wait()

    def attend(self):
        z, r, hd = self.z, self.z.r, self.z.hd
        content_bias = self.content_bias_v[pl.ds(self.head, 1), :]
        position_bias = self.position_bias_v[pl.ds(self.head, 1), :]
        for unit in range(z.units):
            queries, keys, values = (
                self.qkv_in[:, :, which * LANES + unit * hd : which * LANES + (unit + 1) * hd]
                .reshape(z.length, hd)
                for which in range(3)
            )
            self.qc[unit] = low(queries.astype(jnp.float32) + content_bias)
            self.qp[unit] = low(queries.astype(jnp.float32) + position_bias)
            self.keys[unit] = keys
            self.values[unit] = values
        for block in range(z.length // BLOCK):
            lo, hi = block * BLOCK, (block + 1) * BLOCK
            sides = []
            for unit in range(z.units):
                length = self.lengths[self.group * z.units + unit]
                content = dot_nt(self.qc[unit, lo:hi, :], self.keys[unit, :hi, :])
                by_distance = dot_nt(self.qp[unit, lo:hi, :], self.pos[z.length - hi :, :])
                placed = pltpu.roll(by_distance, lo + 1, 1, stride=1, stride_axis=0)
                query_at = lo + lax.broadcasted_iota(jnp.int32, (BLOCK, hi), 0)
                key_at = lax.broadcasted_iota(jnp.int32, (BLOCK, hi), 1)
                valid = (key_at <= query_at) & (3 * key_at < length)
                logits = jnp.where(valid, (content + placed) * hd**-0.5, masked_value)
                raised = jnp.exp(logits - jnp.max(logits, axis=-1, keepdims=True))
                probs = raised / jnp.sum(raised, axis=-1, keepdims=True)
                self.probs[unit, lo:hi, :hi] = probs
                sides.append(low(dot(low(probs), self.values[unit, :hi, :])))
            sides += [jnp.zeros((BLOCK, hd), jnp.bfloat16)] * (LANES // hd - z.units)
            per = BLOCK // r
            self.att_out[block * per : (block + 1) * per] = jnp.concatenate(
                sides, axis=1
            ).reshape(per, r, LANES)
        copies = self.exchange(self.att_out, self.att_in, self.att_send, self.att_recv)
        self.have("output_w", "gain2", "bias2", "inner_w")
        for copy in copies:
            copy.wait()

    def feed_forward(self):
        z, width = self.z, self.z.width
        ff = self.outer_w_v.shape[0]
        self.to_rows(self.att_in, 0, self.att)
        hidden = self.short[...].astype(jnp.float32) + dot(self.att[...], self.output_w_v[...])
        normed, inverse = norm_rows(hidden)
        self.hidden[...] = hidden
        self.ffn_in[...] = low(normed * self.gain2_v[...] + self.bias2_v[...])
        ffn_in = self.ffn_in[...]
        ffn_grad = jnp.zeros((z.rows, width), jnp.float32)
        for lo in range(0, ff, width):
            cut = slice(lo, lo + width)
            inner = dot(ffn_in, self.inner_w_v[:, cut])
            normal_cdf = 0.5 * (1.0 + lax.erf(inner * 0.7071067811865476))
            density = jnp.exp(-0.5 * inner * inner) * 0.3989422804014327
            self.act[:, cut] = low(inner * normal_cdf)
            inner_grad = low(self.act_grad[:, cut] * (normal_cdf + inner * density))
            self.inner_grad[:, cut] = inner_grad
            ffn_grad += dot_nt(inner_grad, self.inner_w_v[:, cut])
        self.small_work[0, 2:3, :] = jnp.sum(ffn_grad * normed, axis=0, keepdims=True)
        self.small_work[0, 3:4, :] = jnp.sum(ffn_grad, axis=0, keepdims=True)
        hidden_grad = self.summed_grad[...].astype(jnp.float32) + norm_backward(
            ffn_grad, normed, inverse, self.gain2_v[...]
        )
        self.hidden_grad[...] = hidden_grad
        self.branch[...] = low(hidden_grad)
        att_grad = low(dot_nt(self.branch[...], self.output_w_v[...]))
        for target in range(z.n):
            self.grad_out[target] = self.by_head(target, [att_grad])
        self.copies = self.exchange(self.grad_out, self.grad_in, self.grad_send, self.grad_recv)
        row = 0
        for lo in range(0, ff, width):
            self.work[row : row + width, :] = low(
                dot_tn(self.act[:, lo : lo + width], self.summed_grad[...])
            )
            row += width
            self.advance(0.6 * row / width)
        for lo in range(0, ff, width):
            self.work[row : row + width, :] = low(
                dot_tn(self.ffn_in[...], self.inner_grad[:, lo : lo + width])
            )
            row += width
            self.advance(0.6 * row / width)
        self.work[row : row + width, :] = low(dot_tn(self.att[...], self.branch[...]))
        row += width
        self.summed[...] = low(self.hidden[...] + dot(self.act[...], self.outer_w_v[...]))
        for lo in range(0, 3 * width, width):
            self.work[row : row + width, :] = low(
                dot_tn(self.summed[...], self.up_rows[:, lo : lo + width])
            )
            row += width
            self.advance(1.8 + 0.6 * row / width)
        self.row = row
        for copy in self.copies:
            copy.wait()

    def upsample(self):
        z, width = self.z, self.z.width
        for part in range(3):
            up = dot(self.summed[...], self.up_w_v[:, part * width : (part + 1) * width])
            set_every_third(
                z, self.bf, 8 + part, every_third(z, self.xf, 8 + part) + up * self.live(part)
            )
        for item in range(z.items):
            for slab in range(width // LANES):
                self.block_low[item, :, slab * LANES : (slab + 1) * LANES] = low(
                    self.bf[item, slab, 8:, :]
                )
        self.block_store = pltpu.make_async_copy(
            self.block_low, self.block_out, self.out_sems.at[0]
        )
        self.block_store.start()

    def attend_back(self):
        z, r, hd, length = self.z, self.z.r, self.z.hd, self.z.length
        flip = reversal()
        content_sum = jnp.zeros((1, hd), jnp.float32)
        position_sum = jnp.zeros((1, hd), jnp.float32)
        self.key_t[...] = jnp.zeros_like(self.key_t)
        self.value_t[...] = jnp.zeros_like(self.value_t)
        self.table_t[...] = jnp.zeros_like(self.table_t)
        now = EARLY_DONE
        for unit in range(z.units):
            att_grad = self.grad_in[:, :, unit * hd : (unit + 1) * hd].reshape(length, hd)
            for block in range(length // BLOCK):
                lo, hi = block * BLOCK, (block + 1) * BLOCK
                block_grad = att_grad[lo:hi]
                probs = self.probs[unit, lo:hi, :hi]
                prob_grad = dot_nt(block_grad, self.values[unit, :hi, :])
                delta = jnp.sum(probs * prob_grad, axis=-1, keepdims=True)
                raw = low(probs * (prob_grad - delta) * hd**-0.5)
                content = dot(raw, self.keys[unit, :hi, :])
                self.key_t[unit, :, :hi] += dot_tn(self.qc[unit, lo:hi, :], raw)
                self.value_t[unit, :, :hi] += dot_tn(block_grad, low(probs))
                by_distance = low(pltpu.roll(dot(flip, raw), 0, 1, stride=1, stride_axis=0))
                position = dot(by_distance, self.pos[length - hi :, :])
                upper = low(position)
                lower = low(position - upper.astype(jnp.float32))
                position = dot(flip, upper) + dot(flip, lower)
                flipped_q = low(dot(flip, self.qp[unit, lo:hi, :]))
                self.table_t[unit, :, length - hi :] += dot_tn(flipped_q, by_distance)
                content_sum += jnp.sum(content, axis=0, keepdims=True)
                position_sum += jnp.sum(position, axis=0, keepdims=True)
                self.query_grad[unit, lo:hi, :] = low(content + position)
                now += 1.2
                self.advance(now)
        own = lax.broadcasted_iota(jnp.int32, (1, z.width), 1) // hd == self.head
        for row, value in ((4, content_sum), (5, position_sum)):
            spread = jnp.concatenate([value] * z.heads, axis=1)
            self.small_work[0, row : row + 1, :] = jnp.where(own, spread, 0.0)
        pad = [jnp.zeros((length, hd), jnp.bfloat16)] * (LANES // hd - z.units)
        sides = [self.query_grad[unit] for unit in range(z.units)] + pad
        sides += [low(self.key_t[unit].T) for unit in range(z.units)] + pad
        sides += [low(self.value_t[unit].T) for unit in range(z.units)] + pad
        self.back_out[...] = jnp.concatenate(sides, axis=1).reshape(z.n, r, 3 * LANES)
        copies = self.exchange(self.back_out, self.back_in, self.back_send, self.back_recv)
        table_sum = 0.0
        for unit in range(z.units):
            table_sum += dot(low(self.table_t[unit]), self.table_v[...])
        half = hd // 2
        base = self.chains[-1]["base"]
        for side in range(2):
            at = pl.multiple_of(base + side * z.heads * half + self.head * half, 16)
            self.work[pl.ds(at, half), :] = low(table_sum[side * half : (side + 1) * half])
        self.advance(BACK_DONE)
        self.upsample()
        self.advance(BACK_DONE + 4.0)
        for copy in copies:
            copy.wait()

    def finish_rows(self):
        z, me, r, width = self.z, self.me, self.z.r, self.z.width
        for which in range(3):
            self.to_rows(self.back_in, which, self.row_grad.at[which])
        attn_grad = (
            dot_nt(self.row_grad[0], self.query_w_v[...])
            + dot_nt(self.row_grad[1], self.key_w_v[...])
            + dot_nt(self.row_grad[2], self.value_w_v[...])
        )
        normed = self.normed1[...]
        self.small_work[0, 0:1, :] = jnp.sum(attn_grad * normed, axis=0, keepdims=True)
        self.small_work[0, 1:2, :] = jnp.sum(attn_grad, axis=0, keepdims=True)
        self.small_work[0, 6:8, :] = jnp.zeros((2, width), jnp.float32)
        short_grad = low(
            self.hidden_grad[...]
            + norm_backward(attn_grad, normed, self.inverse1[...], self.gain1_v[...])
        )
        for item in range(z.items):
            self.first_rows[item] = short_grad[item * r : item * r + 16, :]
            self.later[item, 0:r, :] = short_grad[item * r : (item + 1) * r, :].astype(jnp.float32)
        halo = self.neighbour(self.first_rows, self.next_rows, self.next_sems, z.n - 1)
        self.small_start(0)
        row = self.row
        for which in range(3):
            self.work[row : row + width, :] = low(dot_tn(self.attn_in[...], self.row_grad[which]))
            row += width
        self.advance(LATE[0])
        own = dot_nt(short_grad, self.pool_w_v[2 * width :, :])
        set_every_third(z, self.of, 8, every_third(z, self.of, 8) + own)
        self.work[row + 2 * width : row + 3 * width, :] = low(
            dot_tn(low(every_third(z, self.xf, 8)), short_grad)
        )
        halo.wait()
        for item in range(z.items):
            after = jnp.where(me < z.n - 1, self.next_rows[item].astype(jnp.float32), 0.0)
            self.later[item, r : r + 8, :] = after[0:8, :]
        later = low(
            jnp.concatenate([self.later[item, 1 : r + 1, :] for item in range(z.items)], axis=0)
        )
        for part in range(2):
            cut = slice(row + part * width, row + (part + 1) * width)
            self.work[cut, :] = low(dot_tn(low(every_third(z, self.xf, 9 + part)), later))
        self.advance(LATE[1])
        for part in range(2):
            back = dot_nt(later, self.pool_w_v[part * width : (part + 1) * width, :])
            first = 9 + part
            set_every_third(z, self.of, first, every_third(z, self.of, first) + back)
        for item in range(z.items):
            for slab in range(width // LANES):
                self.input_rows[item, :, slab * LANES : (slab + 1) * LANES] = self.of[
                    item, slab, 8:, :
                ]
        self.input_store = pltpu.make_async_copy(
            self.input_rows, self.input_grad, self.out_sems.at[1]
        )
        self.input_store.start()

    def advance(self, now):
        while self.at < len(self.plan) and self.plan[self.at][0] <= now:
            _, c, k = self.plan[self.at]
            self.sums.start(c, k)
            self.at += 1

    def small_start(self, k):
        self.small_copy = pltpu.make_async_remote_copy(
            src_ref=self.small_work.at[k],
            dst_ref=self.small_landing.at[k],
            send_sem=self.small_send.at[k],
            recv_sem=self.small_recv.at[k],
            device_id=self.sums.partner(self.bits[k]),
            device_id_type=MESH,
        )
        self.small_copy.start()

    def finish_sums(self):
        steps = len(self.bits)
        first = self.plan[self.at][0] if self.at < len(self.plan) else 0.0
        for k in range(steps):
            self.advance(first + 3.0 * (k + 1))
            self.small_copy.wait()
            self.small_work[k + 1] = self.small_work[k] + self.small_landing[k]
            if k + 1 < steps:
                self.small_start(k + 1)
        self.small_total[...] = self.small_work[steps]
        ends = {}
        for order, (_, c, k) in enumerate(self.plan):
            ends[c] = order
        stores = []
        for c in sorted(ends, key=ends.get):
            while self.at <= ends[c]:
                self.sums.start(*self.plan[self.at][1:])
                self.at += 1
            self.sums.finish(c, len(self.chains[c]["steps"]) - 1)
            at, size = self.chains[c]["base"], self.chains[c]["all"]
            stores.append(
                pltpu.make_async_copy(
                    self.total.at[at : at + size],
                    self.total_out.at[at : at + size],
                    self.store_sems.at[c],
                )
            )
            stores[-1].start()
        for store in stores + [self.block_store, self.input_store]:
            store.wait()


def block_kernel(z, plan, chains, bits, names, *refs):
    Pass(z, plan, chains, bits, names, refs).run()


def chains_of(z, ff, nb):
    width = z.width
    copies = Copies(nb, z.n)
    orders = copies.orders()
    units = 3 * (ff * 2 + width * 10) // width // 3
    early = 2 * ff // width + 4
    chosen = CHAINS if len(copies.bits) == 5 and sum(rows for rows, _ in CHAINS) == units else None
    if chosen is None:
        chosen = [(1, k) for k in range(units)]
    chains, base = [], 0
    for rows, order in chosen:
        chains.append(copies.halving(rows * width, orders[order % len(orders)], base * width))
        chains[-1]["all"] = rows * width
        base += rows
        if base <= early - 3:
            chains[-1]["ready"] = 0.6 * base
        elif base <= early:
            chains[-1]["ready"] = 1.8 + 0.6 * base
        else:
            chains[-1]["ready"] = LATE[0] if base <= early + 3 else LATE[1]
    chains.append(copies.by_head(z.heads, z.hd, base * width))
    chains[-1]["all"] = z.heads * z.hd
    chains[-1]["ready"] = BACK_DONE
    return copies, chains


def result_kernel(
    z,
    ff,
    total_ref,
    small_ref,
    block_in_ref,
    input_in_ref,
    block_ref,
    input_ref,
    pool_ref,
    gain1_ref,
    bias1_ref,
    query_ref,
    key_ref,
    value_ref,
    position_ref,
    content_bias_ref,
    position_bias_ref,
    output_ref,
    gain2_ref,
    bias2_ref,
    inner_ref,
    outer_ref,
    up_ref,
    held,
    wide,
    load_sems,
    store_sems,
    pass_sems,
):
    width = z.width
    through = [
        pltpu.make_async_copy(block_in_ref, block_ref, pass_sems.at[0]),
        pltpu.make_async_copy(input_in_ref, input_ref, pass_sems.at[1]),
    ]
    blocks = held.shape[0]
    loads = [
        pltpu.make_async_copy(
            total_ref.at[k * width : (k + 1) * width], held.at[k], load_sems.at[k]
        )
        for k in range(blocks)
    ]
    for copy in loads + through:
        copy.start()
    places = [outer_ref.at[k * width : (k + 1) * width] for k in range(ff // width)]
    places += [inner_ref.at[:, k * width : (k + 1) * width] for k in range(ff // width)]
    places += [output_ref]
    places += [up_ref.at[:, k * width : (k + 1) * width] for k in range(3)]
    places += [query_ref, key_ref, value_ref]
    places += [pool_ref.at[k * width : (k + 1) * width] for k in range(3)]
    places += [position_ref]
    gain1_ref[...] = small_ref[0:1, :]
    bias1_ref[...] = small_ref[1:2, :]
    gain2_ref[...] = small_ref[2:3, :]
    bias2_ref[...] = small_ref[3:4, :]
    for head in range(z.heads):
        lanes = slice(head * z.hd, (head + 1) * z.hd)
        content_bias_ref[head : head + 1, :] = small_ref[4:5, lanes]
        position_bias_ref[head : head + 1, :] = small_ref[5:6, lanes]
    stores = []
    for k in range(blocks):
        loads[k].wait()
        if k + 1 < blocks:
            wide[k] = held[k].astype(jnp.float32)
        else:
            half = z.hd // 2
            for head in range(z.heads):
                rows = [
                    held[k, side * z.heads * half + head * half :][:half] for side in range(2)
                ]
                both = jnp.concatenate(rows, axis=0).astype(jnp.float32)
                wide[k, :, head * z.hd : (head + 1) * z.hd] = both.T
        stores.append(pltpu.make_async_copy(wide.at[k], places[k], store_sems.at[k]))
        stores[-1].start()
    for copy in stores + through:
        copy.wait()


def body(
    byte_rows,
    item_lengths,
    out_grad,
    pool_weight,
    norm1_gain,
    norm1_bias,
    query_weight,
    key_weight,
    value_weight,
    position_weight,
    content_bias,
    position_bias,
    output_weight,
    norm2_gain,
    norm2_bias,
    inner_weight,
    outer_weight,
    upsample_weight,
):
    items, full_rows, width = byte_rows.shape
    heads, hd = content_bias.shape
    n = lax.axis_size("seq")
    ff = inner_weight.shape[1]
    z = Sizes(n, items, full_rows, width, heads)
    r, units, length, rows = z.r, z.units, z.length, z.rows
    bf, f4 = jnp.bfloat16, jnp.float32
    slabs = width // LANES
    dma = pltpu.SemaphoreType.DMA
    copies, chains = chains_of(z, ff, lax.axis_size("batch"))
    near = 16 * n * 0.001
    holds = [
        (0.0, {("seq", 1): 0.7 * near * 16, "line": 1.4 * near * 16}),
        (BACK_DONE - 2.0, {("seq", 1): 2.1 * near * 16, "line": 4.2 * near * 16}),
    ]
    plan = copies.schedule(chains, width, holds)
    bits = copies.bits
    count, landing = Sums.needs(chains)
    total_rows = chains[-1]["base"] + chains[-1]["all"]
    operands = {
        "x": byte_rows,
        "pool_w": pool_weight,
        "gain1": norm1_gain.reshape(1, width),
        "bias1": norm1_bias.reshape(1, width),
        "query_w": query_weight,
        "key_w": key_weight,
        "value_w": value_weight,
        "og": out_grad,
        "up_w": upsample_weight,
        "outer_w": outer_weight,
        "table": distance_table(length, width),
        "position_w": position_weight,
        "content_bias": content_bias,
        "position_bias": position_bias,
        "output_w": output_weight,
        "gain2": norm2_gain.reshape(1, width),
        "bias2": norm2_bias.reshape(1, width),
        "inner_w": inner_weight,
    }
    outs = {
        "block_out": (byte_rows.shape, bf, ANY),
        "input_grad": (byte_rows.shape, f4, ANY),
        "total_out": ((total_rows, width), bf, ANY),
        "small_total": ((8, width), f4, VMEM),
    }
    slab_rows = pltpu.VMEM((items, slabs, 3 * r + 8, LANES), f4)
    scratch = {name + "_v": pltpu.VMEM(operands[name].shape, operands[name].dtype) for name in OPERANDS}
    scratch.update(
        xf=slab_rows,
        of=slab_rows,
        bf=slab_rows,
        block_low=pltpu.VMEM(byte_rows.shape, bf),
        input_rows=pltpu.VMEM(byte_rows.shape, f4),
        halo=pltpu.VMEM((items, 16, width), bf),
        first_rows=pltpu.VMEM((items, 16, width), bf),
        next_rows=pltpu.VMEM((items, 16, width), bf),
        later=pltpu.VMEM((items, r + 8, width), f4),
        short=pltpu.VMEM((rows, width), bf),
        normed1=pltpu.VMEM((rows, width), f4),
        inverse1=pltpu.VMEM((rows, 1), f4),
        attn_in=pltpu.VMEM((rows, width), bf),
        qkv_out=pltpu.VMEM((n, r, 3 * LANES), bf),
        qkv_in=pltpu.VMEM((n, r, 3 * LANES), bf),
        att_out=pltpu.VMEM((n, r, LANES), bf),
        att_in=pltpu.VMEM((n, r, LANES), bf),
        grad_out=pltpu.VMEM((n, r, LANES), bf),
        grad_in=pltpu.VMEM((n, r, LANES), bf),
        back_out=pltpu.VMEM((n, r, 3 * LANES), bf),
        back_in=pltpu.VMEM((n, r, 3 * LANES), bf),
        qc=pltpu.VMEM((units, length, hd), bf),
        qp=pltpu.VMEM((units, length, hd), bf),
        keys=pltpu.VMEM((units, length, hd), bf),
        values=pltpu.VMEM((units, length, hd), bf),
        pos=pltpu.VMEM((length, hd), bf),
        probs=pltpu.VMEM((units, length, length), f4),
        query_grad=pltpu.VMEM((units, length, hd), bf),
        key_t=pltpu.VMEM((units, hd, length), f4),
        value_t=pltpu.VMEM((units, hd, length), f4),
        table_t=pltpu.VMEM((units, hd, length), f4),
        att=pltpu.VMEM((rows, width), bf),
        hidden=pltpu.VMEM((rows, width), f4),
        ffn_in=pltpu.VMEM((rows, width), bf),
        act=pltpu.VMEM((rows, ff), bf),
        act_grad=pltpu.VMEM((rows, ff), f4),
        inner_grad=pltpu.VMEM((rows, ff), bf),
        up_rows=pltpu.VMEM((rows, 3 * width), bf),
        summed=pltpu.VMEM((rows, width), bf),
        summed_grad=pltpu.VMEM((rows, width), bf),
        hidden_grad=pltpu.VMEM((rows, width), f4),
        branch=pltpu.VMEM((rows, width), bf),
        row_grad=pltpu.VMEM((3, rows, width), bf),
        work=pltpu.VMEM((total_rows, width), bf),
        landing=pltpu.VMEM((landing, width), bf),
        total=pltpu.VMEM((total_rows, width), bf),
        small_work=pltpu.VMEM((len(bits) + 1, 8, width), f4),
        small_landing=pltpu.VMEM((len(bits), 8, width), f4),
        load_sems=dma((len(OPERANDS),)),
        halo_sems=dma((2,)),
        next_sems=dma((2,)),
        qkv_send=dma((n,)),
        qkv_recv=dma((n,)),
        att_send=dma((n,)),
        att_recv=dma((n,)),
        grad_send=dma((n,)),
        grad_recv=dma((n,)),
        back_send=dma((n,)),
        back_recv=dma((n,)),
        sum_send=dma((count,)),
        sum_recv=dma((count,)),
        small_send=dma((len(bits),)),
        small_recv=dma((len(bits),)),
        store_sems=dma((len(chains),)),
        out_sems=dma((2,)),
    )
    names = ("lengths",) + OPERANDS + tuple(outs) + tuple(scratch)
    block_out, input_grad, total, small_t = pl.pallas_call(
        functools.partial(block_kernel, z, plan, chains, bits, names),
        out_shape=[jax.ShapeDtypeStruct(shape, dtype) for shape, dtype, _ in outs.values()],
        in_specs=[SMEM] + [ANY] * len(OPERANDS),
        out_specs=[space for _, _, space in outs.values()],
        scratch_shapes=list(scratch.values()),
        compiler_params=pltpu.CompilerParams(
            collective_id=0, has_side_effects=True, vmem_limit_bytes=60 * 2**20
        ),
    )(item_lengths, *(operands[name] for name in OPERANDS))
    blocks = total.shape[0] // width
    shapes = [
        ((items, full_rows, width), bf, ANY),
        ((items, full_rows, width), f4, ANY),
        ((3 * width, width), f4, ANY),
        ((1, width), f4, VMEM),
        ((1, width), f4, VMEM),
        ((width, width), f4, ANY),
        ((width, width), f4, ANY),
        ((width, width), f4, ANY),
        ((width, width), f4, ANY),
        ((heads, hd), f4, VMEM),
        ((heads, hd), f4, VMEM),
        ((width, width), f4, ANY),
        ((1, width), f4, VMEM),
        ((1, width), f4, VMEM),
        ((width, ff), f4, ANY),
        ((ff, width), f4, ANY),
        ((width, 3 * width), f4, ANY),
    ]
    results = pl.pallas_call(
        functools.partial(result_kernel, z, ff),
        out_shape=[jax.ShapeDtypeStruct(shape, dtype) for shape, dtype, _ in shapes],
        in_specs=[ANY, VMEM, ANY, ANY],
        out_specs=[space for _, _, space in shapes],
        scratch_shapes=[
            pltpu.VMEM((blocks, width, width), bf),
            pltpu.VMEM((blocks, width, width), f4),
            dma((blocks,)),
            dma((blocks,)),
            dma((2,)),
        ],
        compiler_params=pltpu.CompilerParams(vmem_limit_bytes=50 * 2**20),
    )(total, small_t, block_out, input_grad)
    return tuple(
        value.reshape(width) if value.shape == (1, width) else value for value in results
    )


def solution(mesh):
    split = P("batch", "seq", None)
    in_specs = (split, P("batch"), split) + (P(),) * 15
    out_specs = (split, split) + (P(),) * 15
    return jax.shard_map(body, mesh=mesh, in_specs=in_specs, out_specs=out_specs, check_vma=False)
```

time: 193 us -> 166 us (0.86)
  Pallas kernels: 177 us -> 162 us
  local copies, waits for them, and re-layouts: 12 us -> 2.84 us
  other arithmetic: 2.72 us -> 0 us
    pallas_call x5 -> x1, Pallas kernels: 166 us -> 151 us  [body(): pl.pallas_call(functools.partial(block_kernel, z, plan, chains, bits, nam...]
    unnamed x48 -> x6, local copies, waits for them, and re-layouts: 9.3 us -> 2.84 us
    mul x4 -> x0, local copies, waits for them, and re-layouts: 2.09 us -> none  [body(): head_bias_g[:, None, :] * mine]
where the time goes in v4:
time: 166 us
  Pallas kernels  162 us (98%)
  local copies, waits for them, and re-layouts  2.84 us (2%)
    pallas_call x1, Pallas kernels, body(): pl.pallas_call(functools.partial(block_kernel, z, plan, chains, bits, nam...  151 us
    pallas_call x1, Pallas kernels, body(): pl.pallas_call(functools.partial(result_kernel, z, ff), out_shape=[jax.Sh...  11.3 us

profile of v4, /device:TPU:0, one launch (start us, length us, event | category | flops | bytes accessed | tf_op | source)
XLA Modules:
  0.0 165.8 jit_solution(6666242735769086544)
XLA Ops:
  0.7 150.8 %shard_map.314 = (bf16[2,192,512]{2,1,0:T(8,128)(2,1)}, f32[2,192,512]{2,1,0:T(8,128)}, bf16[9728,512]{1,0:T(8,128)(2,1)}, f32[8,512]{1,0:T(8,128)}) custom-call(s32[2]{0:T(128)} %refs_0_.1, bf16[2,192,512]{2,1,0:T(8,128)(2,1)} %refs_1_.1, bf16[1536,512]{1,0:T(8,128)(2,1)} %refs_2_.1, f32[1,512]{1,0:T(1,128)} %bitcast.8, f32[1,512]{1,0:T(1,128)} %bitcast.9, ...), custom_call_target="tpu_custom_call" | custom-call | tf_op jit(solution)/shard_map/pallas_call | solution.py:1016
  151.5 0.0 copy-start
  151.5 1.1 copy-done
  152.6 0.0 copy-start.1
  152.6 1.0 copy-done.1
  153.6 0.0 copy-start.2
  153.6 0.7 copy-done.2
  154.3 11.3 %shard_map.315 = (bf16[2,192,512]{2,1,0:T(8,128)(2,1)}, f32[2,192,512]{2,1,0:T(8,128)}, f32[1536,512]{1,0:T(8,128)}, f32[1,512]{1,0:T(1,128)}, f32[1,512]{1,0:T(...) custom-call(bf16[9728,512]{1,0:T(8,128)(2,1)} %get-tuple-element.38., ...), custom_call_target="tpu_custom_call" | custom-call | tf_op jit(solution)/shard_map/pallas_call | solution.py:1046
Async XLA Ops:
  151.5 1.1 copy-start
  152.6 1.0 copy-start.1
  153.6 0.7 copy-start.2

commit v5 on v4

--- a/solution.py
+++ b/solution.py
@@ -11,10 +11,25 @@
 MESH = pl.DeviceIdType.MESH
 epsilon = 1e-05
 masked_value = -1e30
-CHAINS = [(2, 0), (2, 1), (1, 2), (1, 3), (2, 0), (1, 1), (1, 8), (1, 4), (1, 5), (1, 0), (1, 1), (1, 3), (1, 9), (1, 2), (1, 4)]
-EARLY_DONE = 9.0
-BACK_DONE = 21.0
-LATE = (31.0, 34.0)
+CHAINS = (
+    (1, "z1xyz0"),
+    (2, "xyz0z1"),
+    (1, "z0z1yx"),
+    (2, "yxz0z1"),
+    (1, "z0yz1x"),
+    (1, "yxz0z1"),
+    (2, "xyz0z1"),
+    (1, "yxz1z0"),
+    (1, "z0xyz1"),
+    (1, "xyz0z1"),
+    (1, "yxz0z1"),
+    (1, "yxz1z0"),
+    (1, "yxz0z1"),
+    (1, "xyz1z0"),
+    (1, "xyz0z1"),
+)
+LAG, CORE_LAG, ISSUE, MARGIN = 2.8, 1.0, 0.15, 0.3
+UNIT, BLOCK_STEP, SEND, TABLE, UP, ROWS, QKV, POOL, INPUT = 0.33, 0.7, 0.3, 0.4, 1.5, 2.2, 0.9, 1.6, 1.2
 BLOCK = 128
 LANES = 128
 VMEM = pl.BlockSpec(memory_space=pltpu.VMEM)
@@ -81,22 +96,30 @@
         assert n % heads == 0 and self.units * self.hd <= LANES
 
 
-def send_all(n, me, source, target, send_sem, recv_sem):
-    copies = []
-    for step in range(1, n):
-        peer = lax.rem(me + step, n)
-        copies.append(
+class Exchange:
+    def __init__(self, n, me, source, target, sems):
+        target[me] = source[me]
+        for step in range(1, n):
+            peer = lax.rem(me + step, n)
             pltpu.make_async_remote_copy(
-                src_ref=source(peer),
+                src_ref=source.at[peer],
                 dst_ref=target.at[me],
-                send_sem=send_sem.at[step],
-                recv_sem=recv_sem.at[step],
+                send_sem=sems.at[0],
+                recv_sem=sems.at[1],
                 device_id={"seq": peer},
                 device_id_type=MESH,
-            )
-        )
-        copies[-1].start()
-    return copies
+            ).start()
+        self.all = pltpu.make_async_remote_copy(
+            src_ref=source.at[1:],
+            dst_ref=target.at[1:],
+            send_sem=sems.at[0],
+            recv_sem=sems.at[1],
+            device_id={"seq": lax.rem(me + 1, n)},
+            device_id_type=MESH,
+        )
+
+    def wait(self):
+        self.all.wait()
 
 
 def rows_by_three(z, x_ref, xf_ref):
@@ -152,33 +175,25 @@
             return {bit: near}
         return {"line": near, bit: near * (mask // 2)}
 
-    def orders(self):
-        if len(self.bits) != 5:
-            links = self.chips + self.line
-            return [self.core + links[k:] + links[:k] for k in range(len(links))] * 4
-        c, x, y, z0, z1 = self.bits
-        names = (
-            "xyz0z1",
-            "yxz0z1",
-            "yz0xz1",
-            "z0xyz1",
-            "z1xz0y",
-            "yxz1z0",
-            "xyz1z0",
-            "yz0z1x",
-            "xz0yz1",
-            "z0z1xy",
-        )
-        found = []
-        for name in names:
-            order = [c]
-            while name:
-                for key, bit in (("x", x), ("y", y), ("z0", z0), ("z1", z1)):
-                    if name.startswith(key):
-                        order.append(bit)
-                        name = name[len(key) :]
-            found.append(order)
-        return found
+    def order(self, name):
+        order = list(self.core)
+        links = {"x": self.chips[0], "y": self.line[0], "z0": self.line[1], "z1": self.line[2]}
+        while name:
+            for key, bit in links.items():
+                if name.startswith(key):
+                    order.append(bit)
+                    name = name[len(key) :]
+        return order
+
+    def rotated(self, k):
+        links = self.chips + self.line
+        k %= len(links)
+        return self.core + links[k:] + links[:k]
+
+    def hold(self, size):
+        count = 1 << len(self.line)
+        y = 2 * size * count / 2 / 92e3
+        return {self.line[0]: y, "line": 1.5 * y, self.line[-1]: 2 * y}
 
     def halving(self, rows, order, base):
         down, up = [], []
@@ -213,45 +228,77 @@
         fixed = [(bit, strides[bit]) for bit in head_bits]
         return {"base": base, "fixed": fixed, "steps": down + up, "rows": rows, "strides": strides}
 
-    def schedule(self, chains, width, holds=()):
+    def schedule(self, chains, width, segments, size):
         left = []
         for chain in chains:
             total = [0.0]
             for _, bit, _, rows in chain["steps"][::-1]:
                 busy = max(self.cost(bit, 2 * rows * width).values())
-                total.append(total[-1] + busy + 2.0)
+                total.append(total[-1] + busy + LAG)
             left.append(total[::-1])
-        free, ready = {}, [chain["ready"] for chain in chains]
-        at = [0] * len(chains)
-        plan, holds = [], sorted(holds, key=lambda hold: hold[0])
-        self.end = 0.0
+        free, at, plan = {}, [0] * len(chains), []
+        ready = [None] * len(chains)
+        now, segment, sent = 0.0, 0, {}
+
+        def hold(name, times):
+            for link, busy in self.hold(times * size).items():
+                free[link] = max(free.get(link, 0.0), now) + busy
+            sent[name] = max(free[link] for link in self.hold(size)) + LAG + 0.5
+
+        hold("grad", 1)
         while True:
-            best = None
+            best, later = None, []
             for c, chain in enumerate(chains):
-                if at[c] < len(chain["steps"]):
+                if ready[c] is None or at[c] > len(chain["steps"]):
+                    continue
+                if at[c] == len(chain["steps"]):
+                    start = ready[c] + MARGIN
+                else:
                     _, bit, _, rows = chain["steps"][at[c]]
                     cost = self.cost(bit, 2 * rows * width)
-                    start = max([ready[c]] + [free.get(link, 0.0) for link in cost])
-                    key = (round(start, 1), -left[c][at[c]], c)
-                    if best is None or key < best[0]:
-                        best = (key, c, cost, start)
-            if best is None:
-                return sorted(plan)
-            _, c, cost, start = best
-            if holds and start >= holds[0][0]:
-                since, taken = holds.pop(0)
-                for link, busy in taken.items():
-                    free[link] = max(free.get(link, 0.0), since) + busy
+                    start = max([ready[c] + (MARGIN if at[c] else 0.0)] + [free.get(link, 0.0) - 0.3 for link in cost])
+                if start <= now:
+                    key = (-left[c][at[c]], c)
+                    best = key if best is None or key < best else best
+                else:
+                    later.append(start)
+            if best is not None:
+                c = best[1]
+                k = at[c]
+                at[c] += 1
+                steps = chains[c]["steps"]
+                now += ISSUE
+                if k and steps[k - 1][0] == "sum":
+                    now += 0.4e-6 * 2 * steps[k - 1][3] * width
+                if k == len(steps):
+                    plan.append(("end", c, k))
+                    continue
+                _, bit, _, rows = steps[k]
+                cost = self.cost(bit, 2 * rows * width)
+                start = max([now] + [free.get(link, 0.0) for link in cost])
+                for link, busy in cost.items():
+                    free[link] = start + busy
+                lag = CORE_LAG if bit in self.core else LAG
+                ready[c] = start + max(cost.values()) + lag
+                plan.append(("sum", c, k))
                 continue
-            for link, busy in cost.items():
-                free[link] = start + busy
-            step = chains[c]["steps"][at[c]]
-            lag = 0.7 if step[1] in self.core else 2.0
-            lag += 1e-6 * 2 * step[3] * width if step[0] == "sum" else 0.0
-            ready[c] = start + max(cost.values()) + lag
-            self.end = max(self.end, ready[c])
-            plan.append((start, c, at[c]))
-            at[c] += 1
+            if segment < len(segments):
+                name, busy, releases = segments[segment]
+                due = sent.get(name, 0.0)
+                if due <= now:
+                    plan.append(("seg", segment, name))
+                    now += busy
+                    for c in releases:
+                        ready[c] = now
+                    if name == "send":
+                        hold("back", 3)
+                    segment += 1
+                    continue
+                later.append(due)
+            if not later:
+                self.end = now
+                return plan
+            now = max(now + 0.01, min(later))
 
 
 class Sums:
@@ -264,7 +311,7 @@
         self.offset = {}
         sem = land = 0
         self.sem, self.land = {}, {}
-        for c, chain in enumerate(chains):
+        for c, chain in enumerate(chains[:-1]):
             self.offset[c] = chain["base"] + sum(
                 self.bit(bit) * stride for bit, stride in chain["fixed"]
             )
@@ -277,7 +324,7 @@
 
     @staticmethod
     def needs(chains):
-        steps = [step for chain in chains for step in chain["steps"]]
+        steps = [step for chain in chains[:-1] for step in chain["steps"]]
         return len(steps), sum(step[3] for step in steps if step[0] == "sum")
 
     def bit(self, bit):
@@ -307,7 +354,7 @@
         copy = pltpu.make_async_remote_copy(
             src_ref=source,
             dst_ref=target,
-            send_sem=self.send_sems.at[self.sem[c, k]],
+            send_sem=self.send_sems.at[c],
             recv_sem=self.recv_sems.at[self.sem[c, k]],
             device_id=self.partner(bit),
             device_id_type=MESH,
@@ -361,7 +408,7 @@
             chains, self.work, self.landing, self.total, self.sum_send, self.sum_recv
         )
         self.at = 0
-        self.loads = {}
+        self.loads, self.stores = {}, []
 
     def run(self):
         self.enter()
@@ -394,7 +441,17 @@
             )
         self.have("x")
         rows_by_three(z, self.x_v, self.xf)
+        self.xf[:, :, 0:8, :] = jnp.zeros((z.items, z.width // LANES, 8, LANES), jnp.float32)
+        self.have("pool_w")
+        self.pooled[...] = self.pool(2)
         pl.semaphore_wait(barrier, z.n - 1 + len(batch))
+
+    def pool(self, part):
+        width = self.z.width
+        return dot(
+            low(every_third(self.z, self.xf, 6 + part)),
+            self.pool_w_v[part * width : (part + 1) * width, :],
+        )
 
     def have(self, *names):
         for name in names:
@@ -413,10 +470,8 @@
         copy.start()
         return copy
 
-    def exchange(self, source, target, send, recv):
-        copies = send_all(self.z.n, self.me, lambda peer: source.at[peer], target, send, recv)
-        target[self.me] = source[self.me]
-        return copies
+    def exchange(self, source, target, sems):
+        return Exchange(self.z.n, self.me, source, target, sems)
 
     def by_head(self, target, values):
         z = self.z
@@ -451,18 +506,16 @@
         halo = self.neighbour(
             self.x_v.at[:, 3 * r - 16 :, :], self.halo, self.halo_sems, 1
         )
-        self.have("pool_w")
-        pooled = dot(low(every_third(z, self.xf, 8)), self.pool_w_v[2 * width :, :])
+        pooled = self.pooled[...] + self.pool(0) + self.pool(1)
         halo.wait()
+        before = jnp.where(me > 0, self.halo[...].astype(jnp.float32), 0.0)
+        before = low(before.reshape(z.items * 16, width))
+        parts = [dot(before, self.pool_w_v[part * width : (part + 1) * width, :]) for part in (0, 1)]
+        row = lax.broadcasted_iota(jnp.int32, (z.rows, 1), 0)
         for item in range(z.items):
-            before = jnp.where(me > 0, self.halo[item].astype(jnp.float32), 0.0)
-            for slab in range(width // LANES):
-                self.xf[item, slab, 0:8, :] = before[8:16, slab * LANES : (slab + 1) * LANES]
-        for part in range(2):
-            pooled += dot(
-                low(every_third(z, self.xf, 6 + part)),
-                self.pool_w_v[part * width : (part + 1) * width, :],
-            )
+            at = item * 16 + 14
+            extra = parts[0][at : at + 1, :] + parts[1][at + 1 : at + 2, :]
+            pooled += jnp.where(row == item * r, extra, 0.0)
         self.short[...] = low(pooled)
         normed, inverse = norm_rows(self.short[...].astype(jnp.float32))
         self.normed1[...] = normed
@@ -473,7 +526,7 @@
         qkv = [low(dot(attn_in, w[...])) for w in (self.query_w_v, self.key_w_v, self.value_w_v)]
         for target in range(z.n):
             self.qkv_out[target] = self.by_head(target, qkv)
-        copies = self.exchange(self.qkv_out, self.qkv_in, self.qkv_send, self.qkv_recv)
+        copies = self.exchange(self.qkv_out, self.qkv_in, self.qkv_sems)
         self.have("og", "up_w", "outer_w")
         rows_by_three(z, self.og_v, self.of)
         for part in range(3):
@@ -491,8 +544,7 @@
         pair = pl.ds(pl.multiple_of(lax.div(first, LANES) * LANES, LANES), LANES)
         both = dot(self.table_v[...], self.position_w_v[:, pair])
         self.pos[...] = low(pltpu.roll(both, LANES - lax.rem(first, LANES), 1)[:, : z.hd])
-        for copy in copies:
-            copy.wait()
+        copies.wait()
 
     def attend(self):
         z, r, hd = self.z, self.z.r, self.z.hd
@@ -529,10 +581,9 @@
             self.att_out[block * per : (block + 1) * per] = jnp.concatenate(
                 sides, axis=1
             ).reshape(per, r, LANES)
-        copies = self.exchange(self.att_out, self.att_in, self.att_send, self.att_recv)
+        copies = self.exchange(self.att_out, self.att_in, self.att_sems)
         self.have("output_w", "gain2", "bias2", "inner_w")
-        for copy in copies:
-            copy.wait()
+        copies.wait()
 
     def feed_forward(self):
         z, width = self.z, self.z.width
@@ -563,32 +614,33 @@
         att_grad = low(dot_nt(self.branch[...], self.output_w_v[...]))
         for target in range(z.n):
             self.grad_out[target] = self.by_head(target, [att_grad])
-        self.copies = self.exchange(self.grad_out, self.grad_in, self.grad_send, self.grad_recv)
+        self.copies = self.exchange(self.grad_out, self.grad_in, self.grad_sems)
         row = 0
         for lo in range(0, ff, width):
+            self.reach("unit")
             self.work[row : row + width, :] = low(
                 dot_tn(self.act[:, lo : lo + width], self.summed_grad[...])
             )
             row += width
-            self.advance(0.6 * row / width)
         for lo in range(0, ff, width):
+            self.reach("unit")
             self.work[row : row + width, :] = low(
                 dot_tn(self.ffn_in[...], self.inner_grad[:, lo : lo + width])
             )
             row += width
-            self.advance(0.6 * row / width)
+        self.reach("unit")
         self.work[row : row + width, :] = low(dot_tn(self.att[...], self.branch[...]))
         row += width
         self.summed[...] = low(self.hidden[...] + dot(self.act[...], self.outer_w_v[...]))
         for lo in range(0, 3 * width, width):
+            self.reach("unit")
             self.work[row : row + width, :] = low(
                 dot_tn(self.summed[...], self.up_rows[:, lo : lo + width])
             )
             row += width
-            self.advance(1.8 + 0.6 * row / width)
         self.row = row
-        for copy in self.copies:
-            copy.wait()
+        self.reach("grad")
+        self.copies.wait()
 
     def upsample(self):
         z, width = self.z, self.z.width
@@ -615,10 +667,10 @@
         self.key_t[...] = jnp.zeros_like(self.key_t)
         self.value_t[...] = jnp.zeros_like(self.value_t)
         self.table_t[...] = jnp.zeros_like(self.table_t)
-        now = EARLY_DONE
         for unit in range(z.units):
             att_grad = self.grad_in[:, :, unit * hd : (unit + 1) * hd].reshape(length, hd)
             for block in range(length // BLOCK):
+                self.reach("block")
                 lo, hi = block * BLOCK, (block + 1) * BLOCK
                 block_grad = att_grad[lo:hi]
                 probs = self.probs[unit, lo:hi, :hi]
@@ -638,8 +690,7 @@
                 content_sum += jnp.sum(content, axis=0, keepdims=True)
                 position_sum += jnp.sum(position, axis=0, keepdims=True)
                 self.query_grad[unit, lo:hi, :] = low(content + position)
-                now += 1.2
-                self.advance(now)
+        self.reach("send")
         own = lax.broadcasted_iota(jnp.int32, (1, z.width), 1) // hd == self.head
         for row, value in ((4, content_sum), (5, position_sum)):
             spread = jnp.concatenate([value] * z.heads, axis=1)
@@ -649,23 +700,24 @@
         sides += [low(self.key_t[unit].T) for unit in range(z.units)] + pad
         sides += [low(self.value_t[unit].T) for unit in range(z.units)] + pad
         self.back_out[...] = jnp.concatenate(sides, axis=1).reshape(z.n, r, 3 * LANES)
-        copies = self.exchange(self.back_out, self.back_in, self.back_send, self.back_recv)
+        copies = self.exchange(self.back_out, self.back_in, self.back_sems)
+        self.reach("table")
         table_sum = 0.0
         for unit in range(z.units):
             table_sum += dot(low(self.table_t[unit]), self.table_v[...])
         half = hd // 2
-        base = self.chains[-1]["base"]
+        base = self.chains[-2]["base"]
         for side in range(2):
             at = pl.multiple_of(base + side * z.heads * half + self.head * half, 16)
             self.work[pl.ds(at, half), :] = low(table_sum[side * half : (side + 1) * half])
-        self.advance(BACK_DONE)
+        self.reach("up")
         self.upsample()
-        self.advance(BACK_DONE + 4.0)
-        for copy in copies:
-            copy.wait()
+        self.reach("back")
+        copies.wait()
 
     def finish_rows(self):
         z, me, r, width = self.z, self.me, self.z.r, self.z.width
+        self.reach("rows")
         for which in range(3):
             self.to_rows(self.back_in, which, self.row_grad.at[which])
         attn_grad = (
@@ -685,12 +737,12 @@
             self.first_rows[item] = short_grad[item * r : item * r + 16, :]
             self.later[item, 0:r, :] = short_grad[item * r : (item + 1) * r, :].astype(jnp.float32)
         halo = self.neighbour(self.first_rows, self.next_rows, self.next_sems, z.n - 1)
-        self.small_start(0)
         row = self.row
+        self.reach("qkv")
         for which in range(3):
             self.work[row : row + width, :] = low(dot_tn(self.attn_in[...], self.row_grad[which]))
             row += width
-        self.advance(LATE[0])
+        self.reach("pool")
         own = dot_nt(short_grad, self.pool_w_v[2 * width :, :])
         set_every_third(z, self.of, 8, every_third(z, self.of, 8) + own)
         self.work[row + 2 * width : row + 3 * width, :] = low(
@@ -706,7 +758,7 @@
         for part in range(2):
             cut = slice(row + part * width, row + (part + 1) * width)
             self.work[cut, :] = low(dot_tn(low(every_third(z, self.xf, 9 + part)), later))
-        self.advance(LATE[1])
+        self.reach("input")
         for part in range(2):
             back = dot_nt(later, self.pool_w_v[part * width : (part + 1) * width, :])
             first = 9 + part
@@ -721,11 +773,37 @@
         )
         self.input_store.start()
 
-    def advance(self, now):
-        while self.at < len(self.plan) and self.plan[self.at][0] <= now:
-            _, c, k = self.plan[self.at]
-            self.sums.start(c, k)
+    def reach(self, name=None):
+        while self.at < len(self.plan):
+            kind, c, k = self.plan[self.at]
             self.at += 1
+            if kind == "seg":
+                assert k == name
+                return
+            if c == len(self.chains) - 1:
+                self.small(k)
+            elif kind == "sum":
+                self.sums.start(c, k)
+            else:
+                self.sums.finish(c, k - 1)
+                at, size = self.chains[c]["base"], self.chains[c]["all"]
+                self.stores.append(
+                    pltpu.make_async_copy(
+                        self.total.at[at : at + size],
+                        self.total_out.at[at : at + size],
+                        self.store_sems.at[c],
+                    )
+                )
+                self.stores[-1].start()
+
+    def small(self, k):
+        if k:
+            self.small_copy.wait()
+            self.small_work[k] = self.small_work[k - 1] + self.small_landing[k - 1]
+        if k < len(self.bits):
+            self.small_start(k)
+        else:
+            self.small_total[...] = self.small_work[k]
 
     def small_start(self, k):
         self.small_copy = pltpu.make_async_remote_copy(
@@ -739,34 +817,8 @@
         self.small_copy.start()
 
     def finish_sums(self):
-        steps = len(self.bits)
-        first = self.plan[self.at][0] if self.at < len(self.plan) else 0.0
-        for k in range(steps):
-            self.advance(first + 3.0 * (k + 1))
-            self.small_copy.wait()
-            self.small_work[k + 1] = self.small_work[k] + self.small_landing[k]
-            if k + 1 < steps:
-                self.small_start(k + 1)
-        self.small_total[...] = self.small_work[steps]
-        ends = {}
-        for order, (_, c, k) in enumerate(self.plan):
-            ends[c] = order
-        stores = []
-        for c in sorted(ends, key=ends.get):
-            while self.at <= ends[c]:
-                self.sums.start(*self.plan[self.at][1:])
-                self.at += 1
-            self.sums.finish(c, len(self.chains[c]["steps"]) - 1)
-            at, size = self.chains[c]["base"], self.chains[c]["all"]
-            stores.append(
-                pltpu.make_async_copy(
-                    self.total.at[at : at + size],
-                    self.total_out.at[at : at + size],
-                    self.store_sems.at[c],
-                )
-            )
-            stores[-1].start()
-        for store in stores + [self.block_store, self.input_store]:
+        self.reach()
+        for store in self.stores + [self.block_store, self.input_store]:
             store.wait()
 
 
@@ -777,27 +829,32 @@
 def chains_of(z, ff, nb):
     width = z.width
     copies = Copies(nb, z.n)
-    orders = copies.orders()
-    units = 3 * (ff * 2 + width * 10) // width // 3
     early = 2 * ff // width + 4
-    chosen = CHAINS if len(copies.bits) == 5 and sum(rows for rows, _ in CHAINS) == units else None
-    if chosen is None:
-        chosen = [(1, k) for k in range(units)]
+    units = early + 6
+    searched = len(copies.bits) == 5 and sum(rows for rows, _ in CHAINS) == units
+    chosen = CHAINS if searched else [(1, k) for k in range(units)]
     chains, base = [], 0
-    for rows, order in chosen:
-        chains.append(copies.halving(rows * width, orders[order % len(orders)], base * width))
+    for rows, name in chosen:
+        order = copies.order(name) if searched else copies.rotated(name)
+        chains.append(copies.halving(rows * width, order, base * width))
         chains[-1]["all"] = rows * width
         base += rows
-        if base <= early - 3:
-            chains[-1]["ready"] = 0.6 * base
-        elif base <= early:
-            chains[-1]["ready"] = 1.8 + 0.6 * base
-        else:
-            chains[-1]["ready"] = LATE[0] if base <= early + 3 else LATE[1]
+        chains[-1]["units"] = base
     chains.append(copies.by_head(z.heads, z.hd, base * width))
     chains[-1]["all"] = z.heads * z.hd
-    chains[-1]["ready"] = BACK_DONE
-    return copies, chains
+    chains.append({"steps": [("small", bit, 0, 16) for bit in copies.bits]})
+    blocks = z.units * z.length // BLOCK
+
+    def done(first, last):
+        return [c for c, chain in enumerate(chains) if first < chain.get("units", 0) <= last]
+
+    segments = [("unit", UNIT, done(unit, unit + 1)) for unit in range(early)]
+    segments += [("grad", 0.0, [])] + [("block", BLOCK_STEP, [])] * blocks
+    segments += [("send", SEND, []), ("table", TABLE, [len(chains) - 2]), ("up", UP, [])]
+    segments += [("back", 0.0, []), ("rows", ROWS, [len(chains) - 1])]
+    segments += [("qkv", QKV, done(early, early + 3)), ("pool", POOL, done(early + 3, units))]
+    segments += [("input", INPUT, [])]
+    return copies, chains, segments
 
 
 def result_kernel(
@@ -826,14 +883,16 @@
     up_ref,
     held,
     wide,
+    block_held,
+    input_held,
     load_sems,
     store_sems,
     pass_sems,
 ):
     width = z.width
     through = [
-        pltpu.make_async_copy(block_in_ref, block_ref, pass_sems.at[0]),
-        pltpu.make_async_copy(input_in_ref, input_ref, pass_sems.at[1]),
+        pltpu.make_async_copy(block_in_ref, block_held, pass_sems.at[0]),
+        pltpu.make_async_copy(input_in_ref, input_held, pass_sems.at[1]),
     ]
     blocks = held.shape[0]
     loads = [
@@ -842,7 +901,7 @@
         )
         for k in range(blocks)
     ]
-    for copy in loads + through:
+    for copy in through + loads:
         copy.start()
     places = [outer_ref.at[k * width : (k + 1) * width] for k in range(ff // width)]
     places += [inner_ref.at[:, k * width : (k + 1) * width] for k in range(ff // width)]
@@ -860,6 +919,12 @@
         content_bias_ref[head : head + 1, :] = small_ref[4:5, lanes]
         position_bias_ref[head : head + 1, :] = small_ref[5:6, lanes]
     stores = []
+    for which, (source, target) in enumerate(
+        ((block_held, block_ref), (input_held, input_ref))
+    ):
+        through[which].wait()
+        stores.append(pltpu.make_async_copy(source, target, pass_sems.at[2 + which]))
+        stores[-1].start()
     for k in range(blocks):
         loads[k].wait()
         if k + 1 < blocks:
@@ -874,7 +939,7 @@
                 wide[k, :, head * z.hd : (head + 1) * z.hd] = both.T
         stores.append(pltpu.make_async_copy(wide.at[k], places[k], store_sems.at[k]))
         stores[-1].start()
-    for copy in stores + through:
+    for copy in stores:
         copy.wait()
 
 
@@ -907,16 +972,11 @@
     bf, f4 = jnp.bfloat16, jnp.float32
     slabs = width // LANES
     dma = pltpu.SemaphoreType.DMA
-    copies, chains = chains_of(z, ff, lax.axis_size("batch"))
-    near = 16 * n * 0.001
-    holds = [
-        (0.0, {("seq", 1): 0.7 * near * 16, "line": 1.4 * near * 16}),
-        (BACK_DONE - 2.0, {("seq", 1): 2.1 * near * 16, "line": 4.2 * near * 16}),
-    ]
-    plan = copies.schedule(chains, width, holds)
+    copies, chains, segments = chains_of(z, ff, lax.axis_size("batch"))
+    plan = copies.schedule(chains, width, segments, r * LANES * 2)
     bits = copies.bits
     count, landing = Sums.needs(chains)
-    total_rows = chains[-1]["base"] + chains[-1]["all"]
+    total_rows = chains[-2]["base"] + chains[-2]["all"]
     operands = {
         "x": byte_rows,
         "pool_w": pool_weight,
@@ -955,6 +1015,7 @@
         first_rows=pltpu.VMEM((items, 16, width), bf),
         next_rows=pltpu.VMEM((items, 16, width), bf),
         later=pltpu.VMEM((items, r + 8, width), f4),
+        pooled=pltpu.VMEM((rows, width), f4),
         short=pltpu.VMEM((rows, width), bf),
         normed1=pltpu.VMEM((rows, width), f4),
         inverse1=pltpu.VMEM((rows, 1), f4),
@@ -997,19 +1058,15 @@
         load_sems=dma((len(OPERANDS),)),
         halo_sems=dma((2,)),
         next_sems=dma((2,)),
-        qkv_send=dma((n,)),
-        qkv_recv=dma((n,)),
-        att_send=dma((n,)),
-        att_recv=dma((n,)),
-        grad_send=dma((n,)),
-        grad_recv=dma((n,)),
-        back_send=dma((n,)),
-        back_recv=dma((n,)),
-        sum_send=dma((count,)),
+        qkv_sems=dma((2,)),
+        att_sems=dma((2,)),
+        grad_sems=dma((2,)),
+        back_sems=dma((2,)),
+        sum_send=dma((len(chains) - 1,)),
         sum_recv=dma((count,)),
         small_send=dma((len(bits),)),
         small_recv=dma((len(bits),)),
-        store_sems=dma((len(chains),)),
+        store_sems=dma((len(chains) - 1,)),
         out_sems=dma((2,)),
     )
     names = ("lengths",) + OPERANDS + tuple(outs) + tuple(scratch)
@@ -1051,11 +1108,13 @@
         scratch_shapes=[
             pltpu.VMEM((blocks, width, width), bf),
             pltpu.VMEM((blocks, width, width), f4),
+            pltpu.VMEM(byte_rows.shape, bf),
+            pltpu.VMEM(byte_rows.shape, f4),
             dma((blocks,)),
             dma((blocks,)),
-            dma((2,)),
+            dma((4,)),
         ],
-        compiler_params=pltpu.CompilerParams(vmem_limit_bytes=50 * 2**20),
+        compiler_params=pltpu.CompilerParams(vmem_limit_bytes=62 * 2**20),
     )(total, small_t, block_out, input_grad)
     return tuple(
         value.reshape(width) if value.shape == (1, width) else value for value in results

time: 166 us -> 130 us (0.78)
  Pallas kernels: 162 us -> 129 us
  local copies, waits for them, and re-layouts: 2.84 us -> 0 us
    pallas_call x1, Pallas kernels: 151 us -> 116 us  [body(): pl.pallas_call(functools.partial(block_kernel, z, plan, chains, bits, nam...]
    unnamed x6 -> x0, local copies, waits for them, and re-layouts: 2.84 us -> none
where the time goes in v5:
time: 130 us
  Pallas kernels  129 us (99%)
    pallas_call x1, Pallas kernels, body(): pl.pallas_call(functools.partial(block_kernel, z, plan, chains, bits, nam...  116 us
    pallas_call x1, Pallas kernels, body(): pl.pallas_call(functools.partial(result_kernel, z, ff), out_shape=[jax.Sh...  12.9 us

profile of v5, /device:TPU:0, one launch (start us, length us, event | category | flops | bytes accessed | tf_op | source)
XLA Modules:
  0.0 130.2 jit_solution(5738215702450382976)
XLA Ops:
  0.7 116.5 %shard_map.314 = (bf16[2,192,512]{2,1,0:T(8,128)(2,1)}, f32[2,192,512]{2,1,0:T(8,128)}, bf16[9728,512]{1,0:T(8,128)(2,1)}, f32[8,512]{1,0:T(8,128)}) custom-call(s32[2]{0:T(128)} %refs_0_.1, bf16[2,192,512]{2,1,0:T(8,128)(2,1)} %refs_1_.1, bf16[1536,512]{1,0:T(8,128)(2,1)} %refs_2_.1, f32[1,512]{1,0:T(1,128)} %bitcast.8, f32[1,512]{1,0:T(1,128)} %bitcast.9, ...), custom_call_target="tpu_custom_call" | custom-call | tf_op jit(solution)/shard_map/pallas_call | solution.py:1073
  117.1 12.9 %shard_map.315 = (bf16[2,192,512]{2,1,0:T(8,128)(2,1)}, f32[2,192,512]{2,1,0:T(8,128)}, f32[1536,512]{1,0:T(8,128)}, f32[1,512]{1,0:T(1,128)}, f32[1,512]{1,0:T(...) custom-call(bf16[9728,512]{1,0:T(8,128)(2,1)} %get-tuple-element.38., ...), custom_call_target="tpu_custom_call" | custom-call | tf_op jit(solution)/shard_map/pallas_call | solution.py:1103

commit v6 on v5

--- a/solution.py
+++ b/solution.py
@@ -12,23 +12,23 @@
 epsilon = 1e-05
 masked_value = -1e30
 CHAINS = (
-    (1, "z1xyz0"),
-    (2, "xyz0z1"),
-    (1, "z0z1yx"),
-    (2, "yxz0z1"),
-    (1, "z0yz1x"),
-    (1, "yxz0z1"),
-    (2, "xyz0z1"),
-    (1, "yxz1z0"),
-    (1, "z0xyz1"),
-    (1, "xyz0z1"),
-    (1, "yxz0z1"),
-    (1, "yxz1z0"),
-    (1, "yxz0z1"),
-    (1, "xyz1z0"),
-    (1, "xyz0z1"),
+    (1, "yxz0z1", -1),
+    (2, "z0yz1x", -4),
+    (1, "xyz0z1", 13),
+    (1, "xyz0z1", 2),
+    (2, "yxz0z1", 20),
+    (1, "xz0yz1", 1),
+    (1, "xyz1z0", 6),
+    (1, "z0yxz1", 1),
+    (2, "xyz0z1", 4),
+    (1, "yxz0z1", 1),
+    (1, "xz0yz1", 11),
+    (1, "yxz0z1", -3),
+    (1, "xyz1z0", -2),
+    (1, "yxz0z1", 5),
+    (1, "xyz0z1", -5),
 )
-LAG, CORE_LAG, ISSUE, MARGIN = 2.8, 1.0, 0.15, 0.3
+LAG, CORE_LAG, ISSUE, MARGIN = 2.6, 1.0, 0.15, 0.1
 UNIT, BLOCK_STEP, SEND, TABLE, UP, ROWS, QKV, POOL, INPUT = 0.33, 0.7, 0.3, 0.4, 1.5, 2.2, 0.9, 1.6, 1.2
 BLOCK = 128
 LANES = 128
@@ -146,6 +146,16 @@
             xf_ref[item, slab, pl.ds(first, z.r, stride=3), :] = value[
                 item * z.r : (item + 1) * z.r, slab * LANES : (slab + 1) * LANES
             ]
+
+
+def fold(value):
+    half = value.shape[-2] // 2
+    return jnp.concatenate([value[..., :half, :], value[..., half:, :]], axis=-1)
+
+
+def unfold(value):
+    half = value.shape[-1] // 2
+    return jnp.concatenate([value[..., :half], value[..., half:]], axis=-2)
 
 
 def live_rows(z, me, length, part):
@@ -245,6 +255,7 @@
                 free[link] = max(free.get(link, 0.0), now) + busy
             sent[name] = max(free[link] for link in self.hold(size)) + LAG + 0.5
 
+        sends = sum(name == "send" for name, _, _ in segments)
         hold("grad", 1)
         while True:
             best, later = None, []
@@ -258,7 +269,7 @@
                     cost = self.cost(bit, 2 * rows * width)
                     start = max([ready[c] + (MARGIN if at[c] else 0.0)] + [free.get(link, 0.0) - 0.3 for link in cost])
                 if start <= now:
-                    key = (-left[c][at[c]], c)
+                    key = (-left[c][at[c]] - chain.get("bias", 0), c)
                     best = key if best is None or key < best else best
                 else:
                     later.append(start)
@@ -291,7 +302,7 @@
                     for c in releases:
                         ready[c] = now
                     if name == "send":
-                        hold("back", 3)
+                        hold("back", 3 / sends)
                     segment += 1
                     continue
                 later.append(due)
@@ -408,7 +419,7 @@
             chains, self.work, self.landing, self.total, self.sum_send, self.sum_recv
         )
         self.at = 0
-        self.loads, self.stores = {}, []
+        self.loads = {}
 
     def run(self):
         self.enter()
@@ -439,12 +450,10 @@
             pl.semaphore_signal(
                 barrier, inc=1, device_id=self.sums.partner(bit), device_id_type=MESH
             )
-        self.have("x")
-        rows_by_three(z, self.x_v, self.xf)
-        self.xf[:, :, 0:8, :] = jnp.zeros((z.items, z.width // LANES, 8, LANES), jnp.float32)
-        self.have("pool_w")
-        self.pooled[...] = self.pool(2)
         pl.semaphore_wait(barrier, z.n - 1 + len(batch))
+        self.before = self.neighbour(
+            self.x.at[:, 3 * z.r - 16 :, :], self.halo, self.halo_sems, 1
+        )
 
     def pool(self, part):
         width = self.z.width
@@ -470,31 +479,40 @@
         copy.start()
         return copy
 
-    def exchange(self, source, target, sems):
-        return Exchange(self.z.n, self.me, source, target, sems)
-
-    def by_head(self, target, values):
+    def exchange(self, name, unit):
+        source, target, sems = (getattr(self, name + end) for end in ("_out", "_in", "_sems"))
+        return Exchange(
+            self.z.n, self.me, source.at[unit], target.at[unit], sems.at[unit]
+        )
+
+    def part(self, value, target, unit):
         z = self.z
-        pad = [jnp.zeros((z.r, z.hd), jnp.bfloat16)] * (LANES // z.hd - z.units)
-        lanes = slice(target % z.heads * z.hd, (target % z.heads + 1) * z.hd)
-        sides = []
-        for value in values:
-            for unit in range(z.units):
-                item = target // z.heads * z.units + unit
-                sides.append(value[item * z.r : (item + 1) * z.r, lanes])
-            sides += pad
-        return jnp.concatenate(sides, axis=1)
-
-    def to_rows(self, source_ref, which, target_ref):
+        item = target // z.heads * z.units + unit
+        head = target % z.heads
+        return value[item * z.r : (item + 1) * z.r, head * z.hd : (head + 1) * z.hd]
+
+    def to_rows(self, name, parts, target_refs):
         z = self.z
-        for source in range(z.n):
-            for unit in range(z.units):
+        source_ref = getattr(self, name + "_in")
+        for unit in range(z.units):
+            for source in range(z.n):
                 item = source // z.heads * z.units + unit
                 head = source % z.heads
-                first = which * LANES + unit * z.hd
-                target_ref[item * z.r : (item + 1) * z.r, head * z.hd : (head + 1) * z.hd] = (
-                    source_ref[source, :, first : first + z.hd]
-                )
+                rows = slice(item * z.r, (item + 1) * z.r)
+                lanes = slice(head * z.hd, (head + 1) * z.hd)
+                for value, target_ref in zip(parts(source_ref[unit, source]), target_refs):
+                    target_ref[rows, lanes] = value
+
+    def pack(self, first, second, third):
+        return jnp.concatenate([jnp.concatenate([first, second], axis=-1), fold(third)], axis=-2)
+
+    def unpack(self, value):
+        z = self.z
+        return (
+            value[..., : z.r, : z.hd],
+            value[..., : z.r, z.hd :],
+            unfold(value[..., z.r :, :]),
+        )
 
     def live(self, part):
         z = self.z
@@ -503,11 +521,12 @@
 
     def project(self):
         z, me, r, width = self.z, self.me, self.z.r, self.z.width
-        halo = self.neighbour(
-            self.x_v.at[:, 3 * r - 16 :, :], self.halo, self.halo_sems, 1
-        )
-        pooled = self.pooled[...] + self.pool(0) + self.pool(1)
-        halo.wait()
+        self.have("x")
+        rows_by_three(z, self.x_v, self.xf)
+        self.xf[:, :, 0:8, :] = jnp.zeros((z.items, width // LANES, 8, LANES), jnp.float32)
+        self.have("pool_w")
+        pooled = self.pool(0) + self.pool(1) + self.pool(2)
+        self.before.wait()
         before = jnp.where(me > 0, self.halo[...].astype(jnp.float32), 0.0)
         before = low(before.reshape(z.items * 16, width))
         parts = [dot(before, self.pool_w_v[part * width : (part + 1) * width, :]) for part in (0, 1)]
@@ -524,9 +543,16 @@
         self.attn_in[...] = low(normed * self.gain1_v[...] + self.bias1_v[...])
         attn_in = self.attn_in[...]
         qkv = [low(dot(attn_in, w[...])) for w in (self.query_w_v, self.key_w_v, self.value_w_v)]
-        for target in range(z.n):
-            self.qkv_out[target] = self.by_head(target, qkv)
-        copies = self.exchange(self.qkv_out, self.qkv_in, self.qkv_sems)
+        self.moves = []
+
+        def send(unit):
+            for target in range(z.n):
+                self.qkv_out[unit, target] = self.pack(
+                    *(self.part(value, target, unit) for value in qkv)
+                )
+            self.moves.append(self.exchange("qkv", unit))
+
+        send(0)
         self.have("og", "up_w", "outer_w")
         rows_by_three(z, self.og_v, self.of)
         for part in range(3):
@@ -534,6 +560,8 @@
                 every_third(z, self.of, 8 + part) * self.live(part)
             )
         self.summed_grad[...] = low(dot_nt(self.up_rows[...], self.up_w_v[...]))
+        for unit in range(1, z.units):
+            send(unit)
         ff = self.outer_w_v.shape[0]
         for lo in range(0, ff, width):
             self.act_grad[:, lo : lo + width] = dot_nt(
@@ -544,27 +572,24 @@
         pair = pl.ds(pl.multiple_of(lax.div(first, LANES) * LANES, LANES), LANES)
         both = dot(self.table_v[...], self.position_w_v[:, pair])
         self.pos[...] = low(pltpu.roll(both, LANES - lax.rem(first, LANES), 1)[:, : z.hd])
-        copies.wait()
 
     def attend(self):
-        z, r, hd = self.z, self.z.r, self.z.hd
+        z, hd = self.z, self.z.hd
         content_bias = self.content_bias_v[pl.ds(self.head, 1), :]
         position_bias = self.position_bias_v[pl.ds(self.head, 1), :]
+        moves = []
         for unit in range(z.units):
+            self.moves[unit].wait()
             queries, keys, values = (
-                self.qkv_in[:, :, which * LANES + unit * hd : which * LANES + (unit + 1) * hd]
-                .reshape(z.length, hd)
-                for which in range(3)
+                value.reshape(z.length, hd) for value in self.unpack(self.qkv_in[unit])
             )
             self.qc[unit] = low(queries.astype(jnp.float32) + content_bias)
             self.qp[unit] = low(queries.astype(jnp.float32) + position_bias)
             self.keys[unit] = keys
             self.values[unit] = values
-        for block in range(z.length // BLOCK):
-            lo, hi = block * BLOCK, (block + 1) * BLOCK
-            sides = []
-            for unit in range(z.units):
-                length = self.lengths[self.group * z.units + unit]
+            length = self.lengths[self.group * z.units + unit]
+            for block in range(z.length // BLOCK):
+                lo, hi = block * BLOCK, (block + 1) * BLOCK
                 content = dot_nt(self.qc[unit, lo:hi, :], self.keys[unit, :hi, :])
                 by_distance = dot_nt(self.qp[unit, lo:hi, :], self.pos[z.length - hi :, :])
                 placed = pltpu.roll(by_distance, lo + 1, 1, stride=1, stride_axis=0)
@@ -575,20 +600,20 @@
                 raised = jnp.exp(logits - jnp.max(logits, axis=-1, keepdims=True))
                 probs = raised / jnp.sum(raised, axis=-1, keepdims=True)
                 self.probs[unit, lo:hi, :hi] = probs
-                sides.append(low(dot(low(probs), self.values[unit, :hi, :])))
-            sides += [jnp.zeros((BLOCK, hd), jnp.bfloat16)] * (LANES // hd - z.units)
-            per = BLOCK // r
-            self.att_out[block * per : (block + 1) * per] = jnp.concatenate(
-                sides, axis=1
-            ).reshape(per, r, LANES)
-        copies = self.exchange(self.att_out, self.att_in, self.att_sems)
+                attended = low(dot(low(probs), self.values[unit, :hi, :]))
+                per = BLOCK // z.r
+                self.att_out[unit, block * per : (block + 1) * per] = fold(
+                    attended.reshape(per, z.r, hd)
+                )
+            moves.append(self.exchange("att", unit))
         self.have("output_w", "gain2", "bias2", "inner_w")
-        copies.wait()
+        for move in moves:
+            move.wait()
 
     def feed_forward(self):
         z, width = self.z, self.z.width
         ff = self.outer_w_v.shape[0]
-        self.to_rows(self.att_in, 0, self.att)
+        self.to_rows("att", lambda value: [unfold(value)], [self.att])
         hidden = self.short[...].astype(jnp.float32) + dot(self.att[...], self.output_w_v[...])
         normed, inverse = norm_rows(hidden)
         self.hidden[...] = hidden
@@ -612,9 +637,11 @@
         self.hidden_grad[...] = hidden_grad
         self.branch[...] = low(hidden_grad)
         att_grad = low(dot_nt(self.branch[...], self.output_w_v[...]))
-        for target in range(z.n):
-            self.grad_out[target] = self.by_head(target, [att_grad])
-        self.copies = self.exchange(self.grad_out, self.grad_in, self.grad_sems)
+        self.moves = []
+        for unit in range(z.units):
+            for target in range(z.n):
+                self.grad_out[unit, target] = fold(self.part(att_grad, target, unit))
+            self.moves.append(self.exchange("grad", unit))
         row = 0
         for lo in range(0, ff, width):
             self.reach("unit")
@@ -640,7 +667,6 @@
             row += width
         self.row = row
         self.reach("grad")
-        self.copies.wait()
 
     def upsample(self):
         z, width = self.z, self.z.width
@@ -651,24 +677,22 @@
             )
         for item in range(z.items):
             for slab in range(width // LANES):
-                self.block_low[item, :, slab * LANES : (slab + 1) * LANES] = low(
+                self.block_out[item, :, slab * LANES : (slab + 1) * LANES] = low(
                     self.bf[item, slab, 8:, :]
                 )
-        self.block_store = pltpu.make_async_copy(
-            self.block_low, self.block_out, self.out_sems.at[0]
-        )
-        self.block_store.start()
 
     def attend_back(self):
         z, r, hd, length = self.z, self.z.r, self.z.hd, self.z.length
         flip = reversal()
+        moves = []
         content_sum = jnp.zeros((1, hd), jnp.float32)
         position_sum = jnp.zeros((1, hd), jnp.float32)
         self.key_t[...] = jnp.zeros_like(self.key_t)
         self.value_t[...] = jnp.zeros_like(self.value_t)
         self.table_t[...] = jnp.zeros_like(self.table_t)
         for unit in range(z.units):
-            att_grad = self.grad_in[:, :, unit * hd : (unit + 1) * hd].reshape(length, hd)
+            self.moves[unit].wait()
+            att_grad = unfold(self.grad_in[unit]).reshape(length, hd)
             for block in range(length // BLOCK):
                 self.reach("block")
                 lo, hi = block * BLOCK, (block + 1) * BLOCK
@@ -690,17 +714,18 @@
                 content_sum += jnp.sum(content, axis=0, keepdims=True)
                 position_sum += jnp.sum(position, axis=0, keepdims=True)
                 self.query_grad[unit, lo:hi, :] = low(content + position)
-        self.reach("send")
+            self.reach("send")
+            parts = (
+                self.query_grad[unit],
+                low(self.key_t[unit].T),
+                low(self.value_t[unit].T),
+            )
+            self.back_out[unit] = self.pack(*(value.reshape(z.n, r, hd) for value in parts))
+            moves.append(self.exchange("back", unit))
         own = lax.broadcasted_iota(jnp.int32, (1, z.width), 1) // hd == self.head
         for row, value in ((4, content_sum), (5, position_sum)):
             spread = jnp.concatenate([value] * z.heads, axis=1)
             self.small_work[0, row : row + 1, :] = jnp.where(own, spread, 0.0)
-        pad = [jnp.zeros((length, hd), jnp.bfloat16)] * (LANES // hd - z.units)
-        sides = [self.query_grad[unit] for unit in range(z.units)] + pad
-        sides += [low(self.key_t[unit].T) for unit in range(z.units)] + pad
-        sides += [low(self.value_t[unit].T) for unit in range(z.units)] + pad
-        self.back_out[...] = jnp.concatenate(sides, axis=1).reshape(z.n, r, 3 * LANES)
-        copies = self.exchange(self.back_out, self.back_in, self.back_sems)
         self.reach("table")
         table_sum = 0.0
         for unit in range(z.units):
@@ -713,13 +738,13 @@
         self.reach("up")
         self.upsample()
         self.reach("back")
-        copies.wait()
+        for move in moves:
+            move.wait()
 
     def finish_rows(self):
         z, me, r, width = self.z, self.me, self.z.r, self.z.width
         self.reach("rows")
-        for which in range(3):
-            self.to_rows(self.back_in, which, self.row_grad.at[which])
+        self.to_rows("back", self.unpack, [self.row_grad.at[which] for which in range(3)])
         attn_grad = (
             dot_nt(self.row_grad[0], self.query_w_v[...])
             + dot_nt(self.row_grad[1], self.key_w_v[...])
@@ -765,13 +790,9 @@
             set_every_third(z, self.of, first, every_third(z, self.of, first) + back)
         for item in range(z.items):
             for slab in range(width // LANES):
-                self.input_rows[item, :, slab * LANES : (slab + 1) * LANES] = self.of[
+                self.input_grad[item, :, slab * LANES : (slab + 1) * LANES] = self.of[
                     item, slab, 8:, :
                 ]
-        self.input_store = pltpu.make_async_copy(
-            self.input_rows, self.input_grad, self.out_sems.at[1]
-        )
-        self.input_store.start()
 
     def reach(self, name=None):
         while self.at < len(self.plan):
@@ -786,15 +807,6 @@
                 self.sums.start(c, k)
             else:
                 self.sums.finish(c, k - 1)
-                at, size = self.chains[c]["base"], self.chains[c]["all"]
-                self.stores.append(
-                    pltpu.make_async_copy(
-                        self.total.at[at : at + size],
-                        self.total_out.at[at : at + size],
-                        self.store_sems.at[c],
-                    )
-                )
-                self.stores[-1].start()
 
     def small(self, k):
         if k:
@@ -818,8 +830,6 @@
 
     def finish_sums(self):
         self.reach()
-        for store in self.stores + [self.block_store, self.input_store]:
-            store.wait()
 
 
 def block_kernel(z, plan, chains, bits, names, *refs):
@@ -831,26 +841,28 @@
     copies = Copies(nb, z.n)
     early = 2 * ff // width + 4
     units = early + 6
-    searched = len(copies.bits) == 5 and sum(rows for rows, _ in CHAINS) == units
-    chosen = CHAINS if searched else [(1, k) for k in range(units)]
+    searched = len(copies.bits) == 5 and sum(rows for rows, _, _ in CHAINS) == units
+    chosen = CHAINS if searched else [(1, k, 0) for k in range(units)]
     chains, base = [], 0
-    for rows, name in chosen:
+    for rows, name, bias in chosen:
         order = copies.order(name) if searched else copies.rotated(name)
         chains.append(copies.halving(rows * width, order, base * width))
         chains[-1]["all"] = rows * width
+        chains[-1]["bias"] = bias
         base += rows
         chains[-1]["units"] = base
     chains.append(copies.by_head(z.heads, z.hd, base * width))
     chains[-1]["all"] = z.heads * z.hd
     chains.append({"steps": [("small", bit, 0, 16) for bit in copies.bits]})
-    blocks = z.units * z.length // BLOCK
+    blocks = z.length // BLOCK
 
     def done(first, last):
         return [c for c, chain in enumerate(chains) if first < chain.get("units", 0) <= last]
 
     segments = [("unit", UNIT, done(unit, unit + 1)) for unit in range(early)]
-    segments += [("grad", 0.0, [])] + [("block", BLOCK_STEP, [])] * blocks
-    segments += [("send", SEND, []), ("table", TABLE, [len(chains) - 2]), ("up", UP, [])]
+    segments += [("grad", 0.0, [])]
+    segments += ([("block", BLOCK_STEP, [])] * blocks + [("send", SEND, [])]) * z.units
+    segments += [("table", TABLE, [len(chains) - 2]), ("up", UP, [])]
     segments += [("back", 0.0, []), ("rows", ROWS, [len(chains) - 1])]
     segments += [("qkv", QKV, done(early, early + 3)), ("pool", POOL, done(early + 3, units))]
     segments += [("input", INPUT, [])]
@@ -881,28 +893,12 @@
     inner_ref,
     outer_ref,
     up_ref,
-    held,
     wide,
-    block_held,
-    input_held,
-    load_sems,
     store_sems,
     pass_sems,
 ):
     width = z.width
-    through = [
-        pltpu.make_async_copy(block_in_ref, block_held, pass_sems.at[0]),
-        pltpu.make_async_copy(input_in_ref, input_held, pass_sems.at[1]),
-    ]
-    blocks = held.shape[0]
-    loads = [
-        pltpu.make_async_copy(
-            total_ref.at[k * width : (k + 1) * width], held.at[k], load_sems.at[k]
-        )
-        for k in range(blocks)
-    ]
-    for copy in through + loads:
-        copy.start()
+    blocks = wide.shape[0]
     places = [outer_ref.at[k * width : (k + 1) * width] for k in range(ff // width)]
     places += [inner_ref.at[:, k * width : (k + 1) * width] for k in range(ff // width)]
     places += [output_ref]
@@ -920,21 +916,20 @@
         position_bias_ref[head : head + 1, :] = small_ref[5:6, lanes]
     stores = []
     for which, (source, target) in enumerate(
-        ((block_held, block_ref), (input_held, input_ref))
+        ((block_in_ref, block_ref), (input_in_ref, input_ref))
     ):
-        through[which].wait()
-        stores.append(pltpu.make_async_copy(source, target, pass_sems.at[2 + which]))
+        stores.append(pltpu.make_async_copy(source, target, pass_sems.at[which]))
         stores[-1].start()
     for k in range(blocks):
-        loads[k].wait()
         if k + 1 < blocks:
-            wide[k] = held[k].astype(jnp.float32)
+            wide[k] = total_ref[k * width : (k + 1) * width, :].astype(jnp.float32)
         else:
             half = z.hd // 2
             for head in range(z.heads):
-                rows = [
-                    held[k, side * z.heads * half + head * half :][:half] for side in range(2)
-                ]
+                rows = []
+                for side in range(2):
+                    at = k * width + side * z.heads * half + head * half
+                    rows.append(total_ref[at : at + half, :])
                 both = jnp.concatenate(rows, axis=0).astype(jnp.float32)
                 wide[k, :, head * z.hd : (head + 1) * z.hd] = both.T
         stores.append(pltpu.make_async_copy(wide.at[k], places[k], store_sems.at[k]))
@@ -998,9 +993,9 @@
         "inner_w": inner_weight,
     }
     outs = {
-        "block_out": (byte_rows.shape, bf, ANY),
-        "input_grad": (byte_rows.shape, f4, ANY),
-        "total_out": ((total_rows, width), bf, ANY),
+        "block_out": (byte_rows.shape, bf, VMEM),
+        "input_grad": (byte_rows.shape, f4, VMEM),
+        "total": ((total_rows, width), bf, VMEM),
         "small_total": ((8, width), f4, VMEM),
     }
     slab_rows = pltpu.VMEM((items, slabs, 3 * r + 8, LANES), f4)
@@ -1009,25 +1004,22 @@
         xf=slab_rows,
         of=slab_rows,
         bf=slab_rows,
-        block_low=pltpu.VMEM(byte_rows.shape, bf),
-        input_rows=pltpu.VMEM(byte_rows.shape, f4),
         halo=pltpu.VMEM((items, 16, width), bf),
         first_rows=pltpu.VMEM((items, 16, width), bf),
         next_rows=pltpu.VMEM((items, 16, width), bf),
         later=pltpu.VMEM((items, r + 8, width), f4),
-        pooled=pltpu.VMEM((rows, width), f4),
         short=pltpu.VMEM((rows, width), bf),
         normed1=pltpu.VMEM((rows, width), f4),
         inverse1=pltpu.VMEM((rows, 1), f4),
         attn_in=pltpu.VMEM((rows, width), bf),
-        qkv_out=pltpu.VMEM((n, r, 3 * LANES), bf),
-        qkv_in=pltpu.VMEM((n, r, 3 * LANES), bf),
-        att_out=pltpu.VMEM((n, r, LANES), bf),
-        att_in=pltpu.VMEM((n, r, LANES), bf),
-        grad_out=pltpu.VMEM((n, r, LANES), bf),
-        grad_in=pltpu.VMEM((n, r, LANES), bf),
-        back_out=pltpu.VMEM((n, r, 3 * LANES), bf),
-        back_in=pltpu.VMEM((n, r, 3 * LANES), bf),
+        qkv_out=pltpu.VMEM((units, n, 3 * r // 2, 2 * hd), bf),
+        qkv_in=pltpu.VMEM((units, n, 3 * r // 2, 2 * hd), bf),
+        att_out=pltpu.VMEM((units, n, r // 2, 2 * hd), bf),
+        att_in=pltpu.VMEM((units, n, r // 2, 2 * hd), bf),
+        grad_out=pltpu.VMEM((units, n, r // 2, 2 * hd), bf),
+        grad_in=pltpu.VMEM((units, n, r // 2, 2 * hd), bf),
+        back_out=pltpu.VMEM((units, n, 3 * r // 2, 2 * hd), bf),
+        back_in=pltpu.VMEM((units, n, 3 * r // 2, 2 * hd), bf),
         qc=pltpu.VMEM((units, length, hd), bf),
         qp=pltpu.VMEM((units, length, hd), bf),
         keys=pltpu.VMEM((units, length, hd), bf),
@@ -1052,32 +1044,32 @@
         row_grad=pltpu.VMEM((3, rows, width), bf),
         work=pltpu.VMEM((total_rows, width), bf),
         landing=pltpu.VMEM((landing, width), bf),
-        total=pltpu.VMEM((total_rows, width), bf),
         small_work=pltpu.VMEM((len(bits) + 1, 8, width), f4),
         small_landing=pltpu.VMEM((len(bits), 8, width), f4),
         load_sems=dma((len(OPERANDS),)),
         halo_sems=dma((2,)),
         next_sems=dma((2,)),
-        qkv_sems=dma((2,)),
-        att_sems=dma((2,)),
-        grad_sems=dma((2,)),
-        back_sems=dma((2,)),
+        qkv_sems=dma((units, 2)),
+        att_sems=dma((units, 2)),
+        grad_sems=dma((units, 2)),
+        back_sems=dma((units, 2)),
         sum_send=dma((len(chains) - 1,)),
         sum_recv=dma((count,)),
         small_send=dma((len(bits),)),
         small_recv=dma((len(bits),)),
-        store_sems=dma((len(chains) - 1,)),
-        out_sems=dma((2,)),
     )
     names = ("lengths",) + OPERANDS + tuple(outs) + tuple(scratch)
     block_out, input_grad, total, small_t = pl.pallas_call(
         functools.partial(block_kernel, z, plan, chains, bits, names),
-        out_shape=[jax.ShapeDtypeStruct(shape, dtype) for shape, dtype, _ in outs.values()],
+        out_shape=[
+            pltpu.VMEM(shape, dtype) if space is VMEM else jax.ShapeDtypeStruct(shape, dtype)
+            for shape, dtype, space in outs.values()
+        ],
         in_specs=[SMEM] + [ANY] * len(OPERANDS),
         out_specs=[space for _, _, space in outs.values()],
         scratch_shapes=list(scratch.values()),
         compiler_params=pltpu.CompilerParams(
-            collective_id=0, has_side_effects=True, vmem_limit_bytes=60 * 2**20
+            collective_id=0, has_side_effects=True, vmem_limit_bytes=50 * 2**20
         ),
     )(item_lengths, *(operands[name] for name in OPERANDS))
     blocks = total.shape[0] // width
@@ -1103,18 +1095,14 @@
     results = pl.pallas_call(
         functools.partial(result_kernel, z, ff),
         out_shape=[jax.ShapeDtypeStruct(shape, dtype) for shape, dtype, _ in shapes],
-        in_specs=[ANY, VMEM, ANY, ANY],
+        in_specs=[VMEM] * 4,
         out_specs=[space for _, _, space in shapes],
         scratch_shapes=[
-            pltpu.VMEM((blocks, width, width), bf),
             pltpu.VMEM((blocks, width, width), f4),
-            pltpu.VMEM(byte_rows.shape, bf),
-            pltpu.VMEM(byte_rows.shape, f4),
             dma((blocks,)),
-            dma((blocks,)),
-            dma((4,)),
+            dma((2,)),
         ],
-        compiler_params=pltpu.CompilerParams(vmem_limit_bytes=62 * 2**20),
+        compiler_params=pltpu.CompilerParams(vmem_limit_bytes=30 * 2**20),
     )(total, small_t, block_out, input_grad)
     return tuple(
         value.reshape(width) if value.shape == (1, width) else value for value in results

time: 130 us -> 120 us (0.923)
  Pallas kernels: 129 us -> 119 us
    pallas_call x1, Pallas kernels: 116 us -> 111 us  [body(): pl.pallas_call(functools.partial(block_kernel, z, plan, chains, bits, nam...]
    pallas_call x1, Pallas kernels: 12.9 us -> 8.01 us  [body(): pl.pallas_call(functools.partial(result_kernel, z, ff), out_shape=[jax.Sh...]
where the time goes in v6:
time: 120 us
  Pallas kernels  119 us (99%)
    pallas_call x1, Pallas kernels, body(): pl.pallas_call(functools.partial(block_kernel, z, plan, chains, bits, nam...  111 us
    pallas_call x1, Pallas kernels, body(): pl.pallas_call(functools.partial(result_kernel, z, ff), out_shape=[jax.Sh...  8.01 us

profile of v6, /device:TPU:0, one launch (start us, length us, event | category | flops | bytes accessed | tf_op | source)
XLA Modules:
  0.0 120.2 jit_solution(10821949754577326965)
XLA Ops:
  0.7 111.4 %shard_map.314 = (bf16[2,192,512]{2,1,0:T(8,128)(2,1)S(1)}, f32[2,192,512]{2,1,0:T(8,128)S(1)}, bf16[9728,512]{1,0:T(8,128)(2,1)S(1)}, f32[8,512]{1,0:T(8,128)S(1)}) custom-call(s32[2]{0:T(128)} %refs_0_.1, bf16[2,192,512]{2,1,0:T(8,128)(2,1)} %refs_1_.1, bf16[1536,512]{1,0:T(8,128)(2,1)} %refs_2_.1, f32[1,512]{1,0:T(1,128)} %bitcast.8, f32[1,512]{1,0:T(1,128)} %bitcast.9, ...), custom_call_target="tpu_custom_call" | custom-call | tf_op jit(solution)/shard_map/pallas_call | solution.py:1062
  112.0 8.0 %shard_map.315 = (bf16[2,192,512]{2,1,0:T(8,128)(2,1)}, f32[2,192,512]{2,1,0:T(8,128)}, f32[1536,512]{1,0:T(8,128)}, f32[1,512]{1,0:T(1,128)}, f32[1,512]{1,0:T(...) custom-call(bf16[9728,512]{1,0:T(8,128)(2,1)S(1)} %get-tuple-element, ...), custom_call_target="tpu_custom_call" | custom-call | tf_op jit(solution)/shard_map/pallas_call | solution.py:1095

commit v7 on v6

--- a/solution.py
+++ b/solution.py
@@ -12,24 +12,22 @@
 epsilon = 1e-05
 masked_value = -1e30
 CHAINS = (
-    (1, "yxz0z1", -1),
-    (2, "z0yz1x", -4),
-    (1, "xyz0z1", 13),
-    (1, "xyz0z1", 2),
-    (2, "yxz0z1", 20),
-    (1, "xz0yz1", 1),
-    (1, "xyz1z0", 6),
-    (1, "z0yxz1", 1),
-    (2, "xyz0z1", 4),
-    (1, "yxz0z1", 1),
-    (1, "xz0yz1", 11),
-    (1, "yxz0z1", -3),
-    (1, "xyz1z0", -2),
-    (1, "yxz0z1", 5),
-    (1, "xyz0z1", -5),
+    (1, "yxz0z1", 19),
+    (1, "z0z1yx", -15),
+    (2, "xyz0z1", 20),
+    (1, "yz0xz1", 17),
+    (2, "yxz1z0", 20),
+    (2, "z0xyz1", 3),
+    (2, "xyz0z1", 14),
+    (1, "xyz0z1", -8),
+    (1, "xyz0z1", -17),
+    (2, "yxz0z1", 3),
+    (1, "xyz0z1", 7),
+    (1, "yxz1z0", 12),
+    (1, "xyz0z1", 7),
 )
 LAG, CORE_LAG, ISSUE, MARGIN = 2.6, 1.0, 0.15, 0.1
-UNIT, BLOCK_STEP, SEND, TABLE, UP, ROWS, QKV, POOL, INPUT = 0.33, 0.7, 0.3, 0.4, 1.5, 2.2, 0.9, 1.6, 1.2
+UNIT, BRANCH, BLOCK_STEP, SEND, TABLE, UP, ROWS, QKV, POOL, INPUT = 0.33, 0.9, 0.7, 0.3, 0.4, 0.5, 0.7, 0.3, 0.4, 0.4
 BLOCK = 128
 LANES = 128
 VMEM = pl.BlockSpec(memory_space=pltpu.VMEM)
@@ -97,21 +95,21 @@
 
 
 class Exchange:
-    def __init__(self, n, me, source, target, sems):
-        target[me] = source[me]
+    def __init__(self, n, me, source, target, sems, rows):
+        target[me, rows] = source[me, rows]
         for step in range(1, n):
             peer = lax.rem(me + step, n)
             pltpu.make_async_remote_copy(
-                src_ref=source.at[peer],
-                dst_ref=target.at[me],
+                src_ref=source.at[peer, rows],
+                dst_ref=target.at[me, rows],
                 send_sem=sems.at[0],
                 recv_sem=sems.at[1],
                 device_id={"seq": peer},
                 device_id_type=MESH,
             ).start()
         self.all = pltpu.make_async_remote_copy(
-            src_ref=source.at[1:],
-            dst_ref=target.at[1:],
+            src_ref=source.at[1:, rows],
+            dst_ref=target.at[1:, rows],
             send_sem=sems.at[0],
             recv_sem=sems.at[1],
             device_id={"seq": lax.rem(me + 1, n)},
@@ -256,7 +254,6 @@
             sent[name] = max(free[link] for link in self.hold(size)) + LAG + 0.5
 
         sends = sum(name == "send" for name, _, _ in segments)
-        hold("grad", 1)
         while True:
             best, later = None, []
             for c, chain in enumerate(chains):
@@ -301,6 +298,8 @@
                     now += busy
                     for c in releases:
                         ready[c] = now
+                    if name == "branch":
+                        hold("grad", 1)
                     if name == "send":
                         hold("back", 3 / sends)
                     segment += 1
@@ -479,11 +478,11 @@
         copy.start()
         return copy
 
-    def exchange(self, name, unit):
-        source, target, sems = (getattr(self, name + end) for end in ("_out", "_in", "_sems"))
-        return Exchange(
-            self.z.n, self.me, source.at[unit], target.at[unit], sems.at[unit]
-        )
+    def exchange(self, name, unit, rows=None, sems=None):
+        source, target = (getattr(self, name + end).at[unit] for end in ("_out", "_in"))
+        sems = getattr(self, name + "_sems").at[unit if sems is None else sems]
+        rows = slice(0, source.shape[1]) if rows is None else rows
+        return Exchange(self.z.n, self.me, source, target, sems, rows)
 
     def part(self, value, target, unit):
         z = self.z
@@ -504,15 +503,16 @@
                     target_ref[rows, lanes] = value
 
     def pack(self, first, second, third):
-        return jnp.concatenate([jnp.concatenate([first, second], axis=-1), fold(third)], axis=-2)
+        pair, folded = jnp.concatenate([first, second], axis=-1), fold(third)
+        parts = [pair[..., 16:, :], folded[..., 16:, :], pair[..., :16, :], folded[..., :16, :]]
+        return jnp.concatenate(parts, axis=-2)
 
     def unpack(self, value):
-        z = self.z
-        return (
-            value[..., : z.r, : z.hd],
-            value[..., : z.r, z.hd :],
-            unfold(value[..., z.r :, :]),
-        )
+        r, hd = self.z.r, self.z.hd
+        late = 3 * r // 2 - 32
+        pair = jnp.concatenate([value[..., late : late + 16, :], value[..., : r - 16, :]], axis=-2)
+        folded = [value[..., late + 16 :, :], value[..., r - 16 : late, :]]
+        return pair[..., :hd], pair[..., hd:], unfold(jnp.concatenate(folded, axis=-2))
 
     def live(self, part):
         z = self.z
@@ -526,33 +526,57 @@
         self.xf[:, :, 0:8, :] = jnp.zeros((z.items, width // LANES, 8, LANES), jnp.float32)
         self.have("pool_w")
         pooled = self.pool(0) + self.pool(1) + self.pool(2)
+        self.have("gain1", "bias1", "query_w", "key_w", "value_w")
+        weights = (self.query_w_v, self.key_w_v, self.value_w_v)
+
+        def normalize(rows):
+            short = low(rows)
+            normed, inverse = norm_rows(short.astype(jnp.float32))
+            attn_in = low(normed * self.gain1_v[...] + self.bias1_v[...])
+            return short, normed, inverse, attn_in
+
+        kept = (self.short, self.normed1, self.inverse1, self.attn_in)
+        for ref, value in zip(kept, normalize(pooled)):
+            ref[...] = value
+        qkv = [low(dot(self.attn_in[...], w[...])) for w in weights]
+        late = 3 * r // 2 - 32
+        self.moves = []
+
+        def fill(unit):
+            for target in range(z.n):
+                self.qkv_out[unit, target] = self.pack(
+                    *(self.part(value, target, unit) for value in qkv)
+                )
+
+        fill(0)
+        self.moves.append([self.exchange("qkv", 0, slice(0, late))])
         self.before.wait()
         before = jnp.where(me > 0, self.halo[...].astype(jnp.float32), 0.0)
         before = low(before.reshape(z.items * 16, width))
         parts = [dot(before, self.pool_w_v[part * width : (part + 1) * width, :]) for part in (0, 1)]
-        row = lax.broadcasted_iota(jnp.int32, (z.rows, 1), 0)
+        row = lax.broadcasted_iota(jnp.int32, (16, 1), 0)
+        first = []
         for item in range(z.items):
             at = item * 16 + 14
             extra = parts[0][at : at + 1, :] + parts[1][at + 1 : at + 2, :]
-            pooled += jnp.where(row == item * r, extra, 0.0)
-        self.short[...] = low(pooled)
-        normed, inverse = norm_rows(self.short[...].astype(jnp.float32))
-        self.normed1[...] = normed
-        self.inverse1[...] = inverse
-        self.have("gain1", "bias1", "query_w", "key_w", "value_w")
-        self.attn_in[...] = low(normed * self.gain1_v[...] + self.bias1_v[...])
-        attn_in = self.attn_in[...]
-        qkv = [low(dot(attn_in, w[...])) for w in (self.query_w_v, self.key_w_v, self.value_w_v)]
-        self.moves = []
-
-        def send(unit):
-            for target in range(z.n):
-                self.qkv_out[unit, target] = self.pack(
-                    *(self.part(value, target, unit) for value in qkv)
-                )
-            self.moves.append(self.exchange("qkv", unit))
-
-        send(0)
+            first.append(pooled[item * r : item * r + 16, :] + jnp.where(row == 0, extra, 0.0))
+        first = normalize(jnp.concatenate(first, axis=0))
+        for ref, value in zip(kept, first):
+            for item in range(z.items):
+                ref[item * r : item * r + 16, :] = value[item * 16 : (item + 1) * 16, :]
+        for which, w in enumerate(weights):
+            value = low(dot(first[3], w[...]))
+            pieces = []
+            for item in range(z.items):
+                pieces += [
+                    value[item * 16 : (item + 1) * 16, :],
+                    qkv[which][item * r + 16 : (item + 1) * r, :],
+                ]
+            qkv[which] = jnp.concatenate(pieces, axis=0)
+        for target in range(z.n):
+            packed = self.pack(*(self.part(value, target, 0) for value in qkv))
+            self.qkv_out[0, target, late:, :] = packed[late:, :]
+        self.moves[0].append(self.exchange("qkv", 0, slice(late, late + 32), z.units))
         self.have("og", "up_w", "outer_w")
         rows_by_three(z, self.og_v, self.of)
         for part in range(3):
@@ -561,7 +585,8 @@
             )
         self.summed_grad[...] = low(dot_nt(self.up_rows[...], self.up_w_v[...]))
         for unit in range(1, z.units):
-            send(unit)
+            fill(unit)
+            self.moves.append([self.exchange("qkv", unit)])
         ff = self.outer_w_v.shape[0]
         for lo in range(0, ff, width):
             self.act_grad[:, lo : lo + width] = dot_nt(
@@ -579,7 +604,8 @@
         position_bias = self.position_bias_v[pl.ds(self.head, 1), :]
         moves = []
         for unit in range(z.units):
-            self.moves[unit].wait()
+            for move in self.moves[unit]:
+                move.wait()
             queries, keys, values = (
                 value.reshape(z.length, hd) for value in self.unpack(self.qkv_in[unit])
             )
@@ -629,6 +655,14 @@
             inner_grad = low(self.act_grad[:, cut] * (normal_cdf + inner * density))
             self.inner_grad[:, cut] = inner_grad
             ffn_grad += dot_nt(inner_grad, self.inner_w_v[:, cut])
+        row = 0
+        for lo in range(0, ff, width):
+            self.reach("unit")
+            self.work[row : row + width, :] = low(
+                dot_tn(self.act[:, lo : lo + width], self.summed_grad[...])
+            )
+            row += width
+        self.reach("branch")
         self.small_work[0, 2:3, :] = jnp.sum(ffn_grad * normed, axis=0, keepdims=True)
         self.small_work[0, 3:4, :] = jnp.sum(ffn_grad, axis=0, keepdims=True)
         hidden_grad = self.summed_grad[...].astype(jnp.float32) + norm_backward(
@@ -642,13 +676,6 @@
             for target in range(z.n):
                 self.grad_out[unit, target] = fold(self.part(att_grad, target, unit))
             self.moves.append(self.exchange("grad", unit))
-        row = 0
-        for lo in range(0, ff, width):
-            self.reach("unit")
-            self.work[row : row + width, :] = low(
-                dot_tn(self.act[:, lo : lo + width], self.summed_grad[...])
-            )
-            row += width
         for lo in range(0, ff, width):
             self.reach("unit")
             self.work[row : row + width, :] = low(
@@ -671,6 +698,7 @@
     def upsample(self):
         z, width = self.z, self.z.width
         for part in range(3):
+            self.reach("up")
             up = dot(self.summed[...], self.up_w_v[:, part * width : (part + 1) * width])
             set_every_third(
                 z, self.bf, 8 + part, every_third(z, self.xf, 8 + part) + up * self.live(part)
@@ -735,7 +763,6 @@
         for side in range(2):
             at = pl.multiple_of(base + side * z.heads * half + self.head * half, 16)
             self.work[pl.ds(at, half), :] = low(table_sum[side * half : (side + 1) * half])
-        self.reach("up")
         self.upsample()
         self.reach("back")
         for move in moves:
@@ -745,11 +772,13 @@
         z, me, r, width = self.z, self.me, self.z.r, self.z.width
         self.reach("rows")
         self.to_rows("back", self.unpack, [self.row_grad.at[which] for which in range(3)])
+        self.reach("rows")
         attn_grad = (
             dot_nt(self.row_grad[0], self.query_w_v[...])
             + dot_nt(self.row_grad[1], self.key_w_v[...])
             + dot_nt(self.row_grad[2], self.value_w_v[...])
         )
+        self.reach("rows")
         normed = self.normed1[...]
         self.small_work[0, 0:1, :] = jnp.sum(attn_grad * normed, axis=0, keepdims=True)
         self.small_work[0, 1:2, :] = jnp.sum(attn_grad, axis=0, keepdims=True)
@@ -763,16 +792,12 @@
             self.later[item, 0:r, :] = short_grad[item * r : (item + 1) * r, :].astype(jnp.float32)
         halo = self.neighbour(self.first_rows, self.next_rows, self.next_sems, z.n - 1)
         row = self.row
-        self.reach("qkv")
         for which in range(3):
+            self.reach("qkv")
             self.work[row : row + width, :] = low(dot_tn(self.attn_in[...], self.row_grad[which]))
             row += width
         self.reach("pool")
-        own = dot_nt(short_grad, self.pool_w_v[2 * width :, :])
-        set_every_third(z, self.of, 8, every_third(z, self.of, 8) + own)
-        self.work[row + 2 * width : row + 3 * width, :] = low(
-            dot_tn(low(every_third(z, self.xf, 8)), short_grad)
-        )
+        self.work[row : row + width, :] = low(dot_tn(low(every_third(z, self.xf, 8)), short_grad))
         halo.wait()
         for item in range(z.items):
             after = jnp.where(me < z.n - 1, self.next_rows[item].astype(jnp.float32), 0.0)
@@ -781,12 +806,14 @@
             jnp.concatenate([self.later[item, 1 : r + 1, :] for item in range(z.items)], axis=0)
         )
         for part in range(2):
-            cut = slice(row + part * width, row + (part + 1) * width)
-            self.work[cut, :] = low(dot_tn(low(every_third(z, self.xf, 9 + part)), later))
-        self.reach("input")
-        for part in range(2):
-            back = dot_nt(later, self.pool_w_v[part * width : (part + 1) * width, :])
-            first = 9 + part
+            row += width
+            self.reach("pool")
+            self.work[row : row + width, :] = low(
+                dot_tn(low(every_third(z, self.xf, 9 + part)), later)
+            )
+        for part, rows, first in ((2, short_grad, 8), (0, later, 9), (1, later, 10)):
+            self.reach("input")
+            back = dot_nt(rows, self.pool_w_v[part * width : (part + 1) * width, :])
             set_every_third(z, self.of, first, every_third(z, self.of, first) + back)
         for item in range(z.items):
             for slab in range(width // LANES):
@@ -860,12 +887,14 @@
         return [c for c, chain in enumerate(chains) if first < chain.get("units", 0) <= last]
 
     segments = [("unit", UNIT, done(unit, unit + 1)) for unit in range(early)]
+    segments.insert(ff // width, ("branch", BRANCH, []))
     segments += [("grad", 0.0, [])]
     segments += ([("block", BLOCK_STEP, [])] * blocks + [("send", SEND, [])]) * z.units
-    segments += [("table", TABLE, [len(chains) - 2]), ("up", UP, [])]
-    segments += [("back", 0.0, []), ("rows", ROWS, [len(chains) - 1])]
-    segments += [("qkv", QKV, done(early, early + 3)), ("pool", POOL, done(early + 3, units))]
-    segments += [("input", INPUT, [])]
+    segments += [("table", TABLE, [len(chains) - 2])] + [("up", UP, [])] * 3 + [("back", 0.0, [])]
+    segments += [("rows", ROWS, []), ("rows", ROWS, []), ("rows", ROWS, [len(chains) - 1])]
+    for name, cost, first in (("qkv", QKV, early), ("pool", POOL, early + 3)):
+        segments += [(name, cost, done(unit, unit + 1)) for unit in range(first, first + 3)]
+    segments += [("input", INPUT, [])] * 3
     return copies, chains, segments
 
 
@@ -904,7 +933,7 @@
     places += [output_ref]
     places += [up_ref.at[:, k * width : (k + 1) * width] for k in range(3)]
     places += [query_ref, key_ref, value_ref]
-    places += [pool_ref.at[k * width : (k + 1) * width] for k in range(3)]
+    places += [pool_ref.at[k * width : (k + 1) * width] for k in (2, 0, 1)]
     places += [position_ref]
     gain1_ref[...] = small_ref[0:1, :]
     bias1_ref[...] = small_ref[1:2, :]
@@ -920,7 +949,8 @@
     ):
         stores.append(pltpu.make_async_copy(source, target, pass_sems.at[which]))
         stores[-1].start()
-    for k in range(blocks):
+    order = list(range(blocks - 1))
+    for k in order[:4] + [blocks - 1] + order[4:]:
         if k + 1 < blocks:
             wide[k] = total_ref[k * width : (k + 1) * width, :].astype(jnp.float32)
         else:
@@ -1049,7 +1079,7 @@
         load_sems=dma((len(OPERANDS),)),
         halo_sems=dma((2,)),
         next_sems=dma((2,)),
-        qkv_sems=dma((units, 2)),
+        qkv_sems=dma((units + 1, 2)),
         att_sems=dma((units, 2)),
         grad_sems=dma((units, 2)),
         back_sems=dma((units, 2)),

time: 120 us -> 116 us (0.967)
  Pallas kernels: 119 us -> 115 us
    pallas_call x1, Pallas kernels: 111 us -> 107 us  [body(): pl.pallas_call(functools.partial(block_kernel, z, plan, chains, bits, nam...]
where the time goes in v7:
time: 116 us
  Pallas kernels  115 us (99%)
    pallas_call x1, Pallas kernels, body(): pl.pallas_call(functools.partial(block_kernel, z, plan, chains, bits, nam...  107 us
    pallas_call x1, Pallas kernels, body(): pl.pallas_call(functools.partial(result_kernel, z, ff), out_shape=[jax.Sh...  8 us

profile of v7, /device:TPU:0, one launch (start us, length us, event | category | flops | bytes accessed | tf_op | source)
XLA Modules:
  0.0 116.3 jit_solution(11974585842742562720)
XLA Ops:
  0.7 107.5 %shard_map.314 = (bf16[2,192,512]{2,1,0:T(8,128)(2,1)S(1)}, f32[2,192,512]{2,1,0:T(8,128)S(1)}, bf16[9728,512]{1,0:T(8,128)(2,1)S(1)}, f32[8,512]{1,0:T(8,128)S(1)}) custom-call(s32[2]{0:T(128)} %refs_0_.1, bf16[2,192,512]{2,1,0:T(8,128)(2,1)} %refs_1_.1, bf16[1536,512]{1,0:T(8,128)(2,1)} %refs_2_.1, f32[1,512]{1,0:T(1,128)} %bitcast.8, f32[1,512]{1,0:T(1,128)} %bitcast.9, ...), custom_call_target="tpu_custom_call" | custom-call | tf_op jit(solution)/shard_map/pallas_call | solution.py:1092
  108.2 8.0 %shard_map.315 = (bf16[2,192,512]{2,1,0:T(8,128)(2,1)}, f32[2,192,512]{2,1,0:T(8,128)}, f32[1536,512]{1,0:T(8,128)}, f32[1,512]{1,0:T(1,128)}, f32[1,512]{1,0:T(...) custom-call(bf16[9728,512]{1,0:T(8,128)(2,1)S(1)} %get-tuple-element, ...), custom_call_target="tpu_custom_call" | custom-call | tf_op jit(solution)/shard_map/pallas_call | solution.py:1125

commit v8 on v7

--- a/solution.py
+++ b/solution.py
@@ -449,10 +449,7 @@
             pl.semaphore_signal(
                 barrier, inc=1, device_id=self.sums.partner(bit), device_id_type=MESH
             )
-        pl.semaphore_wait(barrier, z.n - 1 + len(batch))
-        self.before = self.neighbour(
-            self.x.at[:, 3 * z.r - 16 :, :], self.halo, self.halo_sems, 1
-        )
+        self.greeted = len(batch)
 
     def pool(self, part):
         width = self.z.width
@@ -526,6 +523,10 @@
         self.xf[:, :, 0:8, :] = jnp.zeros((z.items, width // LANES, 8, LANES), jnp.float32)
         self.have("pool_w")
         pooled = self.pool(0) + self.pool(1) + self.pool(2)
+        pl.semaphore_wait(pltpu.get_barrier_semaphore(), z.n - 1 + self.greeted)
+        self.before = self.neighbour(
+            self.x.at[:, 3 * z.r - 16 :, :], self.halo, self.halo_sems, 1
+        )
         self.have("gain1", "bias1", "query_w", "key_w", "value_w")
         weights = (self.query_w_v, self.key_w_v, self.value_w_v)
 
@@ -624,7 +625,7 @@
                 valid = (key_at <= query_at) & (3 * key_at < length)
                 logits = jnp.where(valid, (content + placed) * hd**-0.5, masked_value)
                 raised = jnp.exp(logits - jnp.max(logits, axis=-1, keepdims=True))
-                probs = raised / jnp.sum(raised, axis=-1, keepdims=True)
+                probs = raised * (1.0 / jnp.sum(raised, axis=-1, keepdims=True))
                 self.probs[unit, lo:hi, :hi] = probs
                 attended = low(dot(low(probs), self.values[unit, :hi, :]))
                 per = BLOCK // z.r

time: 116 us -> 116 us (level)
  no operation moved by 1% of the time
where the time goes in v8:
time: 116 us
  Pallas kernels  115 us (99%)
    pallas_call x1, Pallas kernels, body(): pl.pallas_call(functools.partial(block_kernel, z, plan, chains, bits, nam...  107 us
    pallas_call x1, Pallas kernels, body(): pl.pallas_call(functools.partial(result_kernel, z, ff), out_shape=[jax.Sh...  8 us

profile of v8, /device:TPU:0, one launch (start us, length us, event | category | flops | bytes accessed | tf_op | source)
XLA Modules:
  0.0 116.2 jit_solution(18153217047193801812)
XLA Ops:
  0.7 107.4 %shard_map.314 = (bf16[2,192,512]{2,1,0:T(8,128)(2,1)S(1)}, f32[2,192,512]{2,1,0:T(8,128)S(1)}, bf16[9728,512]{1,0:T(8,128)(2,1)S(1)}, f32[8,512]{1,0:T(8,128)S(1)}) custom-call(s32[2]{0:T(128)} %refs_0_.1, bf16[2,192,512]{2,1,0:T(8,128)(2,1)} %refs_1_.1, bf16[1536,512]{1,0:T(8,128)(2,1)} %refs_2_.1, f32[1,512]{1,0:T(1,128)} %bitcast.8, f32[1,512]{1,0:T(1,128)} %bitcast.9, ...), custom_call_target="tpu_custom_call" | custom-call | tf_op jit(solution)/shard_map/pallas_call | solution.py:1093
  108.1 8.0 %shard_map.315 = (bf16[2,192,512]{2,1,0:T(8,128)(2,1)}, f32[2,192,512]{2,1,0:T(8,128)}, f32[1536,512]{1,0:T(8,128)}, f32[1,512]{1,0:T(1,128)}, f32[1,512]{1,0:T(...) custom-call(bf16[9728,512]{1,0:T(8,128)(2,1)S(1)} %get-tuple-element, ...), custom_call_target="tpu_custom_call" | custom-call | tf_op jit(solution)/shard_map/pallas_call | solution.py:1126
